TPU v7x, 32 devices: a whole 2x2x4 slice. The times are simulated.
32 devices in a mesh: fsdp: 8 (over y, x, core), sp: 4 (over z).
Axes of the slice: x: 2, y: 2, z: 4, core: 2. Of those that a mesh axis runs over, the one named last changes fastest.
Arguments:
- tokens: bfloat16 [64, 512, 1024], P('fsdp', 'sp'), may hold values from -6 to 6
- validity: int32 [64, 512], P('fsdp'), may hold values from 0 to 1, as said below
- teacher: bfloat16 [64, 512, 1024], P('fsdp', 'sp'), may hold values from -18 to 18
- query_matrix: bfloat16 [1024, 1024], P(('fsdp', 'sp')), may hold values from -0.1875 to 0.1875
- query_offset_bias: bfloat16 [1024], P(('fsdp', 'sp')), may hold values from -2 to 2
- key_matrix: bfloat16 [1024, 1024], P(('fsdp', 'sp')), may hold values from -0.1875 to 0.1875
- value_matrix: bfloat16 [1024, 1024], P(('fsdp', 'sp')), may hold values from -0.1875 to 0.1875
- value_offset_bias: bfloat16 [1024], P(('fsdp', 'sp')), may hold values from -0.29882812 to 0.29882812
- attention_output_weight: bfloat16 [1024, 1024], P(('fsdp', 'sp')), may hold values from -1.5 to 1.5
- attention_output_bias: bfloat16 [1024], P(('fsdp', 'sp')), may hold values from -0.59765625 to 0.59765625
- first_gain: bfloat16 [1024], P(('fsdp', 'sp')), may hold values from 0.5 to 1.5
- first_shift: bfloat16 [1024], P(('fsdp', 'sp')), may hold values from -0.59765625 to 0.59765625
- expand_weight: bfloat16 [1024, 4096], P(('fsdp', 'sp')), may hold values from -0.1875 to 0.1875
- expand_bias: bfloat16 [4096], P(('fsdp', 'sp')), may hold values from -2 to 2
- contract_weight: bfloat16 [4096, 1024], P(('fsdp', 'sp')), may hold values from -0.09375 to 0.09375
- contract_bias: bfloat16 [1024], P(('fsdp', 'sp')), may hold values from -0.59765625 to 0.59765625
- second_gain: bfloat16 [1024], P(('fsdp', 'sp')), may hold values from 0.5 to 1.5
- second_shift: bfloat16 [1024], P(('fsdp', 'sp')), may hold values from -1.5 to 1.5
Outputs:
- output: bfloat16 [64, 512, 1024], P('fsdp', 'sp')
- loss: float32 [], replicated
- grad_tokens: float32 [64, 512, 1024], P('fsdp', 'sp')
- grad_query_weight: float32 [1024, 1024], P(('fsdp', 'sp'))
- grad_query_bias: float32 [1024], P(('fsdp', 'sp'))
- grad_key_weight: float32 [1024, 1024], P(('fsdp', 'sp'))
- grad_value_weight: float32 [1024, 1024], P(('fsdp', 'sp'))
- grad_value_bias: float32 [1024], P(('fsdp', 'sp'))
- grad_output_weight: float32 [1024, 1024], P(('fsdp', 'sp'))
- grad_output_bias: float32 [1024], P(('fsdp', 'sp'))
- grad_first_gain: float32 [1024], P(('fsdp', 'sp'))
- grad_first_shift: float32 [1024], P(('fsdp', 'sp'))
- grad_inner_weight: float32 [1024, 4096], P(('fsdp', 'sp'))
- grad_inner_bias: float32 [4096], P(('fsdp', 'sp'))
- grad_outer_weight: float32 [4096, 1024], P(('fsdp', 'sp'))
- grad_outer_bias: float32 [1024], P(('fsdp', 'sp'))
- grad_second_gain: float32 [1024], P(('fsdp', 'sp'))
- grad_second_shift: float32 [1024], P(('fsdp', 'sp'))
Inputs may be any that keep to these rules, and one draw needn't show every extreme that they name: `validity`: each sequence's valid tokens form a prefix of 1 to 512 tokens; of the 8 sequences that start at each multiple of 8, one is valid in all 512 tokens.
All inputs are finite; a program needn't handle non-finite values.
Results may differ from a plain program's by a relative error of at most 0.014.
Values may be sent and summed in bfloat16 or wider, within the bound.
A program may use at most 192 MiB of HBM per device.

v0:
```python
import functools
import math

import jax
import jax.numpy as jnp
from jax import lax
from jax.experimental import pallas as pl
from jax.experimental.pallas import tpu as pltpu
from jax.sharding import PartitionSpec as P

HD = 64
BF = jnp.bfloat16
F32 = jnp.float32
MESH = pl.DeviceIdType.MESH
AXES = ("fsdp", "sp")
MIB = 1 << 20


def bits_of(n):
    return n.bit_length() - 1


def gather_steps(a, b, color):
    z = [("sp", k) for k in reversed(range(b))]
    f = [("fsdp", k) for k in reversed(range(a))]
    if color and a >= 2:
        f[0], f[1] = f[1], f[0]
    return z + f


class Place:
    def __init__(self, a, b):
        self.a, self.b = a, b
        self.f = lax.axis_index("fsdp")
        self.z = lax.axis_index("sp")

    def dim(self, step):
        axis, k = step
        return self.a - 1 - k if axis == "fsdp" else self.a + self.b - 1 - k

    def bit(self, step):
        axis, k = step
        me = self.f if axis == "fsdp" else self.z
        return lax.rem(me // (1 << k), 2)

    def own(self):
        out = [None] * (self.a + self.b)
        for step in gather_steps(self.a, self.b, 0):
            out[self.dim(step)] = self.bit(step)
        return out

    def partner(self, step):
        axis, k = step
        change = (1 - 2 * self.bit(step)) * (1 << k)
        if axis == "fsdp":
            return (self.f + change, self.z)
        return (self.f, self.z + change)

    def greet(self):
        barrier = pltpu.get_barrier_semaphore()
        s = 1 << self.b
        others = [(self.f, lax.rem(self.z + k, s)) for k in range(1, s)]
        others += [self.partner(("fsdp", k)) for k in range(self.a)]
        for other in others:
            pl.semaphore_signal(barrier, inc=1, device_id=other, device_id_type=MESH)
        pl.semaphore_wait(barrier, len(others))


def exchange_tokens(place, src, dst, send, recv, local):
    s = 1 << place.b
    copies = [pltpu.make_async_copy(src.at[place.z], dst.at[place.z], local)]
    for k in range(1, s):
        to = lax.rem(place.z + k, s)
        copies.append(
            pltpu.make_async_remote_copy(
                src_ref=src.at[to],
                dst_ref=dst.at[place.z],
                send_sem=send.at[k - 1],
                recv_sem=recv.at[k - 1],
                device_id=(place.f, to),
                device_id_type=MESH,
            )
        )
    return copies


def pieces(rows, columns, parts_r, parts_c):
    out = []
    for i in range(parts_r):
        for j in range(parts_c):
            out.append(
                (
                    pl.ds(i * (rows // parts_r), rows // parts_r),
                    pl.ds(j * (columns // parts_c), columns // parts_c),
                )
            )
    return out


def make_units(shapes):
    cuts = []
    for at, (r, c) in enumerate(shapes):
        parts_r = max(1, min(4, r // 32)) if at == 5 else 1
        parts_c = 4 if at == 4 else 1
        cuts.append([(at,) + piece for piece in pieces(r, c, parts_r, parts_c)])
    q, k, v, o, w1, w2 = cuts
    units = [[q[0] + (0,), k[0] + (1,)], [v[0] + (0,), o[0] + (1,)]]
    for i in range(max(len(w1), len(w2))):
        unit = [w1[i] + (0,)] if i < len(w1) else []
        unit += [w2[i] + (1,)] if i < len(w2) else []
        units.append(unit)
    return units


def front_kernel(a, b, units, *refs):
    n_mat = 6
    tokens, vec = refs[0], refs[1]
    shards = refs[2 : 2 + n_mat]
    out_tokens, out_vec = refs[2 + n_mat], refs[3 + n_mat]
    outs = refs[4 + n_mat : 4 + 2 * n_mat]
    send, recv, local, tok_send, tok_recv, tok_local = refs[4 + 2 * n_mat :]
    place = Place(a, b)
    own = place.own()
    chunks = [[(vec, out_vec, (), 0)] + [(shards[at], outs[at], (r, c), color) for at, r, c, color in units[0]]]
    for unit in units[1:]:
        chunks.append([(shards[at], outs[at], (r, c), color) for at, r, c, color in unit])
    flat = [chunk for unit in chunks for chunk in unit]
    number = {}
    for u, unit in enumerate(chunks):
        for i in range(len(unit)):
            number[u, i] = len(number)
    steps = a + b

    def copy_of(m, s):
        src, out, piece, color = flat[m]
        order = gather_steps(a, b, color)
        index = list(own)
        for step in order[:s]:
            index[place.dim(step)] = slice(None)
        there = out.at[tuple(index) + piece]
        here = (src.at[piece] if piece else src) if s == 0 else there
        return pltpu.make_async_remote_copy(
            src_ref=here,
            dst_ref=there,
            send_sem=send.at[m, s],
            recv_sem=recv.at[m, s],
            device_id=place.partner(order[s]),
            device_id_type=MESH,
        )

    def keep_of(m):
        src, out, piece, _ = flat[m]
        return pltpu.make_async_copy(
            src.at[piece] if piece else src, out.at[tuple(own) + piece], local.at[m]
        )

    for m in range(len(flat)):
        keep_of(m).start()
    place.greet()
    moves = exchange_tokens(place, tokens, out_tokens, tok_send, tok_recv, tok_local)
    for t in range(len(chunks) + steps):
        for s in reversed(range(steps + 1)):
            u = t - s
            if not 0 <= u < len(chunks):
                continue
            for i in range(len(chunks[u])):
                m = number[u, i]
                if s == 1:
                    keep_of(m).wait()
                if s > 0:
                    copy_of(m, s - 1).wait_recv()
                if s < steps:
                    copy_of(m, s).start()
        if t == 1:
            for move in moves:
                move.start()
    for m in range(len(flat)):
        for s in range(steps):
            copy_of(m, s).wait_send()
    for move in moves:
        move.wait()


def front(a, b, tokens, vec, shards):
    lead = (2,) * (a + b)
    units = make_units([w.shape for w in shards])
    n_chunks = 1 + sum(len(u) for u in units)
    steps = a + b
    anyspace = pl.BlockSpec(memory_space=pl.ANY)
    outs = [jax.ShapeDtypeStruct(tokens.shape, tokens.dtype), jax.ShapeDtypeStruct(lead + vec.shape, vec.dtype)]
    outs += [jax.ShapeDtypeStruct(lead + w.shape, w.dtype) for w in shards]
    s = 1 << b
    return pl.pallas_call(
        functools.partial(front_kernel, a, b, units),
        out_shape=outs,
        in_specs=[anyspace] * (2 + len(shards)),
        out_specs=[anyspace] * len(outs),
        scratch_shapes=[
            pltpu.SemaphoreType.DMA((n_chunks, steps)),
            pltpu.SemaphoreType.DMA((n_chunks, steps)),
            pltpu.SemaphoreType.DMA((n_chunks,)),
            pltpu.SemaphoreType.DMA((s - 1,)),
            pltpu.SemaphoreType.DMA((s - 1,)),
            pltpu.SemaphoreType.DMA,
        ],
        compiler_params=pltpu.CompilerParams(collective_id=0, has_side_effects=True),
        name="gather_weights",
    )(tokens, vec, *shards)


def back_kernel(a, b, units, *refs):
    n_mat = 6
    tokens, vec = refs[0], refs[1]
    grads = refs[2 : 2 + n_mat]
    out_tokens, out_vec = refs[2 + n_mat], refs[3 + n_mat]
    outs = refs[4 + n_mat : 4 + 2 * n_mat]
    rest = refs[4 + 2 * n_mat :]
    send, recv, local, tok_send, tok_recv, tok_local = rest[:6]
    steps = a + b
    n_chunks = 1 + sum(len(u) for u in units)
    sums = rest[6 : 6 + n_chunks]
    landed = rest[6 + n_chunks :]
    place = Place(a, b)
    own = place.own()
    chunks = [[(vec, out_vec, (), 0)] + [(grads[at], outs[at], (r, c), color) for at, r, c, color in units[0]]]
    for unit in units[1:]:
        chunks.append([(grads[at], outs[at], (r, c), color) for at, r, c, color in unit])
    flat = [chunk for unit in chunks for chunk in unit]
    number = {}
    for u, unit in enumerate(chunks):
        for i in range(len(unit)):
            number[u, i] = len(number)

    def index_at(m, s, flip):
        order = gather_steps(a, b, flat[m][3])[::-1]
        index = [slice(None)] * steps
        for step in order[: s + 1]:
            index[place.dim(step)] = own[place.dim(step)]
        if flip:
            d = place.dim(order[s])
            index[d] = 1 - own[d]
        return order, index

    def without_first(order, index):
        index = list(index)
        del index[place.dim(order[0])]
        return tuple(index)

    def copy_of(m, s):
        src, out, piece, color = flat[m]
        order, index = index_at(m, s, True)
        here = src.at[tuple(index) + piece] if s == 0 else sums[m].at[without_first(order, index)]
        return pltpu.make_async_remote_copy(
            src_ref=here,
            dst_ref=landed[m * steps + s],
            send_sem=send.at[m, s],
            recv_sem=recv.at[m, s],
            device_id=place.partner(order[s]),
            device_id_type=MESH,
        )

    def keep_of(m):
        src, out, piece, _ = flat[m]
        order, index = index_at(m, 0, False)
        return pltpu.make_async_copy(src.at[tuple(index) + piece], sums[m], local.at[m])

    def add(m, s):
        order, index = index_at(m, s, False)
        index = without_first(order, index)
        free = [d for d, v in enumerate(index) if isinstance(v, slice)]

        def one(i, carry):
            at = list(index)
            bits = []
            for j, d in enumerate(free):
                bit = lax.rem(i // (1 << (len(free) - 1 - j)), 2)
                at[d] = bit
                bits.append(bit)
            total = sums[m][tuple(at)].astype(F32) + landed[m * steps + s][tuple(bits)].astype(F32)
            sums[m][tuple(at)] = total.astype(sums[m].dtype)
            return carry

        if s < steps - 1:
            lax.fori_loop(0, 1 << len(free), one, 0)
        else:
            out, piece = flat[m][1], flat[m][2]
            total = sums[m][tuple(index)].astype(F32) + landed[m * steps + s][...].astype(F32)
            if piece:
                out[piece] = total
            else:
                out[...] = total

    place.greet()
    moves = exchange_tokens(place, tokens, out_tokens, tok_send, tok_recv, tok_local)
    for t in range(len(chunks) + steps):
        for s in reversed(range(steps + 1)):
            u = t - s
            if not 0 <= u < len(chunks):
                continue
            for i in range(len(chunks[u])):
                m = number[u, i]
                if s == 0:
                    keep_of(m).start()
                if s == 1:
                    keep_of(m).wait()
                if s > 0:
                    copy_of(m, s - 1).wait_recv()
                    add(m, s - 1)
                if s < steps:
                    copy_of(m, s).start()
        if t == 0:
            for move in moves:
                move.start()
    for m in range(len(flat)):
        for s in range(steps):
            copy_of(m, s).wait_send()
    for move in moves:
        move.wait()


def back(a, b, tokens, vec, grads):
    lead = a + b
    steps = a + b
    shapes = [g.shape[lead:] for g in grads]
    units = make_units(shapes)
    sizes = [vec.shape[lead:]] + [(r.size, c.size) for unit in units for _, r, c, _ in unit]
    types = [vec.dtype] + [grads[at].dtype for unit in units for at, _, _, _ in unit]
    n_chunks = len(sizes)
    anyspace = pl.BlockSpec(memory_space=pl.ANY)
    vmem = pl.BlockSpec(memory_space=pltpu.VMEM)
    outs = [jax.ShapeDtypeStruct(tokens.shape, tokens.dtype), jax.ShapeDtypeStruct(vec.shape[lead:], F32)]
    outs += [jax.ShapeDtypeStruct(shape, F32) for shape in shapes]
    s = 1 << b
    scratch = [
        pltpu.SemaphoreType.DMA((n_chunks, steps)),
        pltpu.SemaphoreType.DMA((n_chunks, steps)),
        pltpu.SemaphoreType.DMA((n_chunks,)),
        pltpu.SemaphoreType.DMA((s - 1,)),
        pltpu.SemaphoreType.DMA((s - 1,)),
        pltpu.SemaphoreType.DMA,
    ]
    scratch += [pltpu.VMEM((2,) * (steps - 1) + size, kind) for size, kind in zip(sizes, types)]
    for size, kind in zip(sizes, types):
        scratch += [pltpu.VMEM((2,) * (steps - 1 - k) + size, kind) for k in range(steps)]
    return pl.pallas_call(
        functools.partial(back_kernel, a, b, units),
        out_shape=outs,
        in_specs=[anyspace] * (2 + len(grads)),
        out_specs=[anyspace] + [vmem] * (len(outs) - 1),
        scratch_shapes=scratch,
        compiler_params=pltpu.CompilerParams(
            collective_id=1, has_side_effects=True, vmem_limit_bytes=56 * MIB
        ),
        name="sum_grads",
    )(tokens, vec, *grads)


def head_mask(head):
    lane = lax.broadcasted_iota(jnp.int32, (1, 2 * HD), 1)
    return (lane // HD == head).astype(F32)


def dot_nt(x, y):
    return lax.dot_general(x, y, (((1,), (1,)), ((), ())), preferred_element_type=F32)


def dot_tn(x, y):
    return lax.dot_general(x, y, (((0,), (0,)), ((), ())), preferred_element_type=F32)


def dot_nn(x, y):
    return lax.dot_general(x, y, (((1,), (0,)), ((), ())), preferred_element_type=F32)


def attend_kernel(temper, bias_ref, q_ref, k_ref, v_ref, ctx_ref, lse_ref):
    length = bias_ref.shape[-1]
    shape = q_ref.shape
    q = q_ref[...].reshape(length, shape[-1])
    k = k_ref[...].reshape(length, shape[-1])
    v = v_ref[...].reshape(length, shape[-1])
    bias = bias_ref[...].reshape(1, length)
    total = jnp.zeros((length, shape[-1]), F32)
    logs = jnp.zeros((length, shape[-1]), F32)
    for head in range(2):
        mask = head_mask(head)
        scores = dot_nt(q, k * (mask * temper).astype(BF)) + bias
        largest = jnp.max(scores, axis=-1, keepdims=True)
        raised = jnp.exp(scores - largest)
        summed = jnp.sum(raised, axis=-1, keepdims=True)
        part = dot_nn(raised.astype(BF), v * mask.astype(BF))
        total = total + part * (1.0 / summed)
        logs = logs + (largest + jnp.log(summed)) * mask
    ctx_ref[...] = total.astype(BF).reshape(shape)
    lse_ref[...] = logs.reshape(shape)


def attend(bias, q, k, v):
    s, n, t, width = q.shape
    rows = pl.BlockSpec((s, 1, t, 2 * HD), lambda i, j: (0, i, 0, j))
    return pl.pallas_call(
        functools.partial(attend_kernel, 1.0 / math.sqrt(HD)),
        grid=(n, width // (2 * HD)),
        out_shape=[
            jax.ShapeDtypeStruct(q.shape, BF),
            jax.ShapeDtypeStruct(q.shape, F32),
        ],
        in_specs=[pl.BlockSpec((1, 1, s * t), lambda i, j: (i, 0, 0)), rows, rows, rows],
        out_specs=[rows, rows],
        compiler_params=pltpu.CompilerParams(vmem_limit_bytes=32 * MIB),
        cost_estimate=pl.CostEstimate(
            flops=4 * n * (s * t) ** 2 * width, bytes_accessed=16 * s * n * t * width, transcendentals=0
        ),
        name="attend",
    )(bias, q, k, v)


def attend_back_kernel(temper, bias_ref, q_ref, k_ref, v_ref, ctx_ref, lse_ref, grad_ref, gq_ref, gk_ref, gv_ref):
    length = bias_ref.shape[-1]
    shape = q_ref.shape

    def whole(ref):
        return ref[...].reshape(length, shape[-1])

    q, k, v, ctx, grad, lse = (whole(r) for r in (q_ref, k_ref, v_ref, ctx_ref, grad_ref, lse_ref))
    key_bias = jnp.transpose(jnp.broadcast_to(bias_ref[...].reshape(1, length), (2 * HD, length)))[:, :1]
    both = grad.astype(F32) * ctx.astype(F32)
    lse_t = jnp.transpose(lse)
    both_t = jnp.transpose(both)
    gq = jnp.zeros((length, shape[-1]), F32)
    gk = jnp.zeros((length, shape[-1]), F32)
    gv = jnp.zeros((length, shape[-1]), F32)
    for head in range(2):
        mask = head_mask(head)
        low = mask.astype(BF)
        k_head = k * (mask * temper).astype(BF)
        grad_head = grad * low
        log_total = lse_t[head * HD : head * HD + 1]
        inner = jnp.sum(both_t[head * HD : (head + 1) * HD], axis=0, keepdims=True)
        scores = dot_nt(k_head, q) + key_bias
        attention = jnp.exp(scores - log_total)
        gv = gv + dot_nn(attention.astype(BF), grad_head)
        grad_attention = dot_nt(v, grad_head)
        grad_scores = (attention * (grad_attention - inner)).astype(BF)
        gk = gk + dot_nn(grad_scores, q * (mask * temper).astype(BF))
        gq = gq + dot_tn(grad_scores, k_head)
    gq_ref[...] = gq.astype(BF).reshape(shape)
    gk_ref[...] = gk.astype(BF).reshape(shape)
    gv_ref[...] = gv.astype(BF).reshape(shape)


def attend_back(bias, q, k, v, ctx, lse, grad):
    s, n, t, width = q.shape
    rows = pl.BlockSpec((s, 1, t, 2 * HD), lambda i, j: (0, i, 0, j))
    return pl.pallas_call(
        functools.partial(attend_back_kernel, 1.0 / math.sqrt(HD)),
        grid=(n, width // (2 * HD)),
        out_shape=[jax.ShapeDtypeStruct(q.shape, BF)] * 3,
        in_specs=[pl.BlockSpec((1, 1, s * t), lambda i, j: (i, 0, 0))] + [rows] * 6,
        out_specs=[rows] * 3,
        compiler_params=pltpu.CompilerParams(vmem_limit_bytes=32 * MIB),
        cost_estimate=pl.CostEstimate(
            flops=10 * n * (s * t) ** 2 * width, bytes_accessed=20 * s * n * t * width, transcendentals=0
        ),
        name="attend_back",
    )(bias, q, k, v, ctx, lse, grad)


def norm_forward(hidden, gain, shift):
    average = jnp.mean(hidden, axis=-1, keepdims=True)
    centred = hidden - average
    scale = lax.rsqrt(jnp.mean(centred * centred, axis=-1, keepdims=True) + 1e-12)
    xhat = centred * scale
    return xhat * gain + shift, xhat, scale


def norm_backward(grad, gain, xhat, scale):
    scaled = grad * gain
    lead = jnp.mean(scaled, axis=-1, keepdims=True)
    slope = jnp.mean(scaled * xhat, axis=-1, keepdims=True)
    return scale * (scaled - lead - xhat * slope)


def gelu_pair(x):
    cdf = 0.5 * (1.0 + lax.erf(x * (1.0 / math.sqrt(2.0))))
    pdf = jnp.exp(-0.5 * x * x) * (1.0 / math.sqrt(2.0 * math.pi))
    return x * cdf, cdf + x * pdf


def body(tokens, validity, teacher, wq, bq, wk, wv, bv, wo, bo, gain1, shift1, w1, b1, w2, b2, gain2, shift2):
    fs, sp = lax.axis_size("fsdp"), lax.axis_size("sp")
    a, b = bits_of(fs), bits_of(sp)
    devices = fs * sp
    seqs, part, width = tokens.shape
    n = seqs // sp
    length = part * sp
    rows = sp * n * part
    total_tokens = rows * devices
    z = lax.axis_index("sp")
    shard_shape = (sp, n, part, width)

    mine = lax.dynamic_slice_in_dim(validity, z * n, n, 0)
    count = jnp.sum(mine)
    vectors = (bq, bv, bo, gain1, shift1, b2, gain2, shift2, b1)
    sizes = [v.shape[0] for v in vectors]
    held = jnp.concatenate(list(vectors) + [jnp.stack([count // 32, count % 32]).astype(BF)])
    vec = jnp.pad(held, (0, 16 * 128 - held.shape[0])).reshape(16, 128)

    shards = (wq, wk, wv, wo, w1, w2)
    got = front(a, b, tokens.reshape(shard_shape), vec, shards)
    moved, vec_all = got[0], got[1].reshape(devices, -1)
    WQ, WK, WV, WO, W1, W2 = (
        g.reshape((devices * w.shape[0],) + w.shape[1:]) for g, w in zip(got[2:], shards)
    )
    full, at = [], 0
    for size in sizes:
        full.append(vec_all[:, at : at + size].reshape(-1).astype(F32))
        at += size
    BQ, BV, BO, G1, S1, B2, G2, S2, B1 = full
    counted = jnp.sum(vec_all[:, at].astype(F32)) * 32.0 + jnp.sum(vec_all[:, at + 1].astype(F32))

    teacher_moved = lax.all_to_all(
        lax.optimization_barrier((teacher, moved))[0].reshape(shard_shape), "sp", split_axis=0, concat_axis=0
    ).reshape(rows, width)

    valid = mine.astype(F32)
    bias = ((valid - 1.0) * 1e9).reshape(n, 1, length)
    mask_rows = jnp.swapaxes(valid.reshape(n, sp, part), 0, 1).reshape(rows, 1)

    x = moved.reshape(rows, width)
    q = (dot_nn(x, WQ) + BQ).astype(BF)
    k = dot_nn(x, WK).astype(BF)
    v = (dot_nn(x, WV) + BV).astype(BF)
    ctx, lse = attend(bias, *(p.reshape(shard_shape) for p in (q, k, v)))
    ctx_rows = ctx.reshape(rows, width)
    first = x.astype(F32) + dot_nn(ctx_rows, WO) + BO
    normed, xhat1, scale1 = norm_forward(first, G1, S1)
    normed_low = normed.astype(BF)
    inner = dot_nn(normed_low, W1) + B1
    active, slope = gelu_pair(inner)
    active_low = active.astype(BF)
    slope = slope.astype(BF)
    second = normed + dot_nn(active_low, W2) + B2
    final, xhat2, scale2 = norm_forward(second, G2, S2)
    error = final - teacher_moved.astype(F32)
    local_loss = jnp.sum(mask_rows * error * error)
    output = lax.all_to_all(final.astype(BF).reshape(shard_shape), "sp", split_axis=0, concat_axis=0)

    grad_final = (2.0 * total_tokens / counted) * mask_rows * error
    grad_second = norm_backward(grad_final, G2, xhat2, scale2)
    grad_outer = grad_second.astype(BF)
    g_w2 = dot_tn(active_low, grad_outer).astype(BF)
    grad_inner = (dot_nt(grad_outer, W2) * slope.astype(F32)).astype(BF)
    g_w1 = dot_tn(normed_low, grad_inner).astype(BF)
    grad_normed = dot_nt(grad_inner, W1) + grad_second
    grad_first = norm_backward(grad_normed, G1, xhat1, scale1)
    grad_attended = grad_first.astype(BF)
    g_wo = dot_tn(ctx_rows, grad_attended).astype(BF)
    grad_ctx = dot_nt(grad_attended, WO).astype(BF)
    gq, gk, gv = attend_back(
        bias, *(p.reshape(shard_shape) for p in (q, k, v)), ctx, lse, grad_ctx.reshape(shard_shape)
    )
    gq, gk, gv = (g.reshape(rows, width) for g in (gq, gk, gv))
    g_wq = dot_tn(x, gq).astype(BF)
    g_wk = dot_tn(x, gk).astype(BF)
    g_wv = dot_tn(x, gv).astype(BF)
    grad_tokens = (dot_nt(gq, WQ) + dot_nt(gk, WK) + dot_nt(gv, WV) + grad_first).astype(BF)

    def column_sum(value):
        return jnp.sum(value.astype(F32), axis=0)

    vector_grads = (
        column_sum(gq),
        column_sum(gv),
        column_sum(grad_attended),
        jnp.sum(grad_normed * xhat1, axis=0),
        column_sum(grad_normed),
        column_sum(grad_outer),
        jnp.sum(grad_final * xhat2, axis=0),
        column_sum(grad_final),
        column_sum(grad_inner),
    )
    parts = [g.reshape(devices, -1) for g in vector_grads]
    parts.append(jnp.broadcast_to(local_loss, (devices, 1)))
    packed = jnp.concatenate(parts, axis=1)
    packed = jnp.pad(packed, ((0, 0), (0, 8 * 128 - packed.shape[1])))
    lead = (2,) * (a + b)
    summed = back(
        a,
        b,
        grad_tokens.reshape(shard_shape),
        packed.reshape(lead + (8, 128)),
        [g.reshape(lead + w.shape) for g, w in zip((g_wq, g_wk, g_wv, g_wo, g_w1, g_w2), shards)],
    )
    home = summed[0].reshape(seqs, part, width).astype(F32)
    own = summed[1].reshape(-1)
    small, at = [], 0
    for size in sizes:
        small.append(own[at : at + size])
        at += size
    loss = own[at] / (width * counted)
    d_bq, d_bv, d_bo, d_g1, d_s1, d_b2, d_g2, d_s2, d_b1 = small
    d_wq, d_wk, d_wv, d_wo, d_w1, d_w2 = summed[2:]
    return (
        output.reshape(seqs, part, width),
        loss,
        home,
        d_wq,
        d_bq,
        d_wk,
        d_wv,
        d_bv,
        d_wo,
        d_bo,
        d_g1,
        d_s1,
        d_w1,
        d_b1,
        d_w2,
        d_b2,
        d_g2,
        d_s2,
    )


def solution(mesh):
    tokens = P("fsdp", "sp", None)
    matrix = P(AXES, None)
    vector = P(AXES)
    return jax.shard_map(
        body,
        mesh=mesh,
        in_specs=(
            tokens,
            P("fsdp", None),
            tokens,
            matrix,
            vector,
            matrix,
            matrix,
            vector,
            matrix,
            vector,
            vector,
            vector,
            matrix,
            vector,
            matrix,
            vector,
            vector,
            vector,
        ),
        out_specs=(
            tokens,
            P(),
            tokens,
            matrix,
            vector,
            matrix,
            matrix,
            vector,
            matrix,
            vector,
            vector,
            vector,
            matrix,
            vector,
            matrix,
            vector,
            vector,
            vector,
        ),
        check_vma=False,
    )
```

profile of v0, /device:TPU:0, one launch (start us, length us, event | category | flops | bytes accessed | tf_op | source)
XLA Modules:
  0.0 544.0 jit_solution(11553172316520099605)
XLA Ops:
  0.7 1.4 dynamic-slice_reduce_fusion
  4.6 6.1 %concatenate.7 = bf16[386]{0:T(512)(128)(2,1)S(1)} concatenate(bf16[32]{0:T(256)(128)(2,1)} %param.22, bf16[32]{0:T(256)(128)(2,1)} %param.25, bf16[32]{0:T(256)(128)(2,1)} %param.27, bf16[32]{0:T(256)(128)(2,1)} %param.28, bf16[32]{0:T(256)(128)(2,1)} %param.29, bf16[32]{0:T(256)(128)(2,1)} %param.33, bf16[32]{0:T(256)(128)(2,1)} %param.34, bf16[32]{0:T(256)(128)(2,1)} %param.35, ...), dimensions={0} | concatenate | bytes 1544 | tf_op jit(solution)/shard_map/concatenate | solution.py:505
  10.7 0.6 pad_bitcast_fusion.1.refs_1_
  11.3 155.9 %gather_weights.1 = (bf16[4,2,128,1024]{3,2,1,0:T(8,128)(2,1)}, bf16[2,2,2,2,2,16,128]{6,5,4,3,2,1,0:T(8,128)(2,1)}, bf16[2,2,2,2,2,32,1024]{6,5,4,3,2,1,0:T(8,1...) custom-call(bf16[4,2,128,1024]{3,2,1,0:T(8,128)(2,1)} %bitcast.130, ...), custom_call_target="tpu_custom_call" | custom-call | tf_op jit(solution)/shard_map/gather_weights/pallas_call | solution.py:193
  167.3 3.8 all-to-all-start.1
  171.0 0.7 add_multiply_fusion.1
  171.8 0.7 convert_reduce_fusion.5
  172.5 0.1 slice_convert_fusion.1
  173.9 0.1 reshape.343
  174.0 0.1 reshape.339
  174.1 0.1 reshape.340
  174.2 0.1 reshape.344
  174.2 0.1 reshape.342
  174.3 0.1 reshape.338
  174.5 4.7 convolution_convert_fusion.4
  179.3 2.3 add_convert_fusion.2
  181.6 2.3 add_convert_fusion.1
  184.0 20.1 %attend.1 = (bf16[4,2,128,1024]{3,2,1,0:T(8,128)(2,1)S(1)}, f32[4,2,128,1024]{3,2,1,0:T(8,128)S(1)}) custom-call(f32[2,1,512]{2,1,0:T(1,128)S(1)} %reshape.297.bias_ref, bf16[4,2,128,1024]{3,2,1,0:T(8,128)(2,1)S(1)} %bitcast.119, bf16[4,2,128,1024]{3,2,1,0:T(8,128)(2,1)S(1)} %bitcast.117, bf16[4,2,128,1024]{3,2,1,0:T(8,128)(2,1)S(1)} %bitcast.121), custom_call_target="tpu_custom_call" | custom-call | flops 2147483648 | bytes 16777216 | tf_op jit(solution)/shard_map/attend/pallas_call | solution.py:400
  204.2 2.5 fusion.17
  206.7 0.7 copy-done.13
  207.3 0.6 multiply_reduce_fusion.5
  207.9 1.6 slice-done
  209.5 1.9 slice-done.1
  211.4 15.3 %multiply_convert_fusion.1 = (bf16[1024,4096]{1,0:T(8,128)(2,1)}, f32[1024,4096]{1,0:T(8,128)}) fusion(f32[4096]{0:T(1024)S(1)} %fusion.8, bf16[1024,4096]{1,0:T(8,128)(2,1)S(1)} %bitcast.150, f32[1024,1024]{1,0:T(8,128)S(1)} %get-tuple-element.97, f32[1024]{0:T(1024)S(1)} %reshape.340, f32[1024]{0:T(1024)S(1)} %reshape.339, f32[1024]{0:T(1024)S(1)} %add_rsqrt_fusion.1, ...), kind=kOutput, calls=%fused_computation.8 | convolution fusion | flops 8620343296 | bytes 37781504 | tf_op jit(solution)/shard_map/dot_general | solution.py:372
  226.7 14.4 %fusion.18 = (f32[1024]{0:T(1024)S(1)}, f32[1024,1024]{1,0:T(8,128)S(1)}) fusion(f32[1024]{0:T(1024)S(1)} %reshape.342, bf16[1024,4096]{1,0:T(8,128)(2,1)} %get-tuple-element.98, bf16[4096,1024]{1,0:T(8,128)(2,1)} %bitcast.151, f32[1024]{0:T(1024)S(1)} %reshape.340, f32[1024]{0:T(1024)S(1)} %reshape.339, f32[1024]{0:T(1024)S(1)} %add_rsqrt_fusion.1, ...), kind=kOutput, calls=%fused_computation.84 | convolution fusion | flops 8597273600 | bytes 25190400 | tf_op jit(solution)/shard_map/dot_general | solution.py:372
  241.1 2.0 copy-done.15
  243.1 0.5 multiply_reduce_fusion.4
  243.7 6.0 %multiply_reduce_fusion.8 = (f32[1024]{0:T(1024)S(1)}, f32[1024]{0:T(1024)S(1)}, f32[1024]{0:T(1024)S(1)}, f32[1024]{0:T(1024)S(1)}, f32[]{:T(128)}) fusion(f32[1024]{0:T(1024)S(1)} %broadcast_multiply_fusion, bf16[4,2,128,1024]{3,2,1,0:T(8,128)(2,1)S(1)} %all-to-all-done.1, f32[1024]{0:T(1024)S(1)} %reshape.344, f32[1024]{0:T(1024)S(1)} %reshape.343, ...), kind=kLoop, calls=%fused_computation.43 | loop fusion | flops 17821696 | bytes 6332420 | tf_op jit(solution)/shard_map/reduce_sum | solution.py:569
  249.7 3.2 convert_reduce_fusion.1
  252.9 20.3 %convert_reduce_fusion = (f32[4096]{0:T(1024)S(1)}, bf16[1024,4096]{1,0:T(8,128)(2,1)}) fusion(f32[1024,4096]{1,0:T(8,128)} %get-tuple-element.99, f32[4096]{0:T(1024)S(1)} %fusion.8, bf16[4096,1024]{1,0:T(8,128)(2,1)} %bitcast.152, f32[1024,1024]{1,0:T(8,128)S(1)} %get-tuple-element.74), kind=kOutput, calls=%fused_computation.6 | convolution fusion | flops 8653893632 | bytes 37781504 | tf_op jit(solution)/shard_map/dot_general | solution.py:364
  273.2 15.3 %multiply_reduce_fusion.1 = (f32[1024]{0:T(1024)S(1)}, f32[1024]{0:T(1024)S(1)}, f32[1024]{0:T(1024)S(1)}, f32[1024]{0:T(1024)S(1)}, f32[1024,1024]{1,0:T(8,128)S(1)}) fusion(f32[1024,1024]{1,0:T(8,128)S(1)} %copy-done.18, f32[1024]{0:T(1024)S(1)} %add_rsqrt_fusion.1, f32[1024]{0:T(1024)S(1)} %broadcast_multiply_fusion.6, f32[1024]{0:T(1024)S(1)} %reshape.339, ...), kind=kOutput, calls=%fused_computation.20 | convolution fusion | flops 8600416256 | bytes 29388800 | tf_op jit(solution)/shard_map/dot_general | solution.py:364
  288.6 14.9 %convolution_convert_fusion.1 = bf16[1024,4096]{1,0:T(8,128)(2,1)} fusion(bf16[1024,4096]{1,0:T(8,128)(2,1)} %get-tuple-element.104, f32[1024,1024]{1,0:T(8,128)S(1)} %copy-done.18, f32[1024]{0:T(1024)S(1)} %reshape.340, f32[1024]{0:T(1024)S(1)} %reshape.339, f32[1024]{0:T(1024)S(1)} %add_rsqrt_fusion.1, f32[1024]{0:T(1024)S(1)} %broadcast_multiply_fusion.6), kind=kOutput, calls=%fused_computation.11 | convolution fusion | flops 8599371776 | bytes 20987904 | tf_op jit(solution)/shard_map/dot_general | solution.py:368
  303.5 1.6 convert_reduce_fusion.2
  305.1 2.4 convolution_convert_fusion.3
  307.4 0.7 copy-done.10
  308.2 3.7 convolution_convert_fusion.2
  311.9 1.1 copy-done.14
  313.0 33.7 %attend_back.1 = (bf16[4,2,128,1024]{3,2,1,0:T(8,128)(2,1)S(1)}, bf16[4,2,128,1024]{3,2,1,0:T(8,128)(2,1)S(1)}, bf16[4,2,128,1024]{3,2,1,0:T(8,128)(2,1)S(1)}) custom-call(f32[2,1,512]{2,1,0:T(1,128)S(1)} %copy-done.2, bf16[4,2,128,1024]{3,2,1,0:T(8,128)(2,1)S(1)} %bitcast.120, bf16[4,2,128,1024]{3,2,1,0:T(8,128)(2,1)S(1)} %bitcast.118, ...), custom_call_target="tpu_custom_call" | custom-call | flops 5368709120 | bytes 20971520 | tf_op jit(solution)/shard_map/attend_back/pallas_call | solution.py:454
  346.7 0.4 convert_reduce_fusion.4
  347.1 3.8 bitcast_convert_fusion.2
  350.8 0.4 convert_reduce_fusion.3
  351.2 5.3 all-to-all-start
  357.0 0.7 broadcast_in_dim.2
  357.7 0.1 concatenate.8
  357.8 0.7 copy.50
  358.5 4.7 fusion.19
  363.3 3.7 bitcast_convert_fusion.1
  367.0 2.4 fusion.20
  369.4 0.5 copy-done.34
  369.9 4.0 add_convert_fusion
  373.9 3.8 bitcast_convert_fusion
  377.7 14.8 %convolution_convert_fusion = bf16[4096,1024]{1,0:T(8,128)(2,1)} fusion(bf16[1024,4096]{1,0:T(8,128)(2,1)} %get-tuple-element.98, f32[1024,1024]{1,0:T(8,128)S(1)} %copy-done.20), kind=kOutput, calls=%fused_computation.10 | convolution fusion | flops 8595177472 | bytes 20971520 | tf_op jit(solution)/shard_map/dot_general | solution.py:368
  392.5 133.7 %sum_grads.1 = (bf16[4,2,128,1024]{3,2,1,0:T(8,128)(2,1)}, f32[8,128]{1,0:T(8,128)}, f32[32,1024]{1,0:T(8,128)}, f32[32,1024]{1,0:T(8,128)}, f32[32,1024]{1,0:T(...) custom-call(bf16[4,2,128,1024]{3,2,1,0:T(8,128)(2,1)} %bitcast.135, ...), custom_call_target="tpu_custom_call" | custom-call | tf_op jit(solution)/shard_map/sum_grads/pallas_call | solution.py:345
  526.2 1.2 slice.77
  528.1 1.2 slice_bitcast_fusion.1
  529.3 1.6 fusion.16
  530.9 4.1 bitcast_convert_fusion.3
  535.0 3.2 copy.60
  538.2 0.7 copy.61
  538.8 0.7 copy.62
  539.5 0.7 copy.63
  540.1 0.7 copy.64
  540.8 0.8 copy.65
  541.6 0.8 copy.66
  (100 shorter events, 1.0 us)
Async XLA Ops:
  167.3 4.5 copy-start.29
  167.3 76.4 %all-to-all-start.1 = ((bf16[4,2,128,1024]{3,2,1,0:T(8,128)(2,1)}), bf16[4,2,128,1024]{3,2,1,0:T(8,128)(2,1)S(1)}, u32[]{:S(2)}, u32[]{:S(2)}) async-start(bf16[4,2,128,1024]{3,2,1,0:T(8,128)(2,1)} %bitcast.131), calls=%async_computation.1 | async-start | bytes 4194304 | tf_op jit(solution)/shard_map/all_to_all | solution.py:521
  172.6 11.4 %copy-start.1 = (f32[2,1,512]{2,1,0:T(1,128)}, f32[2,1,512]{2,1,0:T(1,128)S(1)}, u32[]{:S(2)}) copy-start(f32[2,1,512]{2,1,0:T(1,128)S(1)} %reshape.297.bias_ref) | copy-start | bytes 12292
  174.5 4.7 copy-start.30
  174.5 4.7 copy-start.36
  179.2 4.8 copy-start.3
  179.3 2.4 copy-start.33
  181.6 2.4 copy-start.5
  184.0 22.7 %copy-start.7 = (bf16[1024,1024]{1,0:T(8,128)(2,1)}, bf16[1024,1024]{1,0:T(8,128)(2,1)S(1)}, u32[]{:S(2)}) copy-start(bf16[1024,1024]{1,0:T(8,128)(2,1)S(1)} %add_convert_fusion.1) | copy-start | bytes 6291460
  184.0 20.2 %copy-start.37 = (bf16[2,2,2,2,2,32,1024]{6,5,4,3,2,1,0:T(8,128)(2,1)S(1)}, bf16[2,2,2,2,2,32,1024]{6,5,4,3,2,1,0:T(8,128)(2,1)}, u32[]{:S(2)}) copy-start(bf16[2,2,2,2,2,32,1024]{6,5,4,3,2,1,0:T(8,128)(2,1)} %get-tuple-element.46) | copy-start | bytes 6291460
  204.1 2.5 copy-start.9
  204.1 3.2 copy-start.13
  204.1 5.3 slice-start
  204.2 7.2 %slice-start.1 = ((s8[8388608]{0:T(1024)(128)(4,1)}), s8[4194304]{0:T(1024)(128)(4,1)S(1)}, s32[]{:S(2)}) async-start(s8[8388608]{0:T(1024)(128)(4,1)} %bitcast.148), calls=%async_computation.3 | async-start | bytes 8388608
  207.3 19.4 %copy-start.17 = (f32[1024,1024]{1,0:T(8,128)}, f32[1024,1024]{1,0:T(8,128)S(1)}, u32[]{:S(2)}) copy-start(f32[1024,1024]{1,0:T(8,128)S(1)} %get-tuple-element.97) | copy-start | bytes 12582916
  241.1 2.0 copy-start.15
  243.7 6.0 %copy-start.16 = (f32[1024,1024]{1,0:T(8,128)S(1)}, f32[1024,1024]{1,0:T(8,128)}, u32[]{:S(2)}) copy-start(f32[1024,1024]{1,0:T(8,128)} %copy-done.15) | copy-start | bytes 12582916
  252.9 20.3 %copy-start.19 = (f32[1024,1024]{1,0:T(8,128)}, f32[1024,1024]{1,0:T(8,128)S(1)}, u32[]{:S(2)}) copy-start(f32[1024,1024]{1,0:T(8,128)S(1)} %get-tuple-element.74) | copy-start | bytes 12582916
  252.9 20.3 %copy-start.18 = (f32[1024,1024]{1,0:T(8,128)S(1)}, f32[1024,1024]{1,0:T(8,128)}, u32[]{:S(2)}) copy-start(f32[1024,1024]{1,0:T(8,128)} %copy-done.17) | copy-start | bytes 12582916
  303.5 1.6 copy-start.38
  305.0 2.4 copy-start.21
  305.0 3.1 copy-start.10
  308.2 3.8 copy-start.2
  308.2 3.8 copy-start.4
  308.2 3.8 copy-start.6
  308.2 3.8 copy-start.8
  308.2 4.8 copy-start.14
  313.0 34.1 %copy-start.31 = (bf16[4,2,128,1024]{3,2,1,0:T(8,128)(2,1)S(1)}, bf16[4,2,128,1024]{3,2,1,0:T(8,128)(2,1)}, u32[]{:S(2)}) copy-start(bf16[4,2,128,1024]{3,2,1,0:T(8,128)(2,1)} %get-tuple-element.40) | copy-start | bytes 6291460
  346.7 4.1 copy-start
  346.7 4.1 copy-start.11
  351.2 183.8 %all-to-all-start = ((bf16[4,2,128,1024]{3,2,1,0:T(8,128)(2,1)}), bf16[4,2,128,1024]{3,2,1,0:T(8,128)(2,1)}, u32[]{:S(2)}, u32[]{:S(2)}) async-start(bf16[4,2,128,1024]{3,2,1,0:T(8,128)(2,1)} %bitcast.129), calls=%async_computation | async-start | bytes 4194304 | tf_op jit(solution)/shard_map/all_to_all | solution.py:546
  358.5 4.7 copy-start.12
  358.5 4.8 copy-start.32
  363.3 3.8 copy-start.35
  367.0 2.4 copy-start.22
  367.0 2.9 copy-start.34
  373.9 3.8 copy-start.20
  530.8 7.3 %copy-start.28 = (f32[32,1024]{1,0:T(8,128)S(1)}, f32[32,1024]{1,0:T(8,128)}, u32[]{:S(2)}) copy-start(f32[32,1024]{1,0:T(8,128)} %get-tuple-element.128) | copy-start | bytes 393220
  530.8 8.0 %copy-start.27 = (f32[32,1024]{1,0:T(8,128)S(1)}, f32[32,1024]{1,0:T(8,128)}, u32[]{:S(2)}) copy-start(f32[32,1024]{1,0:T(8,128)} %get-tuple-element.130) | copy-start | bytes 393220
  530.8 8.6 %copy-start.26 = (f32[32,1024]{1,0:T(8,128)S(1)}, f32[32,1024]{1,0:T(8,128)}, u32[]{:S(2)}) copy-start(f32[32,1024]{1,0:T(8,128)} %get-tuple-element.131) | copy-start | bytes 393220
  530.9 9.3 %copy-start.25 = (f32[32,1024]{1,0:T(8,128)S(1)}, f32[32,1024]{1,0:T(8,128)}, u32[]{:S(2)}) copy-start(f32[32,1024]{1,0:T(8,128)} %get-tuple-element.133) | copy-start | bytes 393220
  535.0 5.8 %copy-start.24 = (f32[32,4096]{1,0:T(8,128)S(1)}, f32[32,4096]{1,0:T(8,128)}, u32[]{:S(2)}) copy-start(f32[32,4096]{1,0:T(8,128)} %get-tuple-element.137) | copy-start | bytes 1572868
  535.0 6.6 %copy-start.23 = (f32[128,1024]{1,0:T(8,128)S(1)}, f32[128,1024]{1,0:T(8,128)}, u32[]{:S(2)}) copy-start(f32[128,1024]{1,0:T(8,128)} %get-tuple-element.139) | copy-start | bytes 1572868
where the time goes:
time: 554 us; the launch traced here: 544 us
  Pallas kernels  343 us (62%)
  matrix products  135 us (24%)
  local copies, waits for them, and re-layouts  29.2 us (5%)
  other arithmetic  19.6 us (4%)
  starting transfers between devices  9.03 us (2%)
  between operations  7.38 us (1%)
    pallas_call x1, Pallas kernels, front(): pl.pallas_call(functools.partial(front_kernel, a, b, units), out_shape=ou...  156 us
    pallas_call x1, Pallas kernels, back(): pl.pallas_call(functools.partial(back_kernel, a, b, units), out_shape=out...  134 us
    dot_general x6, matrix products, dot_nt(): lax.dot_general(x, y, (((1,), (1,)), ((), ())), preferred_element_type=F32)  49.1 us
    dot_general x6, matrix products, dot_tn(): lax.dot_general(x, y, (((0,), (0,)), ((), ())), preferred_element_type=F32)  44.7 us
    dot_general x6, matrix products, dot_nn(): lax.dot_general(x, y, (((1,), (0,)), ((), ())), preferred_element_type=F32)  41.6 us
    pallas_call x1, Pallas kernels, attend_back(): pl.pallas_call(functools.partial(attend_back_kernel, 1.0 / math.sqrt(HD))...  33.7 us
    pallas_call x1, Pallas kernels, attend(): pl.pallas_call(functools.partial(attend_kernel, 1.0 / math.sqrt(HD)), gri...  20.1 us
    unnamed x92, local copies, waits for them, and re-layouts  16.7 us
  transfers between devices with their start and end apart: 2, of which 0 were waited for; matrix products, arithmetic and copies ran while one was open for 16% of the time, Pallas kernels for 28%

commit v1 on v0

--- a/solution.py
+++ b/solution.py
@@ -14,6 +14,9 @@
 MESH = pl.DeviceIdType.MESH
 AXES = ("fsdp", "sp")
 MIB = 1 << 20
+GATHER_PAIRS = ((0, 1, 1), (2, 3, 1), (4, 5, 4))
+SUM_PAIRS = ((4, 5, 4), (3, 3, 1), (0, 1, 1), (2, 2, 1))
+WAVE_STEPS = (0, 2, 5, 12, 19)
 
 
 def bits_of(n):
@@ -97,18 +100,22 @@
     return out
 
 
-def make_units(shapes):
-    cuts = []
-    for at, (r, c) in enumerate(shapes):
-        parts_r = max(1, min(4, r // 32)) if at == 5 else 1
-        parts_c = 4 if at == 4 else 1
-        cuts.append([(at,) + piece for piece in pieces(r, c, parts_r, parts_c)])
-    q, k, v, o, w1, w2 = cuts
-    units = [[q[0] + (0,), k[0] + (1,)], [v[0] + (0,), o[0] + (1,)]]
-    for i in range(max(len(w1), len(w2))):
-        unit = [w1[i] + (0,)] if i < len(w1) else []
-        unit += [w2[i] + (1,)] if i < len(w2) else []
-        units.append(unit)
+def make_units(shapes, pairs):
+    units = []
+    for x, y, n in pairs:
+        (rx, cx), (ry, cy) = shapes[x], shapes[y]
+        if x == y:
+            left, right = pieces(rx, cx, 1, 2)
+            units.append([(x,) + left + (0,), (y,) + right + (1,)])
+            continue
+        ny = max(1, min(n, ry // 16)) if ry > rx else 1
+        xs = pieces(rx, cx, 1, n)
+        ys = pieces(ry, cy, ny, 1)
+        for k in range(n):
+            unit = [(x,) + xs[k] + (0,)]
+            if k < ny:
+                unit.append((y,) + ys[k] + (1,))
+            units.append(unit)
     return units
 
 
@@ -158,32 +165,32 @@
         keep_of(m).start()
     place.greet()
     moves = exchange_tokens(place, tokens, out_tokens, tok_send, tok_recv, tok_local)
-    for t in range(len(chunks) + steps):
-        for s in reversed(range(steps + 1)):
-            u = t - s
-            if not 0 <= u < len(chunks):
-                continue
-            for i in range(len(chunks[u])):
-                m = number[u, i]
-                if s == 1:
-                    keep_of(m).wait()
-                if s > 0:
-                    copy_of(m, s - 1).wait_recv()
-                if s < steps:
-                    copy_of(m, s).start()
-        if t == 1:
+    lead = [b + 1, b] + list(range(b - 1, -1, -1)) + list(range(b + 2, steps + 1))
+    events = [(u + k, lead.index(k), u, k) for u in range(len(chunks)) for k in range(steps + 1)]
+    events.append((len(chunks) + 0.5, 0, -1, -1))
+    for _, _, u, k in sorted(events):
+        if u < 0:
             for move in moves:
                 move.start()
+            continue
+        for i in range(len(chunks[u])):
+            m = number[u, i]
+            if k == 1:
+                keep_of(m).wait()
+            if k > 0:
+                copy_of(m, k - 1).wait_recv()
+            if k < steps:
+                copy_of(m, k).start()
     for m in range(len(flat)):
-        for s in range(steps):
-            copy_of(m, s).wait_send()
+        for k in range(steps):
+            copy_of(m, k).wait_send()
     for move in moves:
         move.wait()
 
 
 def front(a, b, tokens, vec, shards):
     lead = (2,) * (a + b)
-    units = make_units([w.shape for w in shards])
+    units = make_units([w.shape for w in shards], GATHER_PAIRS)
     n_chunks = 1 + sum(len(u) for u in units)
     steps = a + b
     anyspace = pl.BlockSpec(memory_space=pl.ANY)
@@ -208,153 +215,6 @@
     )(tokens, vec, *shards)
 
 
-def back_kernel(a, b, units, *refs):
-    n_mat = 6
-    tokens, vec = refs[0], refs[1]
-    grads = refs[2 : 2 + n_mat]
-    out_tokens, out_vec = refs[2 + n_mat], refs[3 + n_mat]
-    outs = refs[4 + n_mat : 4 + 2 * n_mat]
-    rest = refs[4 + 2 * n_mat :]
-    send, recv, local, tok_send, tok_recv, tok_local = rest[:6]
-    steps = a + b
-    n_chunks = 1 + sum(len(u) for u in units)
-    sums = rest[6 : 6 + n_chunks]
-    landed = rest[6 + n_chunks :]
-    place = Place(a, b)
-    own = place.own()
-    chunks = [[(vec, out_vec, (), 0)] + [(grads[at], outs[at], (r, c), color) for at, r, c, color in units[0]]]
-    for unit in units[1:]:
-        chunks.append([(grads[at], outs[at], (r, c), color) for at, r, c, color in unit])
-    flat = [chunk for unit in chunks for chunk in unit]
-    number = {}
-    for u, unit in enumerate(chunks):
-        for i in range(len(unit)):
-            number[u, i] = len(number)
-
-    def index_at(m, s, flip):
-        order = gather_steps(a, b, flat[m][3])[::-1]
-        index = [slice(None)] * steps
-        for step in order[: s + 1]:
-            index[place.dim(step)] = own[place.dim(step)]
-        if flip:
-            d = place.dim(order[s])
-            index[d] = 1 - own[d]
-        return order, index
-
-    def without_first(order, index):
-        index = list(index)
-        del index[place.dim(order[0])]
-        return tuple(index)
-
-    def copy_of(m, s):
-        src, out, piece, color = flat[m]
-        order, index = index_at(m, s, True)
-        here = src.at[tuple(index) + piece] if s == 0 else sums[m].at[without_first(order, index)]
-        return pltpu.make_async_remote_copy(
-            src_ref=here,
-            dst_ref=landed[m * steps + s],
-            send_sem=send.at[m, s],
-            recv_sem=recv.at[m, s],
-            device_id=place.partner(order[s]),
-            device_id_type=MESH,
-        )
-
-    def keep_of(m):
-        src, out, piece, _ = flat[m]
-        order, index = index_at(m, 0, False)
-        return pltpu.make_async_copy(src.at[tuple(index) + piece], sums[m], local.at[m])
-
-    def add(m, s):
-        order, index = index_at(m, s, False)
-        index = without_first(order, index)
-        free = [d for d, v in enumerate(index) if isinstance(v, slice)]
-
-        def one(i, carry):
-            at = list(index)
-            bits = []
-            for j, d in enumerate(free):
-                bit = lax.rem(i // (1 << (len(free) - 1 - j)), 2)
-                at[d] = bit
-                bits.append(bit)
-            total = sums[m][tuple(at)].astype(F32) + landed[m * steps + s][tuple(bits)].astype(F32)
-            sums[m][tuple(at)] = total.astype(sums[m].dtype)
-            return carry
-
-        if s < steps - 1:
-            lax.fori_loop(0, 1 << len(free), one, 0)
-        else:
-            out, piece = flat[m][1], flat[m][2]
-            total = sums[m][tuple(index)].astype(F32) + landed[m * steps + s][...].astype(F32)
-            if piece:
-                out[piece] = total
-            else:
-                out[...] = total
-
-    place.greet()
-    moves = exchange_tokens(place, tokens, out_tokens, tok_send, tok_recv, tok_local)
-    for t in range(len(chunks) + steps):
-        for s in reversed(range(steps + 1)):
-            u = t - s
-            if not 0 <= u < len(chunks):
-                continue
-            for i in range(len(chunks[u])):
-                m = number[u, i]
-                if s == 0:
-                    keep_of(m).start()
-                if s == 1:
-                    keep_of(m).wait()
-                if s > 0:
-                    copy_of(m, s - 1).wait_recv()
-                    add(m, s - 1)
-                if s < steps:
-                    copy_of(m, s).start()
-        if t == 0:
-            for move in moves:
-                move.start()
-    for m in range(len(flat)):
-        for s in range(steps):
-            copy_of(m, s).wait_send()
-    for move in moves:
-        move.wait()
-
-
-def back(a, b, tokens, vec, grads):
-    lead = a + b
-    steps = a + b
-    shapes = [g.shape[lead:] for g in grads]
-    units = make_units(shapes)
-    sizes = [vec.shape[lead:]] + [(r.size, c.size) for unit in units for _, r, c, _ in unit]
-    types = [vec.dtype] + [grads[at].dtype for unit in units for at, _, _, _ in unit]
-    n_chunks = len(sizes)
-    anyspace = pl.BlockSpec(memory_space=pl.ANY)
-    vmem = pl.BlockSpec(memory_space=pltpu.VMEM)
-    outs = [jax.ShapeDtypeStruct(tokens.shape, tokens.dtype), jax.ShapeDtypeStruct(vec.shape[lead:], F32)]
-    outs += [jax.ShapeDtypeStruct(shape, F32) for shape in shapes]
-    s = 1 << b
-    scratch = [
-        pltpu.SemaphoreType.DMA((n_chunks, steps)),
-        pltpu.SemaphoreType.DMA((n_chunks, steps)),
-        pltpu.SemaphoreType.DMA((n_chunks,)),
-        pltpu.SemaphoreType.DMA((s - 1,)),
-        pltpu.SemaphoreType.DMA((s - 1,)),
-        pltpu.SemaphoreType.DMA,
-    ]
-    scratch += [pltpu.VMEM((2,) * (steps - 1) + size, kind) for size, kind in zip(sizes, types)]
-    for size, kind in zip(sizes, types):
-        scratch += [pltpu.VMEM((2,) * (steps - 1 - k) + size, kind) for k in range(steps)]
-    return pl.pallas_call(
-        functools.partial(back_kernel, a, b, units),
-        out_shape=outs,
-        in_specs=[anyspace] * (2 + len(grads)),
-        out_specs=[anyspace] + [vmem] * (len(outs) - 1),
-        scratch_shapes=scratch,
-        compiler_params=pltpu.CompilerParams(
-            collective_id=1, has_side_effects=True, vmem_limit_bytes=56 * MIB
-        ),
-        name="sum_grads",
-    )(tokens, vec, *grads)
-
-
 def head_mask(head):
     lane = lax.broadcasted_iota(jnp.int32, (1, 2 * HD), 1)
     return (lane // HD == head).astype(F32)
@@ -391,7 +251,9 @@
         total = total + part * (1.0 / summed)
         logs = logs + (largest + jnp.log(summed)) * mask
     ctx_ref[...] = total.astype(BF).reshape(shape)
-    lse_ref[...] = logs.reshape(shape)
+    turned = jnp.transpose(logs)
+    for head in range(2):
+        lse_ref[0, 0, head : head + 1] = turned[head * HD : head * HD + 1]
 
 
 def attend(bias, q, k, v):
@@ -402,10 +264,10 @@
         grid=(n, width // (2 * HD)),
         out_shape=[
             jax.ShapeDtypeStruct(q.shape, BF),
-            jax.ShapeDtypeStruct(q.shape, F32),
+            jax.ShapeDtypeStruct((n, width // (2 * HD), 8, s * t), F32),
         ],
         in_specs=[pl.BlockSpec((1, 1, s * t), lambda i, j: (i, 0, 0)), rows, rows, rows],
-        out_specs=[rows, rows],
+        out_specs=[rows, pl.BlockSpec((1, 1, 8, s * t), lambda i, j: (i, j, 0, 0))],
         compiler_params=pltpu.CompilerParams(vmem_limit_bytes=32 * MIB),
         cost_estimate=pl.CostEstimate(
             flops=4 * n * (s * t) ** 2 * width, bytes_accessed=16 * s * n * t * width, transcendentals=0
@@ -414,55 +276,362 @@
     )(bias, q, k, v)
 
 
-def attend_back_kernel(temper, bias_ref, q_ref, k_ref, v_ref, ctx_ref, lse_ref, grad_ref, gq_ref, gk_ref, gv_ref):
+def attend_back_pair(temper, bias_ref, q_ref, k_ref, v_ref, ctx_ref, lse_ref, grad_ref):
     length = bias_ref.shape[-1]
-    shape = q_ref.shape
 
     def whole(ref):
-        return ref[...].reshape(length, shape[-1])
-
-    q, k, v, ctx, grad, lse = (whole(r) for r in (q_ref, k_ref, v_ref, ctx_ref, grad_ref, lse_ref))
+        return ref[...].reshape(length, ref.shape[-1])
+
+    q, k, v, ctx, grad = (whole(r) for r in (q_ref, k_ref, v_ref, ctx_ref, grad_ref))
     key_bias = jnp.transpose(jnp.broadcast_to(bias_ref[...].reshape(1, length), (2 * HD, length)))[:, :1]
-    both = grad.astype(F32) * ctx.astype(F32)
-    lse_t = jnp.transpose(lse)
-    both_t = jnp.transpose(both)
-    gq = jnp.zeros((length, shape[-1]), F32)
-    gk = jnp.zeros((length, shape[-1]), F32)
-    gv = jnp.zeros((length, shape[-1]), F32)
+    both = jnp.transpose(grad.astype(F32) * ctx.astype(F32))
+    gq = jnp.zeros(q.shape, F32)
+    gk = jnp.zeros(q.shape, F32)
+    gv = jnp.zeros(q.shape, F32)
     for head in range(2):
         mask = head_mask(head)
-        low = mask.astype(BF)
         k_head = k * (mask * temper).astype(BF)
-        grad_head = grad * low
-        log_total = lse_t[head * HD : head * HD + 1]
-        inner = jnp.sum(both_t[head * HD : (head + 1) * HD], axis=0, keepdims=True)
-        scores = dot_nt(k_head, q) + key_bias
-        attention = jnp.exp(scores - log_total)
+        grad_head = grad * mask.astype(BF)
+        log_total = lse_ref[0, 0, head : head + 1]
+        inner = jnp.sum(both[head * HD : (head + 1) * HD], axis=0, keepdims=True)
+        attention = jnp.exp(dot_nt(k_head, q) + key_bias - log_total)
         gv = gv + dot_nn(attention.astype(BF), grad_head)
         grad_attention = dot_nt(v, grad_head)
         grad_scores = (attention * (grad_attention - inner)).astype(BF)
         gk = gk + dot_nn(grad_scores, q * (mask * temper).astype(BF))
         gq = gq + dot_tn(grad_scores, k_head)
-    gq_ref[...] = gq.astype(BF).reshape(shape)
-    gk_ref[...] = gk.astype(BF).reshape(shape)
-    gv_ref[...] = gv.astype(BF).reshape(shape)
-
-
-def attend_back(bias, q, k, v, ctx, lse, grad):
+    return gq.astype(BF), gk.astype(BF), gv.astype(BF)
+
+
+class Sums:
+    def __init__(self, a, b, chunks, landed, staged, send, recv, local):
+        self.place = Place(a, b)
+        self.own = self.place.own()
+        self.steps = a + b
+        self.chunks, self.landed, self.staged = chunks, landed, staged
+        self.send, self.recv, self.local = send, recv, local
+        self.orders = [gather_steps(a, b, c[3])[::-1] for c in chunks]
+
+    def index(self, m, s, flip):
+        out = [slice(None)] * self.steps
+        for step in self.orders[m][: s + 1]:
+            out[self.place.dim(step)] = self.own[self.place.dim(step)]
+        if flip:
+            d = self.place.dim(self.orders[m][s])
+            out[d] = 1 - self.own[d]
+        return out
+
+    def later(self, m, index):
+        out = list(index)
+        del out[self.place.dim(self.orders[m][0])]
+        return tuple(out)
+
+    def copy(self, m, s):
+        src, _, piece, _ = self.chunks[m]
+        index = self.index(m, s, True)
+        here = src.at[tuple(index) + piece] if s == 0 else self.landed[m][0].at[self.later(m, index)]
+        return pltpu.make_async_remote_copy(
+            src_ref=here,
+            dst_ref=self.landed[m][s],
+            send_sem=self.send.at[m, s],
+            recv_sem=self.recv.at[m, s],
+            device_id=self.place.partner(self.orders[m][s]),
+            device_id_type=MESH,
+        )
+
+    def keep(self, m):
+        src, _, piece, _ = self.chunks[m]
+        index = self.index(m, 0, False)
+        return pltpu.make_async_copy(src.at[tuple(index) + piece], self.staged[m], self.local.at[m])
+
+    def add(self, m, s):
+        total, index = self.landed[m][0], self.later(m, self.index(m, s, False))
+        other = self.staged[m] if s == 0 else self.landed[m][s]
+        if s == self.steps - 1:
+            out, piece = self.chunks[m][1], self.chunks[m][2]
+            value = total[index].astype(F32) + other[...].astype(F32)
+            out[piece if piece else ...] = value
+            return
+        free = [d for d, v in enumerate(index) if isinstance(v, slice)]
+
+        def one(i, carry):
+            at, bits = list(index), []
+            for j, d in enumerate(free):
+                at[d] = lax.rem(i // (1 << (len(free) - 1 - j)), 2)
+                bits.append(at[d])
+            value = total[tuple(at)].astype(F32) + other[tuple(bits)].astype(F32)
+            total[tuple(at)] = value.astype(total.dtype)
+            return carry
+
+        lax.fori_loop(0, 1 << len(free), one, 0)
+
+    def event(self, unit, s):
+        for m in unit:
+            if s == 1:
+                self.keep(m).start()
+        for m in unit:
+            if s > 0:
+                self.copy(m, s - 1).wait_recv()
+                if s == 1:
+                    self.keep(m).wait()
+                self.add(m, s - 1)
+            if s < self.steps:
+                self.copy(m, s).start()
+
+    def finish(self):
+        for m in range(len(self.chunks)):
+            for s in range(self.steps):
+                self.copy(m, s).wait_send()
+
+
+def wave_events(units, steps):
+    waves = []
+    for t in range(units + steps):
+        waves.append([(t - k, k) for k in range(steps, -1, -1) if 0 <= t - k < units])
+    return waves
+
+
+def plan_steps(n, pairs, blocks):
+    out = []
+    for s in range(n):
+        out += [("attend", s, p) for p in range(pairs)]
+        if s == n - 1:
+            out += [("weights", 0, c) for c in range(blocks)]
+        out += [("tokens", s, r) for r in range(blocks)]
+    return out
+
+
+def span(plan, kind, s=None):
+    at = [i for i, step in enumerate(plan) if step[0] == kind and s in (None, step[1])]
+    return at[0], at[-1] + 1
+
+
+def back_kernel(a, b, plan, unit_list, wave_steps, slot, temper, *refs):
+    bias_ref, q_ref, k_ref, v_ref, ctx_ref, lse_ref, grad_ref = refs[:7]
+    x_ref, gf_ref, wq_ref, wk_ref, wv_ref = refs[7:12]
+    vec, g_wo, g_w1, g_w2 = refs[12:16]
+    out_tokens, out_vec, out_bias = refs[16:19]
+    outs = refs[19:25]
+    rest = refs[25:]
+    gq_s, gk_s, gv_s, sum_q, sum_k, sum_v, bias_s, tok_s = rest[:8]
+    send, recv, local, tok_send, tok_recv, tok_local = rest[8:14]
+    rest = rest[14:]
+    steps = a + b
+    sources = {0: sum_q, 1: sum_k, 2: sum_v, 3: g_wo, 4: g_w1, 5: g_w2}
+    chunks, units = [(vec, out_vec, (), 0)], []
+    for unit in unit_list:
+        ids = []
+        for at, r, c, color in unit:
+            ids.append(len(chunks))
+            chunks.append((sources[at], outs[at], (r, c), color))
+        units.append(ids)
+    units[0] = [0] + units[0]
+    units[-1] = units[-1] + [len(chunks)]
+    chunks.append((bias_s, out_bias, (), 0))
+    landed = [rest[m * steps : (m + 1) * steps] for m in range(len(chunks))]
+    staged = rest[len(chunks) * steps :]
+    sums = Sums(a, b, chunks, landed, [staged[k] for k in slot], send, recv, local)
+    place = sums.place
+    i = pl.program_id(0)
+    n, length, width = gq_s.shape
+    sp = 1 << b
+
+    @pl.when(i == 0)
+    def _():
+        place.greet()
+
+    def token_moves(s):
+        out = [pltpu.make_async_copy(tok_s.at[s, place.z], out_tokens.at[place.z, s], tok_local.at[s])]
+        for k in range(1, sp):
+            to = lax.rem(place.z + k, sp)
+            out.append(
+                pltpu.make_async_remote_copy(
+                    src_ref=tok_s.at[s, to],
+                    dst_ref=out_tokens.at[place.z, s],
+                    send_sem=tok_send.at[s, k - 1],
+                    recv_sem=tok_recv.at[s, k - 1],
+                    device_id=(place.f, to),
+                    device_id_type=MESH,
+                )
+            )
+        return out
+
+    for s in range(n):
+        lo, hi = span(plan, "attend", s)
+
+        @pl.when(jnp.logical_and(i >= lo, i < hi))
+        def _(s=s, lo=lo):
+            columns = pl.ds(pl.multiple_of((i - lo) * 2 * HD, 2 * HD), 2 * HD)
+            gq, gk, gv = attend_back_pair(temper, bias_ref, q_ref, k_ref, v_ref, ctx_ref, lse_ref, grad_ref)
+            gq_s[s, :, columns] = gq
+            gk_s[s, :, columns] = gk
+            gv_s[s, :, columns] = gv
+
+        lo, hi = span(plan, "tokens", s)
+
+        @pl.when(jnp.logical_and(i >= lo, i < hi))
+        def _(s=s, lo=lo, hi=hi):
+            wide = wq_ref.shape[0]
+            columns = pl.ds(pl.multiple_of((i - lo) * wide, wide), wide)
+            total = dot_nt(gq_s[s], wq_ref[...]) + dot_nt(gk_s[s], wk_ref[...]) + dot_nt(gv_s[s], wv_ref[...])
+            total = total + gf_ref[...].reshape(length, wide)
+            tok_s[s, :, :, columns] = total.astype(BF).reshape(sp, length // sp, wide)
+
+            @pl.when(i == hi - 1)
+            def _():
+                for move in token_moves(s):
+                    move.start()
+
+    lo, hi = span(plan, "weights")
+
+    @pl.when(jnp.logical_and(i >= lo, i < hi))
+    def _():
+        wide = wq_ref.shape[0]
+        columns = pl.ds(pl.multiple_of((i - lo) * wide, wide), wide)
+        for held, total in ((gq_s, sum_q), (gk_s, sum_k), (gv_s, sum_v)):
+            value = sum(dot_tn(x_ref[:, s].reshape(length, width), held[s, :, columns]) for s in range(n))
+            shape = total.shape[:-1] + (wide,)
+            total[..., columns] = value.astype(BF).reshape(shape)
+
+        @pl.when(i == hi - 1)
+        def _():
+            for at, held in enumerate((gq_s, gv_s)):
+                row = sum(jnp.sum(held[s].astype(F32), axis=0, keepdims=True) for s in range(n))
+                rows = bias_s.shape[-2] // 2
+                wide = width // rows
+                for r in range(rows):
+                    cut = row[:, r * wide : (r + 1) * wide].reshape((1,) * steps + (1, wide))
+                    bias_s[..., at * rows + r : at * rows + r + 1, :] = jnp.broadcast_to(cut, (2,) * steps + (1, wide))
+
+    waves = wave_events(len(units), steps)
+    for k in sorted(set(wave_steps)):
+
+        @pl.when(i == k)
+        def _(k=k):
+            for wave, at in zip(waves, wave_steps):
+                if at == k:
+                    for unit, s in wave:
+                        sums.event(units[unit], s)
+
+    @pl.when(i == len(plan) - 1)
+    def _():
+        sums.finish()
+        for s in range(n):
+            for move in token_moves(s):
+                move.wait()
+
+
+def staging_plan(sizes, types, units):
+    keys, slot = [], [0] * len(sizes)
+    for ids in units:
+        seen = []
+        for m in ids:
+            key = (sizes[m], types[m])
+            key += (seen.count(key),)
+            seen.append(key[:2])
+            if key not in keys:
+                keys.append(key)
+            slot[m] = keys.index(key)
+    return slot, keys
+
+
+def back(a, b, bias, q, k, v, ctx, lse, grad_ctx, x, grad_first, wq, wk, wv, vec, g_wo, g_w1, g_w2):
+    lead, steps = (2,) * (a + b), a + b
     s, n, t, width = q.shape
-    rows = pl.BlockSpec((s, 1, t, 2 * HD), lambda i, j: (0, i, 0, j))
+    pairs, blocks = width // (2 * HD), 4
+    wide = width // blocks
+    length = s * t
+    plan = plan_steps(n, pairs, blocks)
+    rows = width >> steps
+    shapes = [(rows, width)] * 4 + [g_w1.shape[steps:], g_w2.shape[steps:]]
+    unit_list = make_units(shapes, SUM_PAIRS)
+    n_waves = len(unit_list) + steps
+    w_end = span(plan, "weights")[1]
+    last = len(plan) - 1
+    early = len(unit_list) - 2
+    wave_steps = []
+    for wave in range(n_waves):
+        if wave < early:
+            wave_steps.append(min(WAVE_STEPS[wave], w_end - 1) if wave < len(WAVE_STEPS) else w_end - 1)
+        else:
+            wave_steps.append(max(w_end, min(last, w_end + (wave - early))))
+    sizes = [vec.shape[steps:]] + [(r.size, c.size) for unit in unit_list for _, r, c, _ in unit]
+    sizes.append((2 * width // 128, 128))
+    types = [F32] + [BF] * (len(sizes) - 2) + [F32]
+
+    turn = pairs + blocks
+
+    def at_head(i):
+        seq = jnp.minimum(i // turn, n - 1)
+        return seq, jnp.minimum(i - seq * turn, pairs - 1)
+
+    def at_tokens(i):
+        ends = i >= (n - 1) * turn + pairs + blocks
+        seq = jnp.where(ends, n - 1, jnp.clip((i - pairs) // turn, 0, max(n - 2, 0)))
+        start = pairs + seq * turn + jnp.where(seq == n - 1, blocks, 0)
+        return seq, jnp.clip(i - start, 0, blocks - 1)
+
+    def head_map(i):
+        seq, pair = at_head(i)
+        return (0, seq, 0, pair)
+
+    def lse_map(i):
+        seq, pair = at_head(i)
+        return (seq, pair, 0, 0)
+
+    def token_map(i):
+        seq, block = at_tokens(i)
+        return (0, seq, 0, block)
+
+    def weight_map(i):
+        return (at_tokens(i)[1], 0)
+
+    head = pl.BlockSpec((s, 1, t, 2 * HD), head_map)
+    weight = pl.BlockSpec((wide, width), weight_map)
+    anyspace = pl.BlockSpec(memory_space=pl.ANY)
+    in_specs = [pl.BlockSpec((1, 1, length), lambda i: (at_head(i)[0], 0, 0))] + [head] * 4
+    in_specs += [pl.BlockSpec((1, 1, 8, length), lse_map), head]
+    in_specs += [pl.BlockSpec(x.shape, lambda i: (0, 0, 0, 0), pipeline_mode=pl.Buffered(1))]
+    in_specs += [pl.BlockSpec((s, 1, t, wide), token_map)] + [weight] * 3
+    in_specs += [anyspace] * 4
+    outs = [jax.ShapeDtypeStruct((s, n, t, width), BF)]
+    outs += [jax.ShapeDtypeStruct(sizes[0], F32), jax.ShapeDtypeStruct(sizes[-1], F32)]
+    outs += [jax.ShapeDtypeStruct(shape, F32) for shape in shapes]
+    vmem = pl.BlockSpec(memory_space=pltpu.VMEM)
+    n_chunks = len(sizes)
+    scratch = [pltpu.VMEM((n, length, width), BF)] * 3
+    scratch += [pltpu.VMEM(lead + (rows, width), BF)] * 3
+    scratch += [pltpu.VMEM(lead + sizes[-1], F32), pltpu.VMEM((n, s, t, width), BF)]
+    scratch += [
+        pltpu.SemaphoreType.DMA((n_chunks, steps)),
+        pltpu.SemaphoreType.DMA((n_chunks, steps)),
+        pltpu.SemaphoreType.DMA((n_chunks,)),
+        pltpu.SemaphoreType.DMA((n, s - 1)),
+        pltpu.SemaphoreType.DMA((n, s - 1)),
+        pltpu.SemaphoreType.DMA((n,)),
+    ]
+    for size, kind in zip(sizes, types):
+        scratch += [pltpu.VMEM((2,) * (steps - 1 - j) + size, kind) for j in range(steps)]
+    ids, at = [], 1
+    for unit in unit_list:
+        ids.append(list(range(at, at + len(unit))))
+        at += len(unit)
+    ids[0] = [0] + ids[0]
+    ids[-1] = ids[-1] + [at]
+    slot, keys = staging_plan(sizes, types, ids)
+    scratch += [pltpu.VMEM((2,) * (steps - 1) + size, kind) for size, kind, _ in keys]
     return pl.pallas_call(
-        functools.partial(attend_back_kernel, 1.0 / math.sqrt(HD)),
-        grid=(n, width // (2 * HD)),
-        out_shape=[jax.ShapeDtypeStruct(q.shape, BF)] * 3,
-        in_specs=[pl.BlockSpec((1, 1, s * t), lambda i, j: (i, 0, 0))] + [rows] * 6,
-        out_specs=[rows] * 3,
-        compiler_params=pltpu.CompilerParams(vmem_limit_bytes=32 * MIB),
-        cost_estimate=pl.CostEstimate(
-            flops=10 * n * (s * t) ** 2 * width, bytes_accessed=20 * s * n * t * width, transcendentals=0
+        functools.partial(back_kernel, a, b, plan, unit_list, wave_steps, slot, 1.0 / math.sqrt(HD)),
+        grid=(len(plan),),
+        out_shape=outs,
+        in_specs=in_specs,
+        out_specs=[anyspace] + [vmem] * (len(outs) - 1),
+        scratch_shapes=scratch,
+        compiler_params=pltpu.CompilerParams(
+            collective_id=1, has_side_effects=True, vmem_limit_bytes=60 * MIB
         ),
-        name="attend_back",
-    )(bias, q, k, v, ctx, lse, grad)
+        name="back_and_sum",
+    )(bias, q, k, v, ctx, lse, grad_ctx, x, grad_first, wq, wk, wv, vec, g_wo, g_w1, g_w2)
 
 
 def norm_forward(hidden, gain, shift):
@@ -556,21 +725,11 @@
     grad_attended = grad_first.astype(BF)
     g_wo = dot_tn(ctx_rows, grad_attended).astype(BF)
     grad_ctx = dot_nt(grad_attended, WO).astype(BF)
-    gq, gk, gv = attend_back(
-        bias, *(p.reshape(shard_shape) for p in (q, k, v)), ctx, lse, grad_ctx.reshape(shard_shape)
-    )
-    gq, gk, gv = (g.reshape(rows, width) for g in (gq, gk, gv))
-    g_wq = dot_tn(x, gq).astype(BF)
-    g_wk = dot_tn(x, gk).astype(BF)
-    g_wv = dot_tn(x, gv).astype(BF)
-    grad_tokens = (dot_nt(gq, WQ) + dot_nt(gk, WK) + dot_nt(gv, WV) + grad_first).astype(BF)
 
     def column_sum(value):
         return jnp.sum(value.astype(F32), axis=0)
 
     vector_grads = (
-        column_sum(gq),
-        column_sum(gv),
         column_sum(grad_attended),
         jnp.sum(grad_normed * xhat1, axis=0),
         column_sum(grad_normed),
@@ -587,19 +746,32 @@
     summed = back(
         a,
         b,
-        grad_tokens.reshape(shard_shape),
+        bias,
+        *(p.reshape(shard_shape) for p in (q, k, v)),
+        ctx,
+        lse,
+        grad_ctx.reshape(shard_shape),
+        moved,
+        grad_first.reshape(shard_shape),
+        WQ,
+        WK,
+        WV,
         packed.reshape(lead + (8, 128)),
-        [g.reshape(lead + w.shape) for g, w in zip((g_wq, g_wk, g_wv, g_wo, g_w1, g_w2), shards)],
+        *(g.reshape(lead + w.shape) for g, w in ((g_wo, wo), (g_w1, w1), (g_w2, w2))),
     )
     home = summed[0].reshape(seqs, part, width).astype(F32)
     own = summed[1].reshape(-1)
     small, at = [], 0
-    for size in sizes:
+    for g in vector_grads:
+        size = g.shape[0] // devices
         small.append(own[at : at + size])
         at += size
     loss = own[at] / (width * counted)
-    d_bq, d_bv, d_bo, d_g1, d_s1, d_b2, d_g2, d_s2, d_b1 = small
-    d_wq, d_wk, d_wv, d_wo, d_w1, d_w2 = summed[2:]
+    d_bo, d_g1, d_s1, d_b2, d_g2, d_s2, d_b1 = small
+    whole_sums = summed[2].reshape(2, width)
+    mine_at = (lax.axis_index("fsdp") * sp + z) * (width // devices)
+    d_bq, d_bv = (lax.dynamic_slice_in_dim(w, mine_at, width // devices, 0) for w in whole_sums)
+    d_wq, d_wk, d_wv, d_wo, d_w1, d_w2 = summed[3:]
     return (
         output.reshape(seqs, part, width),
         loss,

time: 554 us -> 491 us (0.89)
  Pallas kernels: 343 us -> 301 us
  matrix products: 135 us -> 120 us
    pallas_call x1, Pallas kernels: 156 us -> 130 us  [front(): pl.pallas_call(functools.partial(front_kernel, a, b, units), out_shape=ou...]
    pallas_call x2 -> x1, Pallas kernels: 167 us -> 151 us  [back(): pl.pallas_call(functools.partial(back_kernel, a, b, plan, unit_list, wave...]
    dot_general x6 -> x3, matrix products: 49.1 us -> 39 us  [dot_nt(): lax.dot_general(x, y, (((1,), (1,)), ((), ())), preferred_element_type=F32)]
    dot_general x6 -> x3, matrix products: 44.7 us -> 36.2 us  [dot_tn(): lax.dot_general(x, y, (((0,), (0,)), ((), ())), preferred_element_type=F32)]
    unnamed x92 -> x64, local copies, waits for them, and re-layouts: 16.7 us -> 12.3 us
    reduce_sum x5 -> x3, other arithmetic: 11.5 us -> 10.7 us  [column_sum(): return jnp.sum(value.astype(F32), axis=0)]
  transfers between devices with their start and end apart: 2 -> 2, of which waited for: 0 -> 0; matrix products, arithmetic and copies ran while one was open for 16% -> 17% of each run, Pallas kernels for 28% -> 35%
where the time goes in v1:
time: 491 us; the launch traced here: 483 us
  Pallas kernels  301 us (61%)
  matrix products  120 us (24%)
  local copies, waits for them, and re-layouts  26.6 us (5%)
  other arithmetic  18.8 us (4%)
  starting transfers between devices  9.2 us (2%)
  between operations  7.36 us (1%)
    pallas_call x1, Pallas kernels, back(): pl.pallas_call(functools.partial(back_kernel, a, b, plan, unit_list, wave...  151 us
    pallas_call x1, Pallas kernels, front(): pl.pallas_call(functools.partial(front_kernel, a, b, units), out_shape=ou...  130 us
    dot_general x6, matrix products, dot_nn(): lax.dot_general(x, y, (((1,), (0,)), ((), ())), preferred_element_type=F32)  45.2 us
    dot_general x3, matrix products, dot_nt(): lax.dot_general(x, y, (((1,), (1,)), ((), ())), preferred_element_type=F32)  39 us
    dot_general x3, matrix products, dot_tn(): lax.dot_general(x, y, (((0,), (0,)), ((), ())), preferred_element_type=F32)  36.2 us
    pallas_call x1, Pallas kernels, attend(): pl.pallas_call(functools.partial(attend_kernel, 1.0 / math.sqrt(HD)), gri...  19.9 us
    unnamed x64, local copies, waits for them, and re-layouts  12.3 us
    reduce_sum x3, other arithmetic, column_sum(): return jnp.sum(value.astype(F32), axis=0)  10.7 us
  transfers between devices with their start and end apart: 2, of which 0 were waited for; matrix products, arithmetic and copies ran while one was open for 17% of the time, Pallas kernels for 35%

profile of v1, /device:TPU:0, one launch (start us, length us, event | category | flops | bytes accessed | tf_op | source)
XLA Modules:
  0.0 483.0 jit_solution(8723154948394752505)
XLA Ops:
  0.7 1.4 dynamic-slice_reduce_fusion
  4.6 6.1 %concatenate.7 = bf16[386]{0:T(512)(128)(2,1)S(1)} concatenate(bf16[32]{0:T(256)(128)(2,1)} %param.22, bf16[32]{0:T(256)(128)(2,1)} %param.25, bf16[32]{0:T(256)(128)(2,1)} %param.27, bf16[32]{0:T(256)(128)(2,1)} %param.28, bf16[32]{0:T(256)(128)(2,1)} %param.29, bf16[32]{0:T(256)(128)(2,1)} %param.33, bf16[32]{0:T(256)(128)(2,1)} %param.34, bf16[32]{0:T(256)(128)(2,1)} %param.35, ...), dimensions={0} | concatenate | bytes 1544 | tf_op jit(solution)/shard_map/concatenate | solution.py:674
  10.8 0.6 pad_bitcast_fusion.1.refs_1_
  11.4 129.5 %gather_weights.1 = (bf16[4,2,128,1024]{3,2,1,0:T(8,128)(2,1)}, bf16[2,2,2,2,2,16,128]{6,5,4,3,2,1,0:T(8,128)(2,1)}, bf16[2,2,2,2,2,32,1024]{6,5,4,3,2,1,0:T(8,1...) custom-call(bf16[4,2,128,1024]{3,2,1,0:T(8,128)(2,1)} %bitcast.111, ...), custom_call_target="tpu_custom_call" | custom-call | tf_op jit(solution)/shard_map/gather_weights/pallas_call | solution.py:200
  140.9 3.8 all-to-all-start.1
  144.7 0.7 add_multiply_fusion.1
  145.5 0.7 convert_reduce_fusion.3
  146.1 0.1 slice_convert_fusion.1
  146.2 0.0 copy-start.6
  147.6 0.1 reshape.315
  147.7 0.1 reshape.311
  147.7 0.1 reshape.312
  147.8 0.1 reshape.316
  147.9 0.1 reshape.314
  148.0 0.1 reshape.310
  148.0 0.1 reshape.309
  148.1 0.1 reshape.308
  148.2 4.7 convolution_convert_fusion.4
  152.9 2.3 add_convert_fusion.1
  155.3 2.3 add_convert_fusion
  157.7 19.9 %attend.1 = (bf16[4,2,128,1024]{3,2,1,0:T(8,128)(2,1)S(1)}, f32[2,8,8,512]{3,2,1,0:T(8,128)S(1)}) custom-call(f32[2,1,512]{2,1,0:T(1,128)S(1)} %reshape.277.bias_ref.refs_0_, bf16[4,2,128,1024]{3,2,1,0:T(8,128)(2,1)S(1)} %bitcast.89, bf16[4,2,128,1024]{3,2,1,0:T(8,128)(2,1)S(1)} %bitcast.87, bf16[4,2,128,1024]{3,2,1,0:T(8,128)(2,1)S(1)} %bitcast.91), custom_call_target="tpu_custom_call" | custom-call | flops 2147483648 | bytes 16777216 | tf_op jit(solution)/shard_map/attend/pallas_call | solution.py:262
  177.6 2.5 fusion.17
  180.1 2.0 copy-done.9
  182.1 0.6 multiply_reduce_fusion.5
  182.7 18.5 %multiply_convert_fusion.1 = (bf16[1024,4096]{1,0:T(8,128)(2,1)S(1)}, f32[1024,4096]{1,0:T(8,128)}) fusion(f32[4096]{0:T(1024)S(1)} %fusion.8, bf16[1024,4096]{1,0:T(8,128)(2,1)} %bitcast.124, f32[1024,1024]{1,0:T(8,128)} %copy-done.9, f32[1024]{0:T(1024)S(1)} %reshape.312, f32[1024]{0:T(1024)S(1)} %reshape.311, f32[1024]{0:T(1024)S(1)} %add_rsqrt_fusion.1, ...), kind=kOutput, calls=%fused_computation.8 | convolution fusion | flops 8620343296 | bytes 37781504 | tf_op jit(solution)/shard_map/dot_general | solution.py:232
  201.2 14.8 %fusion.18 = (f32[1024]{0:T(1024)S(1)}, f32[1024,1024]{1,0:T(8,128)S(1)}) fusion(f32[1024]{0:T(1024)S(1)} %reshape.314, bf16[1024,4096]{1,0:T(8,128)(2,1)S(1)} %get-tuple-element.94, bf16[4096,1024]{1,0:T(8,128)(2,1)} %bitcast.126, f32[1024]{0:T(1024)S(1)} %reshape.312, f32[1024]{0:T(1024)S(1)} %reshape.311, f32[1024]{0:T(1024)S(1)} %add_rsqrt_fusion.1, ...), kind=kOutput, calls=%fused_computation.79 | convolution fusion | flops 8597273600 | bytes 25190400 | tf_op jit(solution)/shard_map/dot_general | solution.py:232
  216.0 1.9 copy-done.7
  217.9 0.5 multiply_reduce_fusion.4
  218.5 6.1 %multiply_reduce_fusion.8 = (f32[1024]{0:T(1024)S(1)}, f32[1024]{0:T(1024)S(1)}, f32[1024]{0:T(1024)S(1)}, f32[1024]{0:T(1024)S(1)}, f32[]{:T(128)}) fusion(f32[1024]{0:T(1024)S(1)} %broadcast_multiply_fusion, bf16[4,2,128,1024]{3,2,1,0:T(8,128)(2,1)S(1)} %all-to-all-done.1, f32[1024]{0:T(1024)S(1)} %reshape.316, f32[1024]{0:T(1024)S(1)} %reshape.315, ...), kind=kLoop, calls=%fused_computation.37 | loop fusion | flops 17821696 | bytes 6332420 | tf_op jit(solution)/shard_map/reduce_sum | solution.py:730
  224.6 3.2 convert_reduce_fusion.1
  227.8 20.5 %convert_reduce_fusion = (f32[4096]{0:T(1024)S(1)}, bf16[1024,4096]{1,0:T(8,128)(2,1)}) fusion(f32[1024,4096]{1,0:T(8,128)} %get-tuple-element.95, f32[4096]{0:T(1024)S(1)} %fusion.8, bf16[4096,1024]{1,0:T(8,128)(2,1)} %bitcast.127, f32[1024,1024]{1,0:T(8,128)S(1)} %get-tuple-element.70), kind=kOutput, calls=%fused_computation.6 | convolution fusion | flops 8653893632 | bytes 37781504 | tf_op jit(solution)/shard_map/dot_general | solution.py:224
  248.3 14.9 %multiply_reduce_fusion.1 = (f32[1024]{0:T(1024)S(1)}, f32[1024]{0:T(1024)S(1)}, f32[1024]{0:T(1024)S(1)}, f32[1024]{0:T(1024)S(1)}, f32[1024,1024]{1,0:T(8,128)S(1)}) fusion(f32[1024,1024]{1,0:T(8,128)S(1)} %copy-done.11, f32[1024]{0:T(1024)S(1)} %add_rsqrt_fusion.1, f32[1024]{0:T(1024)S(1)} %broadcast_multiply_fusion.6, f32[1024]{0:T(1024)S(1)} %reshape.311, ...), kind=kOutput, calls=%fused_computation.17 | convolution fusion | flops 8600416256 | bytes 29388800 | tf_op jit(solution)/shard_map/dot_general | solution.py:224
  263.2 15.1 %convolution_convert_fusion.1 = bf16[1024,4096]{1,0:T(8,128)(2,1)} fusion(bf16[1024,4096]{1,0:T(8,128)(2,1)} %get-tuple-element.100, f32[1024,1024]{1,0:T(8,128)S(1)} %copy-done.11, f32[1024]{0:T(1024)S(1)} %reshape.312, f32[1024]{0:T(1024)S(1)} %reshape.311, f32[1024]{0:T(1024)S(1)} %add_rsqrt_fusion.1, f32[1024]{0:T(1024)S(1)} %broadcast_multiply_fusion.6), kind=kOutput, calls=%fused_computation.11 | convolution fusion | flops 8599371776 | bytes 20987904 | tf_op jit(solution)/shard_map/dot_general | solution.py:228
  278.3 1.4 convert_reduce_fusion.2
  279.7 0.0 copy-start.12
  279.7 0.2 copy-done.25
  279.9 3.7 convolution_convert_fusion.3
  283.6 5.4 %all-to-all-start = ((bf16[4,2,128,1024]{3,2,1,0:T(8,128)(2,1)}), bf16[4,2,128,1024]{3,2,1,0:T(8,128)(2,1)}, u32[]{:S(2)}, u32[]{:S(2)}) async-start(bf16[4,2,128,1024]{3,2,1,0:T(8,128)(2,1)} %bitcast.96), calls=%async_computation | async-start | bytes 4194304 | tf_op jit(solution)/shard_map/all_to_all | solution.py:715
  289.0 5.9 %convolution_convert_fusion.2 = bf16[1024,1024]{1,0:T(8,128)(2,1)} fusion(bf16[1024,1024]{1,0:T(8,128)(2,1)S(1)} %bitcast.94, f32[1024,1024]{1,0:T(8,128)} %copy-done.12), kind=kOutput, calls=%fused_computation.40 | convolution fusion | flops 2149580800 | bytes 8388608 | tf_op jit(solution)/shard_map/dot_general | solution.py:228
  295.0 0.1 reshape.296
  295.0 0.1 reshape.299
  295.1 0.1 reshape.297
  295.2 0.1 reshape.301
  295.2 0.1 reshape.298
  295.3 0.1 reshape.300
  295.4 0.7 broadcast_in_dim.2
  296.1 0.1 concatenate.8
  296.2 0.7 copy.38
  296.9 15.2 %convolution_convert_fusion = bf16[4096,1024]{1,0:T(8,128)(2,1)} fusion(bf16[1024,4096]{1,0:T(8,128)(2,1)} %copy-done.26, f32[1024,1024]{1,0:T(8,128)} %copy-done.13), kind=kOutput, calls=%fused_computation.10 | convolution fusion | flops 8595177472 | bytes 20971520 | tf_op jit(solution)/shard_map/dot_general | solution.py:228
  312.1 151.2 %back_and_sum.1 = (bf16[4,2,128,1024]{3,2,1,0:T(8,128)(2,1)}, f32[8,128]{1,0:T(8,128)}, f32[16,128]{1,0:T(8,128)}, f32[32,1024]{1,0:T(8,128)}, f32[32,1024]{1,0:...) custom-call(f32[2,1,512]{2,1,0:T(1,128)} %copy-done.6, ...), custom_call_target="tpu_custom_call" | custom-call | tf_op jit(solution)/shard_map/back_and_sum/pallas_call | solution.py:623
  463.3 1.3 slice.70
  464.6 1.3 slice.74
  465.8 0.7 slice_bitcast_fusion.1
  466.5 0.6 dynamic_slice.11
  467.1 0.6 dynamic_slice.10
  468.3 1.5 fusion.16
  469.8 4.1 bitcast_convert_fusion
  474.0 3.2 copy.48
  477.2 0.7 copy.49
  477.8 0.7 copy.50
  478.5 0.7 copy.51
  479.1 0.7 copy.52
  479.8 0.8 copy.53
  480.6 0.8 copy.54
  (63 shorter events, 0.2 us)
Async XLA Ops:
  140.9 4.5 copy-start.23
  140.9 77.6 %all-to-all-start.1 = ((bf16[4,2,128,1024]{3,2,1,0:T(8,128)(2,1)}), bf16[4,2,128,1024]{3,2,1,0:T(8,128)(2,1)S(1)}, u32[]{:S(2)}, u32[]{:S(2)}) async-start(bf16[4,2,128,1024]{3,2,1,0:T(8,128)(2,1)} %bitcast.112), calls=%async_computation.1 | async-start | bytes 4194304 | tf_op jit(solution)/shard_map/all_to_all | solution.py:690
  146.2 11.4 %copy-start.6 = (f32[2,1,512]{2,1,0:T(1,128)}, f32[2,1,512]{2,1,0:T(1,128)S(1)}, u32[]{:S(2)}) copy-start(f32[2,1,512]{2,1,0:T(1,128)S(1)} %reshape.277.bias_ref.refs_0_) | copy-start | bytes 12292
  148.2 4.7 copy-start.14
  148.2 4.7 copy-start.15
  152.9 4.8 copy-start
  152.9 2.4 copy-start.16
  155.3 2.4 copy-start.1
  157.6 22.4 %copy-start.2 = (bf16[1024,1024]{1,0:T(8,128)(2,1)}, bf16[1024,1024]{1,0:T(8,128)(2,1)S(1)}, u32[]{:S(2)}) copy-start(bf16[1024,1024]{1,0:T(8,128)(2,1)S(1)} %add_convert_fusion) | copy-start | bytes 6291460
  157.6 19.9 %copy-start.24 = (bf16[2,2,2,2,2,32,1024]{6,5,4,3,2,1,0:T(8,128)(2,1)S(1)}, bf16[2,2,2,2,2,32,1024]{6,5,4,3,2,1,0:T(8,128)(2,1)}, u32[]{:S(2)}) copy-start(bf16[2,2,2,2,2,32,1024]{6,5,4,3,2,1,0:T(8,128)(2,1)} %get-tuple-element.44) | copy-start | bytes 6291460
  177.5 2.5 copy-start.3
  177.5 2.5 copy-start.5
  180.1 2.0 copy-start.9
  182.6 18.5 %copy-start.10 = (f32[1024,1024]{1,0:T(8,128)S(1)}, f32[1024,1024]{1,0:T(8,128)}, u32[]{:S(2)}) copy-start(f32[1024,1024]{1,0:T(8,128)} %copy-done.9) | copy-start | bytes 12582916
  201.2 14.8 %copy-start.26 = (bf16[1024,4096]{1,0:T(8,128)(2,1)}, bf16[1024,4096]{1,0:T(8,128)(2,1)S(1)}, u32[]{:S(2)}) copy-start(bf16[1024,4096]{1,0:T(8,128)(2,1)S(1)} %get-tuple-element.94) | copy-start | bytes 25165828
  216.0 1.9 copy-start.7
  218.5 6.1 %copy-start.8 = (f32[1024,1024]{1,0:T(8,128)S(1)}, f32[1024,1024]{1,0:T(8,128)}, u32[]{:S(2)}) copy-start(f32[1024,1024]{1,0:T(8,128)} %copy-done.7) | copy-start | bytes 12582916
  227.8 20.5 %copy-start.13 = (f32[1024,1024]{1,0:T(8,128)}, f32[1024,1024]{1,0:T(8,128)S(1)}, u32[]{:S(2)}) copy-start(f32[1024,1024]{1,0:T(8,128)S(1)} %get-tuple-element.70) | copy-start | bytes 12582916
  227.8 20.5 %copy-start.11 = (f32[1024,1024]{1,0:T(8,128)S(1)}, f32[1024,1024]{1,0:T(8,128)}, u32[]{:S(2)}) copy-start(f32[1024,1024]{1,0:T(8,128)} %copy-done.9) | copy-start | bytes 12582916
  278.3 1.6 copy-start.25
  279.7 3.9 copy-start.12
  283.6 5.5 %copy-start.4 = (bf16[4,2,128,1024]{3,2,1,0:T(8,128)(2,1)S(1)}, bf16[4,2,128,1024]{3,2,1,0:T(8,128)(2,1)}, u32[]{:S(2)}) copy-start(bf16[4,2,128,1024]{3,2,1,0:T(8,128)(2,1)} %copy-done.3) | copy-start | bytes 6291460
  283.6 190.4 %all-to-all-start = ((bf16[4,2,128,1024]{3,2,1,0:T(8,128)(2,1)}), bf16[4,2,128,1024]{3,2,1,0:T(8,128)(2,1)}, u32[]{:S(2)}, u32[]{:S(2)}) async-start(bf16[4,2,128,1024]{3,2,1,0:T(8,128)(2,1)} %bitcast.96), calls=%async_computation | async-start | bytes 4194304 | tf_op jit(solution)/shard_map/all_to_all | solution.py:715
  469.8 7.3 %copy-start.22 = (f32[32,1024]{1,0:T(8,128)S(1)}, f32[32,1024]{1,0:T(8,128)}, u32[]{:S(2)}) copy-start(f32[32,1024]{1,0:T(8,128)} %get-tuple-element.124) | copy-start | bytes 393220
  469.8 8.0 %copy-start.21 = (f32[32,1024]{1,0:T(8,128)S(1)}, f32[32,1024]{1,0:T(8,128)}, u32[]{:S(2)}) copy-start(f32[32,1024]{1,0:T(8,128)} %get-tuple-element.126) | copy-start | bytes 393220
  469.8 8.6 %copy-start.20 = (f32[32,1024]{1,0:T(8,128)S(1)}, f32[32,1024]{1,0:T(8,128)}, u32[]{:S(2)}) copy-start(f32[32,1024]{1,0:T(8,128)} %get-tuple-element.127) | copy-start | bytes 393220
  469.8 9.3 %copy-start.19 = (f32[32,1024]{1,0:T(8,128)S(1)}, f32[32,1024]{1,0:T(8,128)}, u32[]{:S(2)}) copy-start(f32[32,1024]{1,0:T(8,128)} %get-tuple-element.129) | copy-start | bytes 393220
  474.0 5.8 %copy-start.18 = (f32[32,4096]{1,0:T(8,128)S(1)}, f32[32,4096]{1,0:T(8,128)}, u32[]{:S(2)}) copy-start(f32[32,4096]{1,0:T(8,128)} %get-tuple-element.133) | copy-start | bytes 1572868
  474.0 6.6 %copy-start.17 = (f32[128,1024]{1,0:T(8,128)S(1)}, f32[128,1024]{1,0:T(8,128)}, u32[]{:S(2)}) copy-start(f32[128,1024]{1,0:T(8,128)} %get-tuple-element.135) | copy-start | bytes 1572868

commit v2 on v1

--- a/solution.py
+++ b/solution.py
@@ -15,8 +15,6 @@
 AXES = ("fsdp", "sp")
 MIB = 1 << 20
 GATHER_PAIRS = ((0, 1, 1), (2, 3, 1), (4, 5, 4))
-SUM_PAIRS = ((4, 5, 4), (3, 3, 1), (0, 1, 1), (2, 2, 1))
-WAVE_STEPS = (0, 2, 5, 12, 19)
 
 
 def bits_of(n):
@@ -276,14 +274,7 @@
     )(bias, q, k, v)
 
 
-def attend_back_pair(temper, bias_ref, q_ref, k_ref, v_ref, ctx_ref, lse_ref, grad_ref):
-    length = bias_ref.shape[-1]
-
-    def whole(ref):
-        return ref[...].reshape(length, ref.shape[-1])
-
-    q, k, v, ctx, grad = (whole(r) for r in (q_ref, k_ref, v_ref, ctx_ref, grad_ref))
-    key_bias = jnp.transpose(jnp.broadcast_to(bias_ref[...].reshape(1, length), (2 * HD, length)))[:, :1]
+def attend_back_pair(temper, key_bias, q, k, v, ctx, logs, grad):
     both = jnp.transpose(grad.astype(F32) * ctx.astype(F32))
     gq = jnp.zeros(q.shape, F32)
     gk = jnp.zeros(q.shape, F32)
@@ -292,7 +283,7 @@
         mask = head_mask(head)
         k_head = k * (mask * temper).astype(BF)
         grad_head = grad * mask.astype(BF)
-        log_total = lse_ref[0, 0, head : head + 1]
+        log_total = logs[head : head + 1]
         inner = jnp.sum(both[head * HD : (head + 1) * HD], axis=0, keepdims=True)
         attention = jnp.exp(dot_nt(k_head, q) + key_bias - log_total)
         gv = gv + dot_nn(attention.astype(BF), grad_head)
@@ -346,57 +337,50 @@
 
     def add(self, m, s):
         total, index = self.landed[m][0], self.later(m, self.index(m, s, False))
-        other = self.staged[m] if s == 0 else self.landed[m][s]
+        other = self.landed[m][s]
+        if s == 0:
+            src, _, piece, _ = self.chunks[m]
+            other = self.staged[m]
+            if other is None:
+                other = src.at[tuple(self.index(m, 0, False)) + piece]
         if s == self.steps - 1:
             out, piece = self.chunks[m][1], self.chunks[m][2]
             value = total[index].astype(F32) + other[...].astype(F32)
-            out[piece if piece else ...] = value
+            out[piece] = value
             return
         free = [d for d, v in enumerate(index) if isinstance(v, slice)]
 
         def one(i, carry):
-            at, bits = list(index), []
-            for j, d in enumerate(free):
-                at[d] = lax.rem(i // (1 << (len(free) - 1 - j)), 2)
-                bits.append(at[d])
-            value = total[tuple(at)].astype(F32) + other[tuple(bits)].astype(F32)
-            total[tuple(at)] = value.astype(total.dtype)
+            at = list(index)
+            at[free[0]] = i
+            total[tuple(at)] = total[tuple(at)] + other[i]
             return carry
 
-        lax.fori_loop(0, 1 << len(free), one, 0)
-
-    def event(self, unit, s):
-        for m in unit:
-            if s == 1:
-                self.keep(m).start()
+        lax.fori_loop(0, 2, one, 0)
+
+    def event(self, unit, s, load):
         for m in unit:
             if s > 0:
                 self.copy(m, s - 1).wait_recv()
-                if s == 1:
+                if s == 1 and self.staged[m] is not None:
                     self.keep(m).wait()
                 self.add(m, s - 1)
             if s < self.steps:
                 self.copy(m, s).start()
-
-    def finish(self):
-        for m in range(len(self.chunks)):
-            for s in range(self.steps):
-                self.copy(m, s).wait_send()
-
-
-def wave_events(units, steps):
-    waves = []
-    for t in range(units + steps):
-        waves.append([(t - k, k) for k in range(steps, -1, -1) if 0 <= t - k < units])
-    return waves
-
-
-def plan_steps(n, pairs, blocks):
-    out = []
+            else:
+                for k in range(self.steps):
+                    self.copy(m, k).wait_send()
+        for m in load:
+            if self.staged[m] is not None:
+                self.keep(m).start()
+
+
+def plan_steps(n, hidden, parts, blocks):
+    out = [("hidden", 0, j) for j in range(hidden)]
+    out += [("norm", 0, k) for k in range(parts)]
+    out += [("project", 0, r) for r in range(blocks)]
     for s in range(n):
-        out += [("attend", s, p) for p in range(pairs)]
-        if s == n - 1:
-            out += [("weights", 0, c) for c in range(blocks)]
+        out += [("attend" if s < n - 1 else "last", s, c) for c in range(blocks)]
         out += [("tokens", s, r) for r in range(blocks)]
     return out
 
@@ -406,39 +390,173 @@
     return at[0], at[-1] + 1
 
 
-def back_kernel(a, b, plan, unit_list, wave_steps, slot, temper, *refs):
-    bias_ref, q_ref, k_ref, v_ref, ctx_ref, lse_ref, grad_ref = refs[:7]
-    x_ref, gf_ref, wq_ref, wk_ref, wv_ref = refs[7:12]
-    vec, g_wo, g_w1, g_w2 = refs[12:16]
-    out_tokens, out_vec, out_bias = refs[16:19]
-    outs = refs[19:25]
-    rest = refs[25:]
-    gq_s, gk_s, gv_s, sum_q, sum_k, sum_v, bias_s, tok_s = rest[:8]
-    send, recv, local, tok_send, tok_recv, tok_local = rest[8:14]
-    rest = rest[14:]
+STEP_US = {"hidden": 6.6, "norm": 1.2, "project": 2.2, "attend": 3.4, "last": 4.8, "tokens": 1.9}
+LINK_US = 23.0
+CORE_US = 3.0
+HOP_US = 2.5
+SLACK_US = 0.0
+LATE_US = -0.5
+
+
+def plan_events(plan, units, ready, late, a, b):
+    steps = a + b
+    ends, now = [], 0.0
+    for kind, _, _ in plan:
+        now += STEP_US[kind]
+        ends.append(now)
+    free, events = {}, []
+    due = [[ends[r], u, 0] for u, r in enumerate(ready)]
+    while due:
+        due.sort()
+        time, u, k = due.pop(0)
+        slack = SLACK_US if u < late else LATE_US
+        at = min([i for i, end in enumerate(ends) if end >= time + slack] + [len(plan) - 1])
+        start = max(time, ends[at])
+        events.append((at, start, u, k))
+        if k == steps:
+            continue
+        came_all = start
+        for size, color in units[u]:
+            where = gather_steps(a, b, color)[::-1][k]
+            cost = CORE_US if where == ("fsdp", 0) else LINK_US
+            free[where] = max(free.get(where, 0.0), start) + size / (1 << (k + 1)) * cost
+            came_all = max(came_all, free[where])
+        due.append([came_all + HOP_US, u, k + 1])
+    waiting, order, place = sorted(events), [], {}
+    while waiting:
+        for i, (at, _, u, k) in enumerate(waiting):
+            before = [(u, k - 1)] if k else []
+            if k == 1 and u:
+                before.append((u - 1, 1))
+            if late - 1 <= u < len(units) - 1:
+                before.append((u + 1 - late, steps))
+            if not all(b in place for b in before):
+                continue
+            if u < late or k == steps:
+                break
+            freed = place.get((u - late, steps), len(events))
+            if any(place.get((w, k), -1) > freed and (w, k + 1) in place for w in range(u)):
+                break
+        at, _, u, k = waiting.pop(i)
+        place[u, k] = len(order)
+        order.append((max(at, order[-1][0]) if order else at, u, k))
+    loads = [-1] * len(order)
+    for u in range(len(units)):
+        loads[place[u, 0] if u == 0 else max(place[u, 0], place[u - 1, 1])] = u
+    return [event + (load,) for event, load in zip(order, loads)]
+
+
+def staging_plan(sizes, types, units, loaded):
+    keys, slot = [], [None] * len(sizes)
+    for ids in units:
+        used = {}
+        for m in ids:
+            if not loaded[m]:
+                slot[m] = (-1, 0, 0)
+                continue
+            (r, c), kind = sizes[m], types[m]
+            for k, (rows, columns, had) in enumerate(keys):
+                if rows == r and had == kind and used.get(k, 0) + c <= columns:
+                    break
+            else:
+                k = len(keys)
+                keys.append((r, c, kind))
+            slot[m] = (k, used.get(k, 0), c)
+            used[k] = used.get(k, 0) + c
+    return slot, keys
+
+
+def sum_units(shapes, blocks):
+    units = []
+    r, c = shapes[4]
+    parts = pieces(r, c, 1, 8)
+    units += [[(4,) + parts[k] + (0,), (4,) + parts[k + 1] + (1,)] for k in range(0, 8, 2)]
+    r, c = shapes[5]
+    tall = min(4, r // 16)
+    parts = pieces(r, c, tall, 8 // tall)
+    units += [[(5,) + parts[k] + (0,), (5,) + parts[k + 1] + (1,)] for k in range(0, 8, 2)]
+    r, c = shapes[3]
+    left, right = pieces(r, c, 1, 2)
+    units.append([(3,) + left + (0,), (3,) + right + (1,)])
+    r, c = shapes[0]
+    for k in range(blocks):
+        whole = pieces(r, c, 1, blocks)[k]
+        left, right = pieces(r, c, 1, 2 * blocks)[2 * k : 2 * k + 2]
+        units.append([(0,) + whole + (0,), (1,) + whole + (1,), (2,) + left + (0,), (2,) + right + (1,)])
+    return units
+
+
+def bits_index(value, count):
+    return tuple(lax.rem(value // (1 << (count - 1 - k)), 2) for k in range(count))
+
+
+def back_kernel(a, b, plan, unit_list, events, slot, lands, temper, *refs):
+    bias_ref, q_ref, k_ref, v_ref, ctx_ref, lse_ref = refs[:6]
+    active_ref, slope_ref, w2_ref, w1_ref = refs[6:10]
+    xhat_ref, scale_ref, gain_ref, wide_ctx_ref, wo_ref = refs[10:15]
+    x_ref, wq_ref, wk_ref, wv_ref = refs[15:19]
+    vec_ref, grad_outer, normed_low, grad_second = refs[19:23]
+    out_tokens, out_bias = refs[23:25]
+    outs = refs[25:31]
+    g_wo, g_w1, g_w2 = refs[31:34]
+    rest = refs[34:]
+    gq_s, gk_s, gv_s, sum_q, sum_k, sum_v, bias_s, tok_s, flow, lines, w2_st = rest[:11]
+    send, recv, local, tok_send, tok_recv, tok_local, put = rest[11:18]
+    rest = rest[18:]
     steps = a + b
     sources = {0: sum_q, 1: sum_k, 2: sum_v, 3: g_wo, 4: g_w1, 5: g_w2}
-    chunks, units = [(vec, out_vec, (), 0)], []
+    chunks, units = [], []
     for unit in unit_list:
         ids = []
         for at, r, c, color in unit:
             ids.append(len(chunks))
             chunks.append((sources[at], outs[at], (r, c), color))
         units.append(ids)
-    units[0] = [0] + units[0]
     units[-1] = units[-1] + [len(chunks)]
-    chunks.append((bias_s, out_bias, (), 0))
-    landed = [rest[m * steps : (m + 1) * steps] for m in range(len(chunks))]
-    staged = rest[len(chunks) * steps :]
-    sums = Sums(a, b, chunks, landed, [staged[k] for k in slot], send, recv, local)
+    chunks.append((bias_s, out_bias, (slice(None), slice(None)), 0))
+    landed = []
+    for at, start, size in lands:
+        refs_of = rest[at * steps : (at + 1) * steps]
+        if size != refs_of[0].shape[-1]:
+            refs_of = [
+                r.at[(slice(None),) * (len(r.shape) - 1) + (pl.ds(start, size),)] for r in refs_of
+            ]
+        landed.append(refs_of)
+    staged = rest[(1 + max(at for at, _, _ in lands)) * steps :]
+    views = []
+    for m, (k, start, size) in enumerate(slot):
+        if k < 0:
+            views.append(None)
+            continue
+        ref = staged[k]
+        if size != ref.shape[-1]:
+            ref = ref.at[(slice(None),) * steps + (pl.ds(start, size),)]
+        views.append(ref)
+    sums = Sums(a, b, chunks, landed, views, send, recv, local)
     place = sums.place
     i = pl.program_id(0)
     n, length, width = gq_s.shape
     sp = 1 << b
+    part = length // sp
+    rows = n * length
+    hidden = span(plan, "hidden")[1]
+    wide = wq_ref.shape[0]
+    h = w1_ref.shape[1]
+
+    loads = [
+        pltpu.make_async_copy(grad_outer, gq_s, put.at[0]),
+        pltpu.make_async_copy(normed_low, gk_s, put.at[1]),
+        pltpu.make_async_copy(grad_second, flow, put.at[2]),
+    ]
 
     @pl.when(i == 0)
     def _():
+        for load in loads:
+            load.start()
         place.greet()
+        for load in loads:
+            load.wait()
+        lines[...] = jnp.zeros_like(lines)
 
     def token_moves(s):
         out = [pltpu.make_async_copy(tok_s.at[s, place.z], out_tokens.at[place.z, s], tok_local.at[s])]
@@ -456,120 +574,191 @@
             )
         return out
 
-    for s in range(n):
-        lo, hi = span(plan, "attend", s)
-
-        @pl.when(jnp.logical_and(i >= lo, i < hi))
-        def _(s=s, lo=lo):
-            columns = pl.ds(pl.multiple_of((i - lo) * 2 * HD, 2 * HD), 2 * HD)
-            gq, gk, gv = attend_back_pair(temper, bias_ref, q_ref, k_ref, v_ref, ctx_ref, lse_ref, grad_ref)
+    def puts(j):
+        at = lax.rem(j, 2)
+        columns = pl.ds(pl.multiple_of(j * h, h), h)
+        held = pl.ds(pl.multiple_of(at * h, h), h)
+        to_w1 = g_w1.at[(slice(None),) * (steps + 1) + (columns,)]
+        to_w2 = g_w2.at[bits_index(j, bits_of(hidden))]
+        return [
+            pltpu.make_async_copy(sum_q.at[(slice(None),) * (steps + 1) + (held,)], to_w1, put.at[3 + at]),
+            pltpu.make_async_copy(w2_st.at[at], to_w2, put.at[5 + at]),
+        ]
+
+    @pl.when(i < hidden)
+    def _():
+        at = lax.rem(i, 2)
+        grad_out = gq_s[...].reshape(rows, width)
+        normed = gk_s[...].reshape(rows, width)
+        grad_active = dot_nt(grad_out, w2_ref[...])
+        grad_inner = (grad_active * slope_ref[...].astype(F32)).astype(BF)
+        columns = pl.ds(pl.multiple_of(i * h, h), h)
+        lines[0:1, columns] = jnp.sum(grad_inner.astype(F32), axis=0, keepdims=True)
+        value = dot_tn(normed, grad_inner).astype(BF)
+        sum_q[..., pl.ds(pl.multiple_of(at * h, h), h)] = value.reshape(sum_q.shape[:-1] + (h,))
+        value = dot_tn(active_ref[...], grad_out).astype(BF)
+        w2_st[at] = value.reshape(w2_st.shape[1:])
+        for p in puts(i):
+            p.start()
+        flow[...] += dot_nt(grad_inner, w1_ref[...]).reshape(flow.shape)
+
+        @pl.when(i > 0)
+        def _():
+            for p in puts(i - 1):
+                p.wait()
+
+    lo, hi = span(plan, "norm")
+
+    @pl.when(i == lo)
+    def _():
+        for p in puts(hidden - 1):
+            p.wait()
+
+    @pl.when(jnp.logical_and(i >= lo, i < hi))
+    def _():
+        zb = i - lo
+        for s in range(n):
+            grad = flow[zb, s]
+            xhat = xhat_ref[0, s].astype(F32)
+            scaled = grad * gain_ref[...]
+            mean = jnp.mean(scaled, axis=-1, keepdims=True)
+            slope = jnp.mean(scaled * xhat, axis=-1, keepdims=True)
+            first = scale_ref[0, s] * (scaled - mean - xhat * slope)
+            flow[zb, s] = first
+            low = first.astype(BF)
+            tok_s[s, zb] = low
+            for at, value in ((1, grad * xhat), (2, grad), (3, low.astype(F32))):
+                lines[at : at + 1, :width] += jnp.sum(value, axis=0, keepdims=True)
+
+    lo, hi = span(plan, "project")
+    first_attend = hi
+    put_wo = pltpu.make_async_copy(sum_v, g_wo, put.at[7])
+
+    @pl.when(jnp.logical_and(i >= lo, i < hi))
+    def _():
+        r = i - lo
+        columns = pl.ds(pl.multiple_of(r * wide, wide), wide)
+        total = jnp.zeros((wide, width), F32)
+        for s in range(n):
+            grad = tok_s[s].reshape(length, width)
+            gv_s[s, :, columns] = dot_nt(grad, wo_ref[...]).astype(BF)
+            total = total + dot_tn(wide_ctx_ref[:, s].reshape(length, wide), grad)
+        index = bits_index(r, bits_of(hi - lo))
+        sum_v[index] = total.astype(BF).reshape(sum_v.shape[len(index) :])
+
+        @pl.when(i == hi - 1)
+        def _():
+            put_wo.start()
+
+    @pl.when(i == first_attend)
+    def _():
+        put_wo.wait()
+
+    def attend_step(s, c):
+        bias_rows = jnp.broadcast_to(bias_ref[...].reshape(1, length), (2 * HD, length))
+        key_bias = jnp.transpose(bias_rows)[:, :1]
+        for pair in range(wide // (2 * HD)):
+            cut = slice(pair * 2 * HD, (pair + 1) * 2 * HD)
+            columns = pl.ds(pl.multiple_of(c * wide + pair * 2 * HD, 2 * HD), 2 * HD)
+            q, k, v, ctx = (r[:, 0, :, cut].reshape(length, 2 * HD) for r in (q_ref, k_ref, v_ref, ctx_ref))
+            logs = lse_ref[0, pair, 0:2]
+            gq, gk, gv = attend_back_pair(temper, key_bias, q, k, v, ctx, logs, gv_s[s, :, columns])
             gq_s[s, :, columns] = gq
             gk_s[s, :, columns] = gk
             gv_s[s, :, columns] = gv
 
+    def weights_step(c):
+        columns = pl.ds(pl.multiple_of(c * wide, wide), wide)
+        for at, held, total in ((4, gq_s, sum_q), (None, gk_s, sum_k), (5, gv_s, sum_v)):
+            value = sum(dot_tn(x_ref[:, s].reshape(length, width), held[s, :, columns]) for s in range(n))
+            total[..., columns] = value.astype(BF).reshape(total.shape[:-1] + (wide,))
+            if at is not None:
+                row = sum(jnp.sum(held[s, :, columns].astype(F32), axis=0, keepdims=True) for s in range(n))
+                lines[at : at + 1, columns] = row
+
+    for s in range(n):
+        lo, hi = span(plan, "attend" if s < n - 1 else "last", s)
+
+        @pl.when(jnp.logical_and(i >= lo, i < hi))
+        def _(s=s, lo=lo):
+            attend_step(s, i - lo)
+            if s == n - 1:
+                weights_step(i - lo)
+
         lo, hi = span(plan, "tokens", s)
 
         @pl.when(jnp.logical_and(i >= lo, i < hi))
         def _(s=s, lo=lo, hi=hi):
-            wide = wq_ref.shape[0]
             columns = pl.ds(pl.multiple_of((i - lo) * wide, wide), wide)
             total = dot_nt(gq_s[s], wq_ref[...]) + dot_nt(gk_s[s], wk_ref[...]) + dot_nt(gv_s[s], wv_ref[...])
-            total = total + gf_ref[...].reshape(length, wide)
-            tok_s[s, :, :, columns] = total.astype(BF).reshape(sp, length // sp, wide)
+            total = total + flow[:, s, :, columns].reshape(length, wide)
+            tok_s[s, :, :, columns] = total.astype(BF).reshape(sp, part, wide)
 
             @pl.when(i == hi - 1)
             def _():
                 for move in token_moves(s):
                     move.start()
 
-    lo, hi = span(plan, "weights")
-
-    @pl.when(jnp.logical_and(i >= lo, i < hi))
+    @pl.when(i == span(plan, "last")[1] - 1)
     def _():
-        wide = wq_ref.shape[0]
-        columns = pl.ds(pl.multiple_of((i - lo) * wide, wide), wide)
-        for held, total in ((gq_s, sum_q), (gk_s, sum_k), (gv_s, sum_v)):
-            value = sum(dot_tn(x_ref[:, s].reshape(length, width), held[s, :, columns]) for s in range(n))
-            shape = total.shape[:-1] + (wide,)
-            total[..., columns] = value.astype(BF).reshape(shape)
-
-        @pl.when(i == hi - 1)
-        def _():
-            for at, held in enumerate((gq_s, gv_s)):
-                row = sum(jnp.sum(held[s].astype(F32), axis=0, keepdims=True) for s in range(n))
-                rows = bias_s.shape[-2] // 2
-                wide = width // rows
-                for r in range(rows):
-                    cut = row[:, r * wide : (r + 1) * wide].reshape((1,) * steps + (1, wide))
-                    bias_s[..., at * rows + r : at * rows + r + 1, :] = jnp.broadcast_to(cut, (2,) * steps + (1, wide))
-
-    waves = wave_events(len(units), steps)
-    for k in sorted(set(wave_steps)):
+        devices = 1 << steps
+        for d in range(devices):
+            index = tuple((d >> (steps - 1 - k)) & 1 for k in range(steps))
+            for at in range(6):
+                size = (hidden * h if at == 0 else width) // devices
+                tile = d * size // 128
+                bias_s[index + (slice(at, at + 1),)] = lines[at : at + 1, tile * 128 : tile * 128 + 128]
+            bias_s[index + (slice(6, 7),)] = vec_ref[d : d + 1]
+
+    for k in sorted({event[0] for event in events}):
 
         @pl.when(i == k)
         def _(k=k):
-            for wave, at in zip(waves, wave_steps):
+            for at, unit, s, load in events:
                 if at == k:
-                    for unit, s in wave:
-                        sums.event(units[unit], s)
+                    sums.event(units[unit], s, units[load] if load >= 0 else ())
 
     @pl.when(i == len(plan) - 1)
     def _():
-        sums.finish()
         for s in range(n):
             for move in token_moves(s):
                 move.wait()
 
 
-def staging_plan(sizes, types, units):
-    keys, slot = [], [0] * len(sizes)
-    for ids in units:
-        seen = []
-        for m in ids:
-            key = (sizes[m], types[m])
-            key += (seen.count(key),)
-            seen.append(key[:2])
-            if key not in keys:
-                keys.append(key)
-            slot[m] = keys.index(key)
-    return slot, keys
-
-
-def back(a, b, bias, q, k, v, ctx, lse, grad_ctx, x, grad_first, wq, wk, wv, vec, g_wo, g_w1, g_w2):
+def back(a, b, bias, heads, lse, active, slope, W2, W1, xhat, scale, gain, WO, x, WQ, WK, WV, grads, vec):
+    q, k, v, ctx = heads
     lead, steps = (2,) * (a + b), a + b
     s, n, t, width = q.shape
-    pairs, blocks = width // (2 * HD), 4
-    wide = width // blocks
-    length = s * t
-    plan = plan_steps(n, pairs, blocks)
-    rows = width >> steps
-    shapes = [(rows, width)] * 4 + [g_w1.shape[steps:], g_w2.shape[steps:]]
-    unit_list = make_units(shapes, SUM_PAIRS)
-    n_waves = len(unit_list) + steps
-    w_end = span(plan, "weights")[1]
-    last = len(plan) - 1
-    early = len(unit_list) - 2
-    wave_steps = []
-    for wave in range(n_waves):
-        if wave < early:
-            wave_steps.append(min(WAVE_STEPS[wave], w_end - 1) if wave < len(WAVE_STEPS) else w_end - 1)
-        else:
-            wave_steps.append(max(w_end, min(last, w_end + (wave - early))))
-    sizes = [vec.shape[steps:]] + [(r.size, c.size) for unit in unit_list for _, r, c, _ in unit]
-    sizes.append((2 * width // 128, 128))
-    types = [F32] + [BF] * (len(sizes) - 2) + [F32]
-
-    turn = pairs + blocks
+    devices = 1 << steps
+    hidden, blocks = 8, 4
+    h, wide, length, rows = W1.shape[1] // hidden, width // blocks, s * t, s * n * t
+    plan = plan_steps(n, hidden, s, blocks)
+    own_rows = width // devices
+    shapes = [(own_rows, width)] * 4 + [(own_rows, W1.shape[1]), (W2.shape[0] // devices, width)]
+    unit_list = sum_units(shapes, blocks)
+    first, late = span(plan, "attend" if n > 1 else "last")[0], len(unit_list) - blocks
+    ready = [2 * k + 2 for k in range(4)] + [hidden] * 4 + [first]
+    ready += list(range(*span(plan, "last")))
+    megabytes = [[(r.size * c.size * devices * 2 / MIB, color) for _, r, c, color in u] for u in unit_list]
+    events = plan_events(plan, megabytes, ready, late, a, b)
+    sizes = [(r.size, c.size) for unit in unit_list for _, r, c, _ in unit] + [(8, 128)]
+    types = [BF] * (len(sizes) - 1) + [F32]
+    loaded = [at > 2 for unit in unit_list for at, _, _, _ in unit] + [False]
+    turn, last = 2 * blocks, n - 1
+
+    def count_from(i, starts):
+        return sum([(i >= start).astype(jnp.int32) for start in starts], jnp.int32(0))
+
+    def at_kind(i, begin):
+        off = i - begin
+        seq = count_from(off, [k * turn for k in range(1, n)])
+        return seq, jnp.clip(off - seq * turn, 0, blocks - 1)
 
     def at_head(i):
-        seq = jnp.minimum(i // turn, n - 1)
-        return seq, jnp.minimum(i - seq * turn, pairs - 1)
+        return at_kind(i, first)
 
     def at_tokens(i):
-        ends = i >= (n - 1) * turn + pairs + blocks
-        seq = jnp.where(ends, n - 1, jnp.clip((i - pairs) // turn, 0, max(n - 2, 0)))
-        start = pairs + seq * turn + jnp.where(seq == n - 1, blocks, 0)
-        return seq, jnp.clip(i - start, 0, blocks - 1)
+        return at_kind(i, first + blocks)
 
     def head_map(i):
         seq, pair = at_head(i)
@@ -579,29 +768,36 @@
         seq, pair = at_head(i)
         return (seq, pair, 0, 0)
 
-    def token_map(i):
-        seq, block = at_tokens(i)
-        return (0, seq, 0, block)
-
-    def weight_map(i):
-        return (at_tokens(i)[1], 0)
-
-    head = pl.BlockSpec((s, 1, t, 2 * HD), head_map)
-    weight = pl.BlockSpec((wide, width), weight_map)
+    def block_of(kind):
+        lo, hi = span(plan, kind)
+        return lambda i: jnp.clip(i - lo, 0, hi - lo - 1)
+
+    j_of, z_of, r_of = block_of("hidden"), block_of("norm"), block_of("project")
+    head = pl.BlockSpec((s, 1, t, wide), head_map)
+    weight = pl.BlockSpec((wide, width), lambda i: (at_tokens(i)[1], 0))
     anyspace = pl.BlockSpec(memory_space=pl.ANY)
+    vmem = pl.BlockSpec(memory_space=pltpu.VMEM)
     in_specs = [pl.BlockSpec((1, 1, length), lambda i: (at_head(i)[0], 0, 0))] + [head] * 4
-    in_specs += [pl.BlockSpec((1, 1, 8, length), lse_map), head]
+    in_specs += [pl.BlockSpec((1, wide // (2 * HD), 8, length), lse_map)]
+    in_specs += [pl.BlockSpec((rows, h), lambda i: (0, j_of(i)))] * 2
+    in_specs += [pl.BlockSpec((h, width), lambda i: (j_of(i), 0)), pl.BlockSpec((width, h), lambda i: (0, j_of(i)))]
+    in_specs += [pl.BlockSpec((1, n, t, width), lambda i: (z_of(i), 0, 0, 0))]
+    in_specs += [pl.BlockSpec((1, n, t, 1), lambda i: (z_of(i), 0, 0, 0))]
+    in_specs += [pl.BlockSpec((1, width), lambda i: (0, 0))]
+    in_specs += [pl.BlockSpec((s, n, t, wide), lambda i: (0, 0, 0, r_of(i)))]
+    in_specs += [pl.BlockSpec((wide, width), lambda i: (r_of(i), 0))]
     in_specs += [pl.BlockSpec(x.shape, lambda i: (0, 0, 0, 0), pipeline_mode=pl.Buffered(1))]
-    in_specs += [pl.BlockSpec((s, 1, t, wide), token_map)] + [weight] * 3
-    in_specs += [anyspace] * 4
+    in_specs += [weight] * 3 + [pl.BlockSpec(vec.shape, lambda i: (0, 0))] + [anyspace] * 3
     outs = [jax.ShapeDtypeStruct((s, n, t, width), BF)]
-    outs += [jax.ShapeDtypeStruct(sizes[0], F32), jax.ShapeDtypeStruct(sizes[-1], F32)]
+    outs += [jax.ShapeDtypeStruct(sizes[-1], F32)]
     outs += [jax.ShapeDtypeStruct(shape, F32) for shape in shapes]
-    vmem = pl.BlockSpec(memory_space=pltpu.VMEM)
+    outs += [jax.ShapeDtypeStruct(lead + shapes[m], BF) for m in (3, 4, 5)]
     n_chunks = len(sizes)
     scratch = [pltpu.VMEM((n, length, width), BF)] * 3
-    scratch += [pltpu.VMEM(lead + (rows, width), BF)] * 3
+    scratch += [pltpu.VMEM(lead + (own_rows, width), BF)] * 3
     scratch += [pltpu.VMEM(lead + sizes[-1], F32), pltpu.VMEM((n, s, t, width), BF)]
+    scratch += [pltpu.VMEM((s, n, t, width), F32), pltpu.VMEM((8, W1.shape[1]), F32)]
+    scratch += [pltpu.VMEM((2,) + (2,) * (steps - bits_of(hidden)) + shapes[5], BF)]
     scratch += [
         pltpu.SemaphoreType.DMA((n_chunks, steps)),
         pltpu.SemaphoreType.DMA((n_chunks, steps)),
@@ -609,29 +805,65 @@
         pltpu.SemaphoreType.DMA((n, s - 1)),
         pltpu.SemaphoreType.DMA((n, s - 1)),
         pltpu.SemaphoreType.DMA((n,)),
+        pltpu.SemaphoreType.DMA((8,)),
     ]
-    for size, kind in zip(sizes, types):
-        scratch += [pltpu.VMEM((2,) * (steps - 1 - j) + size, kind) for j in range(steps)]
-    ids, at = [], 1
+    ids, at = [], 0
     for unit in unit_list:
         ids.append(list(range(at, at + len(unit))))
         at += len(unit)
-    ids[0] = [0] + ids[0]
     ids[-1] = ids[-1] + [at]
-    slot, keys = staging_plan(sizes, types, ids)
-    scratch += [pltpu.VMEM((2,) * (steps - 1) + size, kind) for size, kind, _ in keys]
+    slot, keys = staging_plan(sizes, types, ids, loaded)
+    lands, held = [None] * len(sizes), []
+    for u, unit in enumerate(ids):
+        used = {}
+        for m in unit:
+            if u >= late and m < len(sizes) - 1:
+                color = [chunk for each in unit_list for chunk in each][m][3]
+                lands[m] = (lands[ids[u - late][color]][0], used.get(color, 0), sizes[m][1])
+                used[color] = used.get(color, 0) + sizes[m][1]
+            else:
+                lands[m] = (len(held), 0, sizes[m][1])
+                held.append((sizes[m], types[m]))
+    for size, kind in held:
+        scratch += [pltpu.VMEM((2,) * (steps - 1 - j) + size, kind) for j in range(steps)]
+    scratch += [pltpu.VMEM((2,) * (steps - 1) + (r, c), kind) for r, c, kind in keys]
+    grad_outer, normed_low, grad_second = grads
     return pl.pallas_call(
-        functools.partial(back_kernel, a, b, plan, unit_list, wave_steps, slot, 1.0 / math.sqrt(HD)),
+        functools.partial(back_kernel, a, b, plan, unit_list, events, slot, lands, 1.0 / math.sqrt(HD)),
         grid=(len(plan),),
         out_shape=outs,
         in_specs=in_specs,
-        out_specs=[anyspace] + [vmem] * (len(outs) - 1),
+        out_specs=[anyspace] + [vmem] * 7 + [anyspace] * 3,
         scratch_shapes=scratch,
         compiler_params=pltpu.CompilerParams(
-            collective_id=1, has_side_effects=True, vmem_limit_bytes=60 * MIB
+            collective_id=1, has_side_effects=True, vmem_limit_bytes=63 * MIB + MIB * 5 // 8
         ),
         name="back_and_sum",
-    )(bias, q, k, v, ctx, lse, grad_ctx, x, grad_first, wq, wk, wv, vec, g_wo, g_w1, g_w2)
+    )(
+        bias,
+        q,
+        k,
+        v,
+        ctx,
+        lse,
+        active,
+        slope,
+        W2,
+        W1,
+        xhat,
+        scale,
+        gain,
+        ctx,
+        WO,
+        x,
+        WQ,
+        WK,
+        WV,
+        vec,
+        grad_outer,
+        normed_low,
+        grad_second,
+    )
 
 
 def norm_forward(hidden, gain, shift):
@@ -717,61 +949,52 @@
     grad_final = (2.0 * total_tokens / counted) * mask_rows * error
     grad_second = norm_backward(grad_final, G2, xhat2, scale2)
     grad_outer = grad_second.astype(BF)
-    g_w2 = dot_tn(active_low, grad_outer).astype(BF)
-    grad_inner = (dot_nt(grad_outer, W2) * slope.astype(F32)).astype(BF)
-    g_w1 = dot_tn(normed_low, grad_inner).astype(BF)
-    grad_normed = dot_nt(grad_inner, W1) + grad_second
-    grad_first = norm_backward(grad_normed, G1, xhat1, scale1)
-    grad_attended = grad_first.astype(BF)
-    g_wo = dot_tn(ctx_rows, grad_attended).astype(BF)
-    grad_ctx = dot_nt(grad_attended, WO).astype(BF)
 
     def column_sum(value):
         return jnp.sum(value.astype(F32), axis=0)
 
-    vector_grads = (
-        column_sum(grad_attended),
-        jnp.sum(grad_normed * xhat1, axis=0),
-        column_sum(grad_normed),
-        column_sum(grad_outer),
-        jnp.sum(grad_final * xhat2, axis=0),
-        column_sum(grad_final),
-        column_sum(grad_inner),
-    )
+    vector_grads = (column_sum(grad_outer), jnp.sum(grad_final * xhat2, axis=0), column_sum(grad_final))
     parts = [g.reshape(devices, -1) for g in vector_grads]
     parts.append(jnp.broadcast_to(local_loss, (devices, 1)))
     packed = jnp.concatenate(parts, axis=1)
-    packed = jnp.pad(packed, ((0, 0), (0, 8 * 128 - packed.shape[1])))
-    lead = (2,) * (a + b)
+    packed = jnp.pad(packed, ((0, 0), (0, 128 - packed.shape[1])))
+    by_rows = (n, length, width)
     summed = back(
         a,
         b,
         bias,
-        *(p.reshape(shard_shape) for p in (q, k, v)),
-        ctx,
+        [p.reshape(shard_shape) for p in (q, k, v)] + [ctx],
         lse,
-        grad_ctx.reshape(shard_shape),
+        active_low,
+        slope,
+        W2,
+        W1,
+        xhat1.astype(BF).reshape(shard_shape),
+        scale1.reshape(sp, n, part, 1),
+        G1.reshape(1, width),
+        WO,
         moved,
-        grad_first.reshape(shard_shape),
         WQ,
         WK,
         WV,
-        packed.reshape(lead + (8, 128)),
-        *(g.reshape(lead + w.shape) for g, w in ((g_wo, wo), (g_w1, w1), (g_w2, w2))),
+        [grad_outer.reshape(by_rows), normed_low.reshape(by_rows), grad_second.reshape(shard_shape)],
+        packed,
     )
     home = summed[0].reshape(seqs, part, width).astype(F32)
-    own = summed[1].reshape(-1)
+    own = summed[1][6]
     small, at = [], 0
     for g in vector_grads:
         size = g.shape[0] // devices
         small.append(own[at : at + size])
         at += size
     loss = own[at] / (width * counted)
-    d_bo, d_g1, d_s1, d_b2, d_g2, d_s2, d_b1 = small
-    whole_sums = summed[2].reshape(2, width)
-    mine_at = (lax.axis_index("fsdp") * sp + z) * (width // devices)
-    d_bq, d_bv = (lax.dynamic_slice_in_dim(w, mine_at, width // devices, 0) for w in whole_sums)
-    d_wq, d_wk, d_wv, d_wo, d_w1, d_w2 = summed[3:]
+    d_b2, d_g2, d_s2 = small
+    me = lax.axis_index("fsdp") * sp + z
+    tiles = []
+    for at, size in enumerate((sizes[8],) + (width // devices,) * 5):
+        tiles.append(lax.dynamic_slice_in_dim(summed[1][at], lax.rem(me * size, 128), size, 0))
+    d_b1, d_g1, d_s1, d_bo, d_bq, d_bv = tiles
+    d_wq, d_wk, d_wv, d_wo, d_w1, d_w2 = summed[2:8]
     return (
         output.reshape(seqs, part, width),
         loss,

time: 491 us -> 460 us (0.937); the launches traced: 483 us -> 458 us
  matrix products: 120 us -> 42.8 us
  Pallas kernels: 301 us -> 347 us
    dot_general x6 -> x0, matrix products: 75.3 us -> none  [the longest x3 39 us: dot_nt(): lax.dot_general(x, y, (((1,), (1,)), ((), ())), preferred_element_type=F32)]
    pallas_call x1, Pallas kernels: 151 us -> 198 us  [back(): pl.pallas_call(functools.partial(back_kernel, a, b, plan, unit_list, even...]
    reduce_sum x3 -> x1, other arithmetic: 10.7 us -> 4.59 us  [column_sum(): return jnp.sum(value.astype(F32), axis=0)]
    reduce_sum x0 -> x1, other arithmetic: none -> 5.92 us  [norm_backward(): lead = jnp.mean(scaled, axis=-1, keepdims=True)]
    unnamed x64 -> x56, local copies, waits for them, and re-layouts: 12.3 us -> 11.5 us
  transfers between devices with their start and end apart: 2 -> 2, of which waited for: 0 -> 0; matrix products, arithmetic and copies ran while one was open for 17% -> 14% of each run, Pallas kernels for 35% -> 47%
where the time goes in v2:
time: 460 us; the launch traced here: 458 us
  Pallas kernels  347 us (75%)
  matrix products  42.8 us (9%)
  local copies, waits for them, and re-layouts  29 us (6%)
  other arithmetic  23.2 us (5%)
  starting transfers between devices  8.8 us (2%)
  between operations  6.99 us (2%)
    pallas_call x1, Pallas kernels, back(): pl.pallas_call(functools.partial(back_kernel, a, b, plan, unit_list, even...  198 us
    pallas_call x1, Pallas kernels, front(): pl.pallas_call(functools.partial(front_kernel, a, b, units), out_shape=ou...  130 us
    dot_general x6, matrix products, dot_nn(): lax.dot_general(x, y, (((1,), (0,)), ((), ())), preferred_element_type=F32)  42.8 us
    pallas_call x1, Pallas kernels, attend(): pl.pallas_call(functools.partial(attend_kernel, 1.0 / math.sqrt(HD)), gri...  19.9 us
    unnamed x56, local copies, waits for them, and re-layouts  11.5 us
  transfers between devices with their start and end apart: 2, of which 0 were waited for; matrix products, arithmetic and copies ran while one was open for 14% of the time, Pallas kernels for 47%

profile of v2, /device:TPU:0, one launch (start us, length us, event | category | flops | bytes accessed | tf_op | source)
XLA Modules:
  0.0 457.7 jit_solution(18407148370555857265)
XLA Ops:
  0.7 1.4 dynamic-slice_reduce_fusion
  4.6 6.1 %concatenate.7 = bf16[386]{0:T(512)(128)(2,1)S(1)} concatenate(bf16[32]{0:T(256)(128)(2,1)} %param.22, bf16[32]{0:T(256)(128)(2,1)} %param.25, bf16[32]{0:T(256)(128)(2,1)} %param.27, bf16[32]{0:T(256)(128)(2,1)} %param.28, bf16[32]{0:T(256)(128)(2,1)} %param.29, bf16[32]{0:T(256)(128)(2,1)} %param.33, bf16[32]{0:T(256)(128)(2,1)} %param.34, bf16[32]{0:T(256)(128)(2,1)} %param.35, ...), dimensions={0} | concatenate | bytes 1544 | tf_op jit(solution)/shard_map/concatenate | solution.py:906
  10.8 0.6 pad_bitcast_fusion.refs_1_
  11.4 129.5 %gather_weights.1 = (bf16[4,2,128,1024]{3,2,1,0:T(8,128)(2,1)}, bf16[2,2,2,2,2,16,128]{6,5,4,3,2,1,0:T(8,128)(2,1)}, bf16[2,2,2,2,2,32,1024]{6,5,4,3,2,1,0:T(8,1...) custom-call(bf16[4,2,128,1024]{3,2,1,0:T(8,128)(2,1)} %bitcast.120, ...), custom_call_target="tpu_custom_call" | custom-call | tf_op jit(solution)/shard_map/gather_weights/pallas_call | solution.py:198
  140.9 3.8 all-to-all-start.1
  144.7 0.7 add_multiply_fusion.1
  145.5 0.7 convert_reduce_fusion.1
  146.1 0.1 slice_convert_fusion.1
  146.2 0.0 copy-start.5
  146.2 0.1 reshape.315
  146.3 0.1 reshape.316
  146.4 0.1 reshape.312
  146.5 0.1 reshape.311
  146.5 0.1 reshape.314
  146.6 0.1 reshape.310
  146.7 0.1 reshape.309
  146.8 0.1 reshape.308
  146.8 4.7 %convolution_convert_fusion = bf16[1024,1024]{1,0:T(8,128)(2,1)S(1)} fusion(bf16[1024,1024]{1,0:T(8,128)(2,1)} %bitcast.108, bf16[1024,1024]{1,0:T(8,128)(2,1)} %bitcast.114), kind=kOutput, calls=%fused_computation.30 | convolution fusion | flops 2148532224 | bytes 6291456 | tf_op jit(solution)/shard_map/dot_general | solution.py:230
  151.6 2.3 add_convert_fusion.1
  153.9 2.3 add_convert_fusion
  156.3 19.9 %attend.1 = (bf16[4,2,128,1024]{3,2,1,0:T(8,128)(2,1)S(1)}, f32[2,8,8,512]{3,2,1,0:T(8,128)S(1)}) custom-call(f32[2,1,512]{2,1,0:T(1,128)S(1)} %reshape.284.bias_ref.refs_0_, bf16[4,2,128,1024]{3,2,1,0:T(8,128)(2,1)S(1)} %bitcast.93, bf16[4,2,128,1024]{3,2,1,0:T(8,128)(2,1)S(1)} %bitcast.91, bf16[4,2,128,1024]{3,2,1,0:T(8,128)(2,1)S(1)} %bitcast.95), custom_call_target="tpu_custom_call" | custom-call | flops 2147483648 | bytes 16777216 | tf_op jit(solution)/shard_map/attend/pallas_call | solution.py:260
  176.2 0.0 copy-start.4
  176.2 2.5 fusion.14
  178.7 0.0 copy-start.8
  178.7 2.0 copy-done.8
  180.7 0.6 multiply_reduce_fusion.3
  182.7 0.0 slice-start
  182.7 4.5 multiply_convert_fusion.1
  187.1 19.2 %fusion.4 = (bf16[1024,4096]{1,0:T(8,128)(2,1)}, bf16[1024,4096]{1,0:T(8,128)(2,1)}) fusion(f32[4096]{0:T(1024)S(1)} %fusion.8, bf16[1024,1024]{1,0:T(8,128)(2,1)S(1)} %get-tuple-element.72, bf16[1024,4096]{1,0:T(8,128)(2,1)} %bitcast.98), kind=kOutput, calls=%fused_computation.5 | convolution fusion | flops 8640266240 | bytes 27279360 | tf_op jit(solution)/shard_map/dot_general | solution.py:230
  206.4 11.8 %fusion.15 = (f32[1024]{0:T(1024)S(1)}, f32[1024,1024]{1,0:T(8,128)S(1)}) fusion(f32[1024]{0:T(1024)S(1)} %reshape.314, bf16[1024,4096]{1,0:T(8,128)(2,1)} %get-tuple-element.69.refs_6_, bf16[4096,1024]{1,0:T(8,128)(2,1)S(1)} %bitcast.103, f32[1024]{0:T(1024)S(1)} %reshape.312, f32[1024]{0:T(1024)S(1)} %reshape.311, f32[1024]{0:T(1024)S(1)} %add_rsqrt_fusion.1, ...), kind=kOutput, calls=%fused_computation.71 | convolution fusion | flops 8597273600 | bytes 25190400 | tf_op jit(solution)/shard_map/dot_general | solution.py:230
  218.2 0.0 copy-start.6
  218.2 2.0 copy-done.6
  220.2 0.5 multiply_reduce_fusion.2
  220.8 0.0 all-to-all-done.1
  220.8 0.0 copy-start.7
  220.8 5.9 %multiply_reduce_fusion.4 = (f32[1024]{0:T(1024)S(1)}, f32[1024]{0:T(1024)S(1)}, f32[1024]{0:T(1024)S(1)}, f32[1024]{0:T(1024)S(1)}, f32[]{:T(128)}) fusion(f32[1024]{0:T(1024)S(1)} %broadcast_multiply_fusion, f32[1024]{0:T(1024)S(1)} %reshape.315, bf16[4,2,128,1024]{3,2,1,0:T(8,128)(2,1)S(1)} %all-to-all-done.1, f32[1024]{0:T(1024)S(1)} %reshape.316, ...), kind=kLoop, calls=%fused_computation.26 | loop fusion | flops 17821696 | bytes 6332420 | tf_op jit(solution)/shard_map/reduce_sum | solution.py:879
  226.7 4.6 %convert_reduce_fusion = (f32[1024]{0:T(1024)S(1)}, bf16[1024,1024]{1,0:T(8,128)(2,1)}, f32[1024,1024]{1,0:T(8,128)}, bf16[1024,1024]{1,0:T(8,128)(2,1)}) fusion(f32[1024]{0:T(1024)S(1)} %get-tuple-element.94, f32[1024]{0:T(1024)S(1)} %get-tuple-element.95, bf16[4,2,128,1024]{3,2,1,0:T(8,128)(2,1)S(1)} %all-to-all-done.1, f32[1024]{0:T(1024)S(1)} %reshape.316, ...), kind=kLoop, calls=%fused_computation.12 | loop fusion | flops 16776192 | bytes 14712832 | tf_op jit(solution)/shard_map/reduce_sum | solution.py:954
  231.3 5.1 %all-to-all-start = ((bf16[4,2,128,1024]{3,2,1,0:T(8,128)(2,1)}), bf16[4,2,128,1024]{3,2,1,0:T(8,128)(2,1)}, u32[]{:S(2)}, u32[]{:S(2)}) async-start(bf16[4,2,128,1024]{3,2,1,0:T(8,128)(2,1)} %bitcast.105), calls=%async_computation | async-start | bytes 4194304 | tf_op jit(solution)/shard_map/all_to_all | solution.py:947
  236.4 0.7 reshape.317.refs_12_
  237.0 1.0 copy.37.refs_11_
  238.1 0.1 reshape.304
  238.1 0.1 reshape.303
  238.2 0.1 reshape.302
  238.3 0.7 pad.13.clone
  239.0 0.1 maximum_maximum_fusion
  239.1 0.6 pad.9.refs_19_
  239.7 197.5 %back_and_sum.1 = (bf16[4,2,128,1024]{3,2,1,0:T(8,128)(2,1)}, f32[8,128]{1,0:T(8,128)}, f32[32,1024]{1,0:T(8,128)}, f32[32,1024]{1,0:T(8,128)}, f32[32,1024]{1,0...) custom-call(f32[2,1,512]{2,1,0:T(1,128)} %copy-done.5, ...), custom_call_target="tpu_custom_call" | custom-call | tf_op jit(solution)/shard_map/back_and_sum/pallas_call | solution.py:831
  437.3 1.3 slice.89
  439.2 1.4 slice_bitcast_fusion.4
  440.6 0.6 fusion.13
  441.2 0.6 fusion.12
  441.8 0.6 fusion.11
  442.3 0.6 fusion.10
  442.9 0.6 fusion.9
  443.5 1.4 slice_bitcast_fusion.1
  444.9 4.1 bitcast_convert_fusion
  449.0 0.0 all-to-all-done
  449.0 3.2 copy.48
  452.2 0.7 copy.49
  452.9 0.7 copy.50
  453.5 0.7 copy.51
  454.2 0.7 copy.52
  454.8 0.8 copy.53
  455.6 0.8 copy.54
  (50 shorter events, 0.2 us)
Async XLA Ops:
  140.9 4.5 copy-start.21
  140.9 79.9 %all-to-all-start.1 = ((bf16[4,2,128,1024]{3,2,1,0:T(8,128)(2,1)}), bf16[4,2,128,1024]{3,2,1,0:T(8,128)(2,1)S(1)}, u32[]{:S(2)}, u32[]{:S(2)}) async-start(bf16[4,2,128,1024]{3,2,1,0:T(8,128)(2,1)} %bitcast.121), calls=%async_computation.1 | async-start | bytes 4194304 | tf_op jit(solution)/shard_map/all_to_all | solution.py:922
  146.2 10.1 %copy-start.5 = (f32[2,1,512]{2,1,0:T(1,128)}, f32[2,1,512]{2,1,0:T(1,128)S(1)}, u32[]{:S(2)}) copy-start(f32[2,1,512]{2,1,0:T(1,128)S(1)} %reshape.284.bias_ref.refs_0_) | copy-start | bytes 12292
  146.8 4.7 %copy-start.11 = (bf16[4,2,128,1024]{3,2,1,0:T(8,128)(2,1)S(1)}, bf16[4,2,128,1024]{3,2,1,0:T(8,128)(2,1)}, u32[]{:S(2)}) copy-start(bf16[4,2,128,1024]{3,2,1,0:T(8,128)(2,1)} %get-tuple-element.37.refs_15_) | copy-start | bytes 6291460
  146.8 4.7 %copy-start.12 = (bf16[2,2,2,2,2,32,1024]{6,5,4,3,2,1,0:T(8,128)(2,1)S(1)}, bf16[2,2,2,2,2,32,1024]{6,5,4,3,2,1,0:T(8,128)(2,1)}, u32[]{:S(2)}) copy-start(bf16[2,2,2,2,2,32,1024]{6,5,4,3,2,1,0:T(8,128)(2,1)} %get-tuple-element.38) | copy-start | bytes 6291460
  151.5 4.8 %copy-start.1 = (bf16[1024,1024]{1,0:T(8,128)(2,1)}, bf16[1024,1024]{1,0:T(8,128)(2,1)S(1)}, u32[]{:S(2)}) copy-start(bf16[1024,1024]{1,0:T(8,128)(2,1)S(1)} %convolution_convert_fusion) | copy-start | bytes 6291460
  151.6 2.4 copy-start.13
  153.9 2.4 copy-start.2
  156.3 22.4 %copy-start.3 = (bf16[1024,1024]{1,0:T(8,128)(2,1)}, bf16[1024,1024]{1,0:T(8,128)(2,1)S(1)}, u32[]{:S(2)}) copy-start(bf16[1024,1024]{1,0:T(8,128)(2,1)S(1)} %add_convert_fusion) | copy-start | bytes 6291460
  156.3 19.9 %copy-start.14 = (bf16[2,2,2,2,2,32,1024]{6,5,4,3,2,1,0:T(8,128)(2,1)S(1)}, bf16[2,2,2,2,2,32,1024]{6,5,4,3,2,1,0:T(8,128)(2,1)}, u32[]{:S(2)}) copy-start(bf16[2,2,2,2,2,32,1024]{6,5,4,3,2,1,0:T(8,128)(2,1)} %get-tuple-element.43) | copy-start | bytes 6291460
  176.2 2.5 copy-start
  176.2 2.5 copy-start.4
  178.7 2.0 copy-start.8
  182.7 23.7 %slice-start = ((s8[8388608]{0:T(1024)(128)(4,1)}), s8[4194304]{0:T(1024)(128)(4,1)S(1)}, s32[]{:S(2)}) async-start(s8[8388608]{0:T(1024)(128)(4,1)} %bitcast.101), calls=%async_computation.2 | async-start | bytes 8388608
  187.1 19.3 %copy-start.10 = (bf16[1024,1024]{1,0:T(8,128)(2,1)}, bf16[1024,1024]{1,0:T(8,128)(2,1)S(1)}, u32[]{:S(2)}) copy-start(bf16[1024,1024]{1,0:T(8,128)(2,1)S(1)} %get-tuple-element.72) | copy-start | bytes 6291460
  187.1 19.3 %copy-start.9 = (f32[1024,1024]{1,0:T(8,128)S(1)}, f32[1024,1024]{1,0:T(8,128)}, u32[]{:S(2)}) copy-start(f32[1024,1024]{1,0:T(8,128)} %copy-done.8) | copy-start | bytes 12582916
  187.1 19.3 %slice-start.1 = ((s8[8388608]{0:T(1024)(128)(4,1)}), s8[4194304]{0:T(1024)(128)(4,1)S(1)}, s32[]{:S(2)}) async-start(s8[8388608]{0:T(1024)(128)(4,1)} %bitcast.101), calls=%async_computation.3 | async-start | bytes 8388608
  218.2 2.0 copy-start.6
  220.8 5.9 %copy-start.7 = (f32[1024,1024]{1,0:T(8,128)S(1)}, f32[1024,1024]{1,0:T(8,128)}, u32[]{:S(2)}) copy-start(f32[1024,1024]{1,0:T(8,128)} %copy-done.6) | copy-start | bytes 12582916
  231.3 217.7 %all-to-all-start = ((bf16[4,2,128,1024]{3,2,1,0:T(8,128)(2,1)}), bf16[4,2,128,1024]{3,2,1,0:T(8,128)(2,1)}, u32[]{:S(2)}, u32[]{:S(2)}) async-start(bf16[4,2,128,1024]{3,2,1,0:T(8,128)(2,1)} %bitcast.105), calls=%async_computation | async-start | bytes 4194304 | tf_op jit(solution)/shard_map/all_to_all | solution.py:947
  444.9 7.3 %copy-start.20 = (f32[32,1024]{1,0:T(8,128)S(1)}, f32[32,1024]{1,0:T(8,128)}, u32[]{:S(2)}) copy-start(f32[32,1024]{1,0:T(8,128)} %get-tuple-element.117) | copy-start | bytes 393220
  444.9 8.0 %copy-start.19 = (f32[32,1024]{1,0:T(8,128)S(1)}, f32[32,1024]{1,0:T(8,128)}, u32[]{:S(2)}) copy-start(f32[32,1024]{1,0:T(8,128)} %get-tuple-element.119) | copy-start | bytes 393220
  444.9 8.6 %copy-start.18 = (f32[32,1024]{1,0:T(8,128)S(1)}, f32[32,1024]{1,0:T(8,128)}, u32[]{:S(2)}) copy-start(f32[32,1024]{1,0:T(8,128)} %get-tuple-element.120) | copy-start | bytes 393220
  444.9 9.3 %copy-start.17 = (f32[32,1024]{1,0:T(8,128)S(1)}, f32[32,1024]{1,0:T(8,128)}, u32[]{:S(2)}) copy-start(f32[32,1024]{1,0:T(8,128)} %get-tuple-element.122) | copy-start | bytes 393220
  449.0 5.8 %copy-start.16 = (f32[32,4096]{1,0:T(8,128)S(1)}, f32[32,4096]{1,0:T(8,128)}, u32[]{:S(2)}) copy-start(f32[32,4096]{1,0:T(8,128)} %get-tuple-element.126) | copy-start | bytes 1572868
  449.0 6.6 %copy-start.15 = (f32[128,1024]{1,0:T(8,128)S(1)}, f32[128,1024]{1,0:T(8,128)}, u32[]{:S(2)}) copy-start(f32[128,1024]{1,0:T(8,128)} %get-tuple-element.128) | copy-start | bytes 1572868

commit v3 on v2

--- a/solution.py
+++ b/solution.py
@@ -14,6 +14,7 @@
 MESH = pl.DeviceIdType.MESH
 AXES = ("fsdp", "sp")
 MIB = 1 << 20
+ATTEND_PAIRS = 4
 GATHER_PAIRS = ((0, 1, 1), (2, 3, 1), (4, 5, 4))
 
 
@@ -233,39 +234,40 @@
 def attend_kernel(temper, bias_ref, q_ref, k_ref, v_ref, ctx_ref, lse_ref):
     length = bias_ref.shape[-1]
     shape = q_ref.shape
-    q = q_ref[...].reshape(length, shape[-1])
-    k = k_ref[...].reshape(length, shape[-1])
-    v = v_ref[...].reshape(length, shape[-1])
     bias = bias_ref[...].reshape(1, length)
-    total = jnp.zeros((length, shape[-1]), F32)
-    logs = jnp.zeros((length, shape[-1]), F32)
-    for head in range(2):
-        mask = head_mask(head)
-        scores = dot_nt(q, k * (mask * temper).astype(BF)) + bias
-        largest = jnp.max(scores, axis=-1, keepdims=True)
-        raised = jnp.exp(scores - largest)
-        summed = jnp.sum(raised, axis=-1, keepdims=True)
-        part = dot_nn(raised.astype(BF), v * mask.astype(BF))
-        total = total + part * (1.0 / summed)
-        logs = logs + (largest + jnp.log(summed)) * mask
-    ctx_ref[...] = total.astype(BF).reshape(shape)
-    turned = jnp.transpose(logs)
-    for head in range(2):
-        lse_ref[0, 0, head : head + 1] = turned[head * HD : head * HD + 1]
+    for pair in range(shape[-1] // (2 * HD)):
+        cut = slice(pair * 2 * HD, (pair + 1) * 2 * HD)
+        q, k, v = (ref[:, 0, :, cut].reshape(length, 2 * HD) for ref in (q_ref, k_ref, v_ref))
+        total = jnp.zeros((length, 2 * HD), F32)
+        logs = jnp.zeros((length, 2 * HD), F32)
+        for head in range(2):
+            mask = head_mask(head)
+            scores = dot_nt(q, k * (mask * temper).astype(BF)) + bias
+            largest = jnp.max(scores, axis=-1, keepdims=True)
+            raised = jnp.exp(scores - largest)
+            summed = jnp.sum(raised, axis=-1, keepdims=True)
+            part = dot_nn(raised.astype(BF), v * mask.astype(BF))
+            total = total + part * (1.0 / summed)
+            logs = logs + (largest + jnp.log(summed)) * mask
+        ctx_ref[:, 0, :, cut] = total.astype(BF).reshape(shape[0], shape[2], 2 * HD)
+        turned = jnp.transpose(logs)
+        for head in range(2):
+            lse_ref[0, pair, head : head + 1] = turned[head * HD : head * HD + 1]
 
 
 def attend(bias, q, k, v):
     s, n, t, width = q.shape
-    rows = pl.BlockSpec((s, 1, t, 2 * HD), lambda i, j: (0, i, 0, j))
+    wide = ATTEND_PAIRS * 2 * HD
+    rows = pl.BlockSpec((s, 1, t, wide), lambda i, j: (0, i, 0, j))
     return pl.pallas_call(
         functools.partial(attend_kernel, 1.0 / math.sqrt(HD)),
-        grid=(n, width // (2 * HD)),
+        grid=(n, width // wide),
         out_shape=[
             jax.ShapeDtypeStruct(q.shape, BF),
             jax.ShapeDtypeStruct((n, width // (2 * HD), 8, s * t), F32),
         ],
         in_specs=[pl.BlockSpec((1, 1, s * t), lambda i, j: (i, 0, 0)), rows, rows, rows],
-        out_specs=[rows, pl.BlockSpec((1, 1, 8, s * t), lambda i, j: (i, j, 0, 0))],
+        out_specs=[rows, pl.BlockSpec((1, ATTEND_PAIRS, 8, s * t), lambda i, j: (i, j, 0, 0))],
         compiler_params=pltpu.CompilerParams(vmem_limit_bytes=32 * MIB),
         cost_estimate=pl.CostEstimate(
             flops=4 * n * (s * t) ** 2 * width, bytes_accessed=16 * s * n * t * width, transcendentals=0
@@ -903,21 +905,24 @@
     count = jnp.sum(mine)
     vectors = (bq, bv, bo, gain1, shift1, b2, gain2, shift2, b1)
     sizes = [v.shape[0] for v in vectors]
-    held = jnp.concatenate(list(vectors) + [jnp.stack([count // 32, count % 32]).astype(BF)])
-    vec = jnp.pad(held, (0, 16 * 128 - held.shape[0])).reshape(16, 128)
+    lines = [jnp.pad(v.reshape(1, -1), ((0, 0), (0, 128 - v.shape[0]))) for v in vectors]
+    lane = lax.broadcasted_iota(jnp.int32, (1, 128), 1)
+    lines.append(jnp.where(lane == 0, count // 32, count % 32).astype(BF))
+    row = lax.broadcasted_iota(jnp.int32, (16, 128), 0)
+    vec = jnp.zeros((16, 128), BF)
+    for at, line in enumerate(lines):
+        vec = jnp.where(row == at, line, vec)
 
     shards = (wq, wk, wv, wo, w1, w2)
     got = front(a, b, tokens.reshape(shard_shape), vec, shards)
-    moved, vec_all = got[0], got[1].reshape(devices, -1)
+    moved, vec_all = got[0], got[1].reshape(devices, 16, 128)
     WQ, WK, WV, WO, W1, W2 = (
         g.reshape((devices * w.shape[0],) + w.shape[1:]) for g, w in zip(got[2:], shards)
     )
-    full, at = [], 0
-    for size in sizes:
-        full.append(vec_all[:, at : at + size].reshape(-1).astype(F32))
-        at += size
+    full = [vec_all[:, at, :size].reshape(-1).astype(F32) for at, size in enumerate(sizes)]
     BQ, BV, BO, G1, S1, B2, G2, S2, B1 = full
-    counted = jnp.sum(vec_all[:, at].astype(F32)) * 32.0 + jnp.sum(vec_all[:, at + 1].astype(F32))
+    counts = vec_all[:, len(sizes), :2].astype(F32)
+    counted = jnp.sum(counts[:, 0]) * 32.0 + jnp.sum(counts[:, 1])
 
     teacher_moved = lax.all_to_all(
         lax.optimization_barrier((teacher, moved))[0].reshape(shard_shape), "sp", split_axis=0, concat_axis=0

time: 460 us -> 452 us (0.983)
  Pallas kernels: 347 us -> 342 us
    concatenate x1 -> x0, local copies, waits for them, and re-layouts: 6.11 us -> none  [body(): jnp.concatenate(list(vectors) + [jnp.stack([count // 32, count % 32]).ast...]
    pallas_call x1, Pallas kernels: 19.9 us -> 14.8 us  [attend(): pl.pallas_call(functools.partial(attend_kernel, 1.0 / math.sqrt(HD)), gri...]
where the time goes in v3:
time: 452 us; the launch traced here: 450 us
  Pallas kernels  342 us (76%)
  matrix products  42.4 us (9%)
  local copies, waits for them, and re-layouts  25.1 us (6%)
  other arithmetic  24.7 us (5%)
  starting transfers between devices  8.8 us (2%)
  between operations  7.07 us (2%)
    pallas_call x1, Pallas kernels, back(): pl.pallas_call(functools.partial(back_kernel, a, b, plan, unit_list, even...  198 us
    pallas_call x1, Pallas kernels, front(): pl.pallas_call(functools.partial(front_kernel, a, b, units), out_shape=ou...  130 us
    dot_general x6, matrix products, dot_nn(): lax.dot_general(x, y, (((1,), (0,)), ((), ())), preferred_element_type=F32)  42.4 us
    pallas_call x1, Pallas kernels, attend(): pl.pallas_call(functools.partial(attend_kernel, 1.0 / math.sqrt(HD)), gri...  14.8 us
    unnamed x56, local copies, waits for them, and re-layouts  11.6 us
  transfers between devices with their start and end apart: 2, of which 0 were waited for; matrix products, arithmetic and copies ran while one was open for 14% of the time, Pallas kernels for 47%

profile of v3, /device:TPU:0, one launch (start us, length us, event | category | flops | bytes accessed | tf_op | source)
XLA Modules:
  0.0 450.1 jit_solution(1154699062934559221)
XLA Ops:
  0.7 1.4 dynamic-slice_reduce_fusion
  4.7 0.7 pad_bitcast_fusion
  5.4 0.7 pad_bitcast_fusion.2
  6.1 0.7 pad_bitcast_fusion.4
  6.8 0.7 pad_bitcast_fusion.6
  7.4 1.3 select_select_fusion.refs_1_
  8.8 129.6 %gather_weights.1 = (bf16[4,2,128,1024]{3,2,1,0:T(8,128)(2,1)}, bf16[2,2,2,2,2,16,128]{6,5,4,3,2,1,0:T(8,128)(2,1)}, bf16[2,2,2,2,2,32,1024]{6,5,4,3,2,1,0:T(8,1...) custom-call(bf16[4,2,128,1024]{3,2,1,0:T(8,128)(2,1)} %bitcast.139, ...), custom_call_target="tpu_custom_call" | custom-call | tf_op jit(solution)/shard_map/gather_weights/pallas_call | solution.py:199
  138.4 3.8 all-to-all-start.1
  142.1 0.7 add_multiply_fusion.1
  142.9 0.3 fusion.9
  143.3 0.0 copy-start.5
  143.3 0.1 reshape.341
  143.4 0.1 copy.43
  143.5 0.6 slice_reduce_fusion
  144.1 0.1 reshape.345
  144.2 0.1 reshape.346
  144.2 0.1 reshape.342
  144.3 0.1 reshape.344
  144.4 0.1 reshape.340
  144.4 0.1 reshape.339
  144.5 0.1 reshape.338
  144.6 4.7 %convolution_convert_fusion = bf16[1024,1024]{1,0:T(8,128)(2,1)S(1)} fusion(bf16[1024,1024]{1,0:T(8,128)(2,1)} %bitcast.127, bf16[1024,1024]{1,0:T(8,128)(2,1)} %bitcast.133), kind=kOutput, calls=%fused_computation.30 | convolution fusion | flops 2148532224 | bytes 6291456 | tf_op jit(solution)/shard_map/dot_general | solution.py:231
  149.3 2.3 add_convert_fusion.1
  151.7 2.3 add_convert_fusion
  154.1 14.8 %attend.1 = (bf16[4,2,128,1024]{3,2,1,0:T(8,128)(2,1)S(1)}, f32[2,8,8,512]{3,2,1,0:T(8,128)S(1)}) custom-call(f32[2,1,512]{2,1,0:T(1,128)S(1)} %reshape.314.bias_ref.refs_0_, bf16[4,2,128,1024]{3,2,1,0:T(8,128)(2,1)S(1)} %bitcast.112, bf16[4,2,128,1024]{3,2,1,0:T(8,128)(2,1)S(1)} %bitcast.110, bf16[4,2,128,1024]{3,2,1,0:T(8,128)(2,1)S(1)} %bitcast.114), custom_call_target="tpu_custom_call" | custom-call | flops 2147483648 | bytes 16777216 | tf_op jit(solution)/shard_map/attend/pallas_call | solution.py:262
  169.0 2.5 fusion.21
  171.4 0.0 copy-start.8
  171.5 2.0 copy-done.8
  173.5 0.6 multiply_reduce_fusion.3
  175.4 4.5 multiply_convert_fusion.1
  179.8 18.9 %fusion.4 = (bf16[1024,4096]{1,0:T(8,128)(2,1)}, bf16[1024,4096]{1,0:T(8,128)(2,1)}) fusion(f32[4096]{0:T(1024)S(1)} %bitcast.148, bf16[1024,1024]{1,0:T(8,128)(2,1)S(1)} %get-tuple-element.79, bf16[1024,4096]{1,0:T(8,128)(2,1)} %bitcast.117), kind=kOutput, calls=%fused_computation.5 | convolution fusion | flops 8640266240 | bytes 27279360 | tf_op jit(solution)/shard_map/dot_general | solution.py:231
  198.8 11.7 %fusion.22 = (f32[1024]{0:T(1024)S(1)}, f32[1024,1024]{1,0:T(8,128)S(1)}) fusion(f32[1024]{0:T(1024)S(1)} %reshape.344, bf16[1024,4096]{1,0:T(8,128)(2,1)} %get-tuple-element.76.refs_6_, bf16[4096,1024]{1,0:T(8,128)(2,1)S(1)} %bitcast.122, f32[1024]{0:T(1024)S(1)} %reshape.342, f32[1024]{0:T(1024)S(1)} %reshape.341, f32[1024]{0:T(1024)S(1)} %add_rsqrt_fusion.1, ...), kind=kOutput, calls=%fused_computation.97 | convolution fusion | flops 8597273600 | bytes 25190400 | tf_op jit(solution)/shard_map/dot_general | solution.py:231
  210.5 0.0 copy-start.6
  210.5 2.0 copy-done.6
  212.5 0.5 multiply_reduce_fusion.2
  213.1 0.0 copy-start.7
  213.1 5.9 %multiply_reduce_fusion.4 = (f32[1024]{0:T(1024)S(1)}, f32[1024]{0:T(1024)S(1)}, f32[1024]{0:T(1024)S(1)}, f32[1024]{0:T(1024)S(1)}, f32[]{:T(128)}) fusion(f32[1024]{0:T(1024)S(1)} %broadcast_multiply_fusion, f32[1024]{0:T(1024)S(1)} %reshape.345, bf16[4,2,128,1024]{3,2,1,0:T(8,128)(2,1)S(1)} %all-to-all-done.1, f32[1024]{0:T(1024)S(1)} %reshape.346, ...), kind=kLoop, calls=%fused_computation.26 | loop fusion | flops 17821696 | bytes 6332420 | tf_op jit(solution)/shard_map/reduce_sum | solution.py:881
  219.0 4.6 %convert_reduce_fusion = (f32[1024]{0:T(1024)S(1)}, bf16[1024,1024]{1,0:T(8,128)(2,1)}, f32[1024,1024]{1,0:T(8,128)}, bf16[1024,1024]{1,0:T(8,128)(2,1)}) fusion(f32[1024]{0:T(1024)S(1)} %broadcast_multiply_fusion.1, f32[1024]{0:T(1024)S(1)} %broadcast_multiply_fusion.2, bf16[4,2,128,1024]{3,2,1,0:T(8,128)(2,1)S(1)} %all-to-all-done.1, ...), kind=kLoop, calls=%fused_computation.12 | loop fusion | flops 16776192 | bytes 14712832 | tf_op jit(solution)/shard_map/reduce_sum | solution.py:959
  223.6 5.1 %all-to-all-start = ((bf16[4,2,128,1024]{3,2,1,0:T(8,128)(2,1)}), bf16[4,2,128,1024]{3,2,1,0:T(8,128)(2,1)}, u32[]{:S(2)}, u32[]{:S(2)}) async-start(bf16[4,2,128,1024]{3,2,1,0:T(8,128)(2,1)} %bitcast.124), calls=%async_computation | async-start | bytes 4194304 | tf_op jit(solution)/shard_map/all_to_all | solution.py:952
  228.7 0.7 reshape.347.refs_12_
  229.4 1.0 copy.41.refs_11_
  230.4 0.1 reshape.334
  230.5 0.1 reshape.333
  230.5 0.1 reshape.332
  230.6 0.7 pad.41.clone
  231.3 0.1 maximum_maximum_fusion
  231.4 0.6 pad.37.refs_19_
  232.0 197.6 %back_and_sum.1 = (bf16[4,2,128,1024]{3,2,1,0:T(8,128)(2,1)}, f32[8,128]{1,0:T(8,128)}, f32[32,1024]{1,0:T(8,128)}, f32[32,1024]{1,0:T(8,128)}, f32[32,1024]{1,0...) custom-call(f32[2,1,512]{2,1,0:T(1,128)} %copy-done.5, ...), custom_call_target="tpu_custom_call" | custom-call | tf_op jit(solution)/shard_map/back_and_sum/pallas_call | solution.py:833
  429.7 1.3 slice.93
  431.6 1.4 slice_bitcast_fusion.3
  433.0 0.6 fusion.19
  433.6 0.6 fusion.18
  434.1 0.6 fusion.17
  434.7 0.6 fusion.16
  435.3 0.6 fusion.15
  435.9 1.4 slice_bitcast_fusion
  437.3 4.1 bitcast_convert_fusion
  441.4 3.2 copy.52
  444.6 0.7 copy.53
  445.2 0.7 copy.54
  445.9 0.7 copy.55
  446.6 0.7 copy.56
  447.2 0.8 copy.57
  448.0 0.8 copy.58
  (64 shorter events, 0.2 us)
Async XLA Ops:
  138.3 4.5 %copy-start.17 = (bf16[2,2,2,2,2,16,128]{6,5,4,3,2,1,0:T(8,128)(2,1)S(1)}, bf16[2,2,2,2,2,16,128]{6,5,4,3,2,1,0:T(8,128)(2,1)}, u32[]{:S(2)}) copy-start(bf16[2,2,2,2,2,16,128]{6,5,4,3,2,1,0:T(8,128)(2,1)} %get-tuple-element.39) | copy-start | bytes 393220
  138.4 74.8 %all-to-all-start.1 = ((bf16[4,2,128,1024]{3,2,1,0:T(8,128)(2,1)}), bf16[4,2,128,1024]{3,2,1,0:T(8,128)(2,1)S(1)}, u32[]{:S(2)}, u32[]{:S(2)}) async-start(bf16[4,2,128,1024]{3,2,1,0:T(8,128)(2,1)} %bitcast.140), calls=%async_computation.1 | async-start | bytes 4194304 | tf_op jit(solution)/shard_map/all_to_all | solution.py:927
  143.3 10.8 %copy-start.5 = (f32[2,1,512]{2,1,0:T(1,128)}, f32[2,1,512]{2,1,0:T(1,128)S(1)}, u32[]{:S(2)}) copy-start(f32[2,1,512]{2,1,0:T(1,128)S(1)} %reshape.314.bias_ref.refs_0_) | copy-start | bytes 12292
  144.6 4.7 %copy-start.11 = (bf16[4,2,128,1024]{3,2,1,0:T(8,128)(2,1)S(1)}, bf16[4,2,128,1024]{3,2,1,0:T(8,128)(2,1)}, u32[]{:S(2)}) copy-start(bf16[4,2,128,1024]{3,2,1,0:T(8,128)(2,1)} %get-tuple-element.37.refs_15_) | copy-start | bytes 6291460
  144.6 4.7 %copy-start.12 = (bf16[2,2,2,2,2,32,1024]{6,5,4,3,2,1,0:T(8,128)(2,1)S(1)}, bf16[2,2,2,2,2,32,1024]{6,5,4,3,2,1,0:T(8,128)(2,1)}, u32[]{:S(2)}) copy-start(bf16[2,2,2,2,2,32,1024]{6,5,4,3,2,1,0:T(8,128)(2,1)} %get-tuple-element.38) | copy-start | bytes 6291460
  149.3 4.8 %copy-start.1 = (bf16[1024,1024]{1,0:T(8,128)(2,1)}, bf16[1024,1024]{1,0:T(8,128)(2,1)S(1)}, u32[]{:S(2)}) copy-start(bf16[1024,1024]{1,0:T(8,128)(2,1)S(1)} %convolution_convert_fusion) | copy-start | bytes 6291460
  149.3 2.4 copy-start.13
  151.7 2.4 copy-start.2
  154.0 17.4 %copy-start.3 = (bf16[1024,1024]{1,0:T(8,128)(2,1)}, bf16[1024,1024]{1,0:T(8,128)(2,1)S(1)}, u32[]{:S(2)}) copy-start(bf16[1024,1024]{1,0:T(8,128)(2,1)S(1)} %add_convert_fusion) | copy-start | bytes 6291460
  154.0 14.9 %copy-start.14 = (bf16[2,2,2,2,2,32,1024]{6,5,4,3,2,1,0:T(8,128)(2,1)S(1)}, bf16[2,2,2,2,2,32,1024]{6,5,4,3,2,1,0:T(8,128)(2,1)}, u32[]{:S(2)}) copy-start(bf16[2,2,2,2,2,32,1024]{6,5,4,3,2,1,0:T(8,128)(2,1)} %get-tuple-element.43) | copy-start | bytes 6291460
  168.9 2.5 copy-start
  168.9 2.5 copy-start.4
  171.4 2.0 copy-start.8
  175.4 23.4 %slice-start = ((s8[8388608]{0:T(1024)(128)(4,1)}), s8[4194304]{0:T(1024)(128)(4,1)S(1)}, s32[]{:S(2)}) async-start(s8[8388608]{0:T(1024)(128)(4,1)} %bitcast.120), calls=%async_computation.2 | async-start | bytes 8388608
  179.8 18.9 %copy-start.10 = (bf16[1024,1024]{1,0:T(8,128)(2,1)}, bf16[1024,1024]{1,0:T(8,128)(2,1)S(1)}, u32[]{:S(2)}) copy-start(bf16[1024,1024]{1,0:T(8,128)(2,1)S(1)} %get-tuple-element.79) | copy-start | bytes 6291460
  179.8 18.9 %copy-start.9 = (f32[1024,1024]{1,0:T(8,128)S(1)}, f32[1024,1024]{1,0:T(8,128)}, u32[]{:S(2)}) copy-start(f32[1024,1024]{1,0:T(8,128)} %copy-done.8) | copy-start | bytes 12582916
  179.8 18.9 %slice-start.1 = ((s8[8388608]{0:T(1024)(128)(4,1)}), s8[4194304]{0:T(1024)(128)(4,1)S(1)}, s32[]{:S(2)}) async-start(s8[8388608]{0:T(1024)(128)(4,1)} %bitcast.120), calls=%async_computation.3 | async-start | bytes 8388608
  210.5 2.0 copy-start.6
  213.1 5.9 %copy-start.7 = (f32[1024,1024]{1,0:T(8,128)S(1)}, f32[1024,1024]{1,0:T(8,128)}, u32[]{:S(2)}) copy-start(f32[1024,1024]{1,0:T(8,128)} %copy-done.6) | copy-start | bytes 12582916
  223.6 217.8 %all-to-all-start = ((bf16[4,2,128,1024]{3,2,1,0:T(8,128)(2,1)}), bf16[4,2,128,1024]{3,2,1,0:T(8,128)(2,1)}, u32[]{:S(2)}, u32[]{:S(2)}) async-start(bf16[4,2,128,1024]{3,2,1,0:T(8,128)(2,1)} %bitcast.124), calls=%async_computation | async-start | bytes 4194304 | tf_op jit(solution)/shard_map/all_to_all | solution.py:952
  437.3 7.3 %copy-start.21 = (f32[32,1024]{1,0:T(8,128)S(1)}, f32[32,1024]{1,0:T(8,128)}, u32[]{:S(2)}) copy-start(f32[32,1024]{1,0:T(8,128)} %get-tuple-element.132) | copy-start | bytes 393220
  437.3 8.0 %copy-start.20 = (f32[32,1024]{1,0:T(8,128)S(1)}, f32[32,1024]{1,0:T(8,128)}, u32[]{:S(2)}) copy-start(f32[32,1024]{1,0:T(8,128)} %get-tuple-element.134) | copy-start | bytes 393220
  437.3 8.6 %copy-start.19 = (f32[32,1024]{1,0:T(8,128)S(1)}, f32[32,1024]{1,0:T(8,128)}, u32[]{:S(2)}) copy-start(f32[32,1024]{1,0:T(8,128)} %get-tuple-element.135) | copy-start | bytes 393220
  437.3 9.3 %copy-start.18 = (f32[32,1024]{1,0:T(8,128)S(1)}, f32[32,1024]{1,0:T(8,128)}, u32[]{:S(2)}) copy-start(f32[32,1024]{1,0:T(8,128)} %get-tuple-element.137) | copy-start | bytes 393220
  441.4 5.8 %copy-start.16 = (f32[32,4096]{1,0:T(8,128)S(1)}, f32[32,4096]{1,0:T(8,128)}, u32[]{:S(2)}) copy-start(f32[32,4096]{1,0:T(8,128)} %get-tuple-element.141) | copy-start | bytes 1572868
  441.4 6.6 %copy-start.15 = (f32[128,1024]{1,0:T(8,128)S(1)}, f32[128,1024]{1,0:T(8,128)}, u32[]{:S(2)}) copy-start(f32[128,1024]{1,0:T(8,128)} %get-tuple-element.143) | copy-start | bytes 1572868

commit v4 on v3

--- a/solution.py
+++ b/solution.py
@@ -14,7 +14,7 @@
 MESH = pl.DeviceIdType.MESH
 AXES = ("fsdp", "sp")
 MIB = 1 << 20
-ATTEND_PAIRS = 4
+ATTEND_PAIRS = 8
 GATHER_PAIRS = ((0, 1, 1), (2, 3, 1), (4, 5, 4))
 
 

time: 452 us -> 443 us (0.980); the launches traced: 450 us -> 436 us
  Pallas kernels: 342 us -> 328 us
    pallas_call x1, Pallas kernels: 198 us -> 184 us  [back(): pl.pallas_call(functools.partial(back_kernel, a, b, plan, unit_list, even...]
  transfers between devices with their start and end apart: 2 -> 2, of which waited for: 0 -> 0; matrix products, arithmetic and copies ran while one was open for 14% -> 15% of each run, Pallas kernels for 47% -> 45%
where the time goes in v4:
time: 443 us; the launch traced here: 436 us
  Pallas kernels  328 us (74%)
  matrix products  43 us (10%)
  local copies, waits for them, and re-layouts  25.1 us (6%)
  other arithmetic  24.7 us (6%)
  starting transfers between devices  8.8 us (2%)
  between operations  7.07 us (2%)
    pallas_call x1, Pallas kernels, back(): pl.pallas_call(functools.partial(back_kernel, a, b, plan, unit_list, even...  184 us
    pallas_call x1, Pallas kernels, front(): pl.pallas_call(functools.partial(front_kernel, a, b, units), out_shape=ou...  130 us
    dot_general x6, matrix products, dot_nn(): lax.dot_general(x, y, (((1,), (0,)), ((), ())), preferred_element_type=F32)  43 us
    pallas_call x1, Pallas kernels, attend(): pl.pallas_call(functools.partial(attend_kernel, 1.0 / math.sqrt(HD)), gri...  14.1 us
    unnamed x56, local copies, waits for them, and re-layouts  11.6 us
  transfers between devices with their start and end apart: 2, of which 0 were waited for; matrix products, arithmetic and copies ran while one was open for 15% of the time, Pallas kernels for 45%

profile of v4, /device:TPU:0, one launch (start us, length us, event | category | flops | bytes accessed | tf_op | source)
XLA Modules:
  0.0 436.3 jit_solution(1976319374719484047)
XLA Ops:
  0.7 1.4 dynamic-slice_reduce_fusion
  4.7 0.7 pad_bitcast_fusion
  5.4 0.7 pad_bitcast_fusion.2
  6.1 0.7 pad_bitcast_fusion.4
  6.8 0.7 pad_bitcast_fusion.6
  7.4 1.3 select_select_fusion.refs_1_
  8.8 129.6 %gather_weights.1 = (bf16[4,2,128,1024]{3,2,1,0:T(8,128)(2,1)}, bf16[2,2,2,2,2,16,128]{6,5,4,3,2,1,0:T(8,128)(2,1)}, bf16[2,2,2,2,2,32,1024]{6,5,4,3,2,1,0:T(8,1...) custom-call(bf16[4,2,128,1024]{3,2,1,0:T(8,128)(2,1)} %bitcast.139, ...), custom_call_target="tpu_custom_call" | custom-call | tf_op jit(solution)/shard_map/gather_weights/pallas_call | solution.py:199
  138.4 3.8 all-to-all-start.1
  142.1 0.7 add_multiply_fusion.1
  142.9 0.3 fusion.9
  143.3 0.0 copy-start.5
  143.3 0.1 reshape.341
  143.4 0.1 copy.43
  143.5 0.6 slice_reduce_fusion
  144.1 0.1 reshape.345
  144.2 0.1 reshape.346
  144.2 0.1 reshape.342
  144.3 0.1 reshape.344
  144.4 0.1 reshape.340
  144.4 0.1 reshape.339
  144.5 0.1 reshape.338
  144.6 4.7 %convolution_convert_fusion = bf16[1024,1024]{1,0:T(8,128)(2,1)S(1)} fusion(bf16[1024,1024]{1,0:T(8,128)(2,1)} %bitcast.127, bf16[1024,1024]{1,0:T(8,128)(2,1)} %bitcast.133), kind=kOutput, calls=%fused_computation.30 | convolution fusion | flops 2148532224 | bytes 6291456 | tf_op jit(solution)/shard_map/dot_general | solution.py:231
  149.3 2.3 add_convert_fusion.1
  151.7 2.3 add_convert_fusion
  154.1 14.1 %attend.1 = (bf16[4,2,128,1024]{3,2,1,0:T(8,128)(2,1)S(1)}, f32[2,8,8,512]{3,2,1,0:T(8,128)S(1)}) custom-call(f32[2,1,512]{2,1,0:T(1,128)S(1)} %reshape.314.bias_ref.refs_0_, bf16[4,2,128,1024]{3,2,1,0:T(8,128)(2,1)S(1)} %bitcast.112, bf16[4,2,128,1024]{3,2,1,0:T(8,128)(2,1)S(1)} %bitcast.110, bf16[4,2,128,1024]{3,2,1,0:T(8,128)(2,1)S(1)} %bitcast.114), custom_call_target="tpu_custom_call" | custom-call | flops 2147483648 | bytes 16777216 | tf_op jit(solution)/shard_map/attend/pallas_call | solution.py:262
  168.2 0.0 copy-start.4
  168.3 2.5 fusion.21
  170.8 0.0 copy-start.8
  170.8 2.0 copy-done.8
  172.8 0.6 multiply_reduce_fusion.3
  174.7 4.5 %multiply_convert_fusion.1 = (bf16[1024,1024]{1,0:T(8,128)(2,1)}, bf16[1024,1024]{1,0:T(8,128)(2,1)S(1)}) fusion(f32[1024,1024]{1,0:T(8,128)} %copy-done.8, f32[1024]{0:T(1024)S(1)} %add_rsqrt_fusion.1, f32[1024]{0:T(1024)S(1)} %broadcast_multiply_fusion.4, f32[1024]{0:T(1024)S(1)} %reshape.342, f32[1024]{0:T(1024)S(1)} %reshape.341), kind=kLoop, calls=%fused_computation.24 | loop fusion | flops 6291456 | bytes 8404992 | tf_op jit(solution)/shard_map/convert_element_type | solution.py:977
  179.2 19.4 %fusion.4 = (bf16[1024,4096]{1,0:T(8,128)(2,1)}, bf16[1024,4096]{1,0:T(8,128)(2,1)}) fusion(f32[4096]{0:T(1024)S(1)} %bitcast.148, bf16[1024,1024]{1,0:T(8,128)(2,1)S(1)} %get-tuple-element.79, bf16[1024,4096]{1,0:T(8,128)(2,1)} %bitcast.117), kind=kOutput, calls=%fused_computation.5 | convolution fusion | flops 8640266240 | bytes 27279360 | tf_op jit(solution)/shard_map/dot_general | solution.py:231
  198.6 11.7 %fusion.22 = (f32[1024]{0:T(1024)S(1)}, f32[1024,1024]{1,0:T(8,128)S(1)}) fusion(f32[1024]{0:T(1024)S(1)} %reshape.344, bf16[1024,4096]{1,0:T(8,128)(2,1)} %get-tuple-element.76.refs_6_, bf16[4096,1024]{1,0:T(8,128)(2,1)S(1)} %bitcast.122, f32[1024]{0:T(1024)S(1)} %reshape.342, f32[1024]{0:T(1024)S(1)} %reshape.341, f32[1024]{0:T(1024)S(1)} %add_rsqrt_fusion.1, ...), kind=kOutput, calls=%fused_computation.97 | convolution fusion | flops 8597273600 | bytes 25190400 | tf_op jit(solution)/shard_map/dot_general | solution.py:231
  210.4 0.0 copy-start.6
  210.4 2.0 copy-done.6
  212.4 0.5 multiply_reduce_fusion.2
  213.0 5.9 %multiply_reduce_fusion.4 = (f32[1024]{0:T(1024)S(1)}, f32[1024]{0:T(1024)S(1)}, f32[1024]{0:T(1024)S(1)}, f32[1024]{0:T(1024)S(1)}, f32[]{:T(128)}) fusion(f32[1024]{0:T(1024)S(1)} %broadcast_multiply_fusion, f32[1024]{0:T(1024)S(1)} %reshape.345, bf16[4,2,128,1024]{3,2,1,0:T(8,128)(2,1)S(1)} %all-to-all-done.1, f32[1024]{0:T(1024)S(1)} %reshape.346, ...), kind=kLoop, calls=%fused_computation.26 | loop fusion | flops 17821696 | bytes 6332420 | tf_op jit(solution)/shard_map/reduce_sum | solution.py:881
  218.9 4.6 %convert_reduce_fusion = (f32[1024]{0:T(1024)S(1)}, bf16[1024,1024]{1,0:T(8,128)(2,1)}, f32[1024,1024]{1,0:T(8,128)}, bf16[1024,1024]{1,0:T(8,128)(2,1)}) fusion(f32[1024]{0:T(1024)S(1)} %broadcast_multiply_fusion.1, f32[1024]{0:T(1024)S(1)} %broadcast_multiply_fusion.2, bf16[4,2,128,1024]{3,2,1,0:T(8,128)(2,1)S(1)} %all-to-all-done.1, ...), kind=kLoop, calls=%fused_computation.12 | loop fusion | flops 16776192 | bytes 14712832 | tf_op jit(solution)/shard_map/reduce_sum | solution.py:959
  223.5 5.1 %all-to-all-start = ((bf16[4,2,128,1024]{3,2,1,0:T(8,128)(2,1)}), bf16[4,2,128,1024]{3,2,1,0:T(8,128)(2,1)}, u32[]{:S(2)}, u32[]{:S(2)}) async-start(bf16[4,2,128,1024]{3,2,1,0:T(8,128)(2,1)} %bitcast.124), calls=%async_computation | async-start | bytes 4194304 | tf_op jit(solution)/shard_map/all_to_all | solution.py:952
  228.6 0.7 reshape.347.refs_12_
  229.2 1.0 copy.41.refs_11_
  230.3 0.1 reshape.334
  230.3 0.1 reshape.333
  230.4 0.1 reshape.332
  230.5 0.7 pad.41.clone
  231.2 0.1 maximum_maximum_fusion
  231.3 0.6 pad.37.refs_19_
  231.9 184.0 %back_and_sum.1 = (bf16[4,2,128,1024]{3,2,1,0:T(8,128)(2,1)}, f32[8,128]{1,0:T(8,128)}, f32[32,1024]{1,0:T(8,128)}, f32[32,1024]{1,0:T(8,128)}, f32[32,1024]{1,0...) custom-call(f32[2,1,512]{2,1,0:T(1,128)} %copy-done.5, ...), custom_call_target="tpu_custom_call" | custom-call | tf_op jit(solution)/shard_map/back_and_sum/pallas_call | solution.py:833
  415.9 1.3 slice.93
  417.8 1.4 slice_bitcast_fusion.3
  419.2 0.6 fusion.19
  419.8 0.6 fusion.18
  420.3 0.6 fusion.17
  420.9 0.6 fusion.16
  421.5 0.6 fusion.15
  422.1 1.4 slice_bitcast_fusion
  423.5 4.1 bitcast_convert_fusion
  427.6 3.2 copy.52
  430.8 0.7 copy.53
  431.4 0.7 copy.54
  432.1 0.7 copy.55
  432.8 0.7 copy.56
  433.4 0.8 copy.57
  434.2 0.8 copy.58
  (64 shorter events, 0.2 us)
Async XLA Ops:
  138.3 4.5 %copy-start.17 = (bf16[2,2,2,2,2,16,128]{6,5,4,3,2,1,0:T(8,128)(2,1)S(1)}, bf16[2,2,2,2,2,16,128]{6,5,4,3,2,1,0:T(8,128)(2,1)}, u32[]{:S(2)}) copy-start(bf16[2,2,2,2,2,16,128]{6,5,4,3,2,1,0:T(8,128)(2,1)} %get-tuple-element.39) | copy-start | bytes 393220
  138.4 74.6 %all-to-all-start.1 = ((bf16[4,2,128,1024]{3,2,1,0:T(8,128)(2,1)}), bf16[4,2,128,1024]{3,2,1,0:T(8,128)(2,1)S(1)}, u32[]{:S(2)}, u32[]{:S(2)}) async-start(bf16[4,2,128,1024]{3,2,1,0:T(8,128)(2,1)} %bitcast.140), calls=%async_computation.1 | async-start | bytes 4194304 | tf_op jit(solution)/shard_map/all_to_all | solution.py:927
  143.3 10.8 %copy-start.5 = (f32[2,1,512]{2,1,0:T(1,128)}, f32[2,1,512]{2,1,0:T(1,128)S(1)}, u32[]{:S(2)}) copy-start(f32[2,1,512]{2,1,0:T(1,128)S(1)} %reshape.314.bias_ref.refs_0_) | copy-start | bytes 12292
  144.6 4.7 %copy-start.11 = (bf16[4,2,128,1024]{3,2,1,0:T(8,128)(2,1)S(1)}, bf16[4,2,128,1024]{3,2,1,0:T(8,128)(2,1)}, u32[]{:S(2)}) copy-start(bf16[4,2,128,1024]{3,2,1,0:T(8,128)(2,1)} %get-tuple-element.37.refs_15_) | copy-start | bytes 6291460
  144.6 4.7 %copy-start.12 = (bf16[2,2,2,2,2,32,1024]{6,5,4,3,2,1,0:T(8,128)(2,1)S(1)}, bf16[2,2,2,2,2,32,1024]{6,5,4,3,2,1,0:T(8,128)(2,1)}, u32[]{:S(2)}) copy-start(bf16[2,2,2,2,2,32,1024]{6,5,4,3,2,1,0:T(8,128)(2,1)} %get-tuple-element.38) | copy-start | bytes 6291460
  149.3 4.8 %copy-start.1 = (bf16[1024,1024]{1,0:T(8,128)(2,1)}, bf16[1024,1024]{1,0:T(8,128)(2,1)S(1)}, u32[]{:S(2)}) copy-start(bf16[1024,1024]{1,0:T(8,128)(2,1)S(1)} %convolution_convert_fusion) | copy-start | bytes 6291460
  149.3 2.4 copy-start.13
  151.7 2.4 copy-start.2
  154.0 16.7 %copy-start.3 = (bf16[1024,1024]{1,0:T(8,128)(2,1)}, bf16[1024,1024]{1,0:T(8,128)(2,1)S(1)}, u32[]{:S(2)}) copy-start(bf16[1024,1024]{1,0:T(8,128)(2,1)S(1)} %add_convert_fusion) | copy-start | bytes 6291460
  154.0 14.2 %copy-start.14 = (bf16[2,2,2,2,2,32,1024]{6,5,4,3,2,1,0:T(8,128)(2,1)S(1)}, bf16[2,2,2,2,2,32,1024]{6,5,4,3,2,1,0:T(8,128)(2,1)}, u32[]{:S(2)}) copy-start(bf16[2,2,2,2,2,32,1024]{6,5,4,3,2,1,0:T(8,128)(2,1)} %get-tuple-element.43) | copy-start | bytes 6291460
  168.2 2.5 copy-start
  168.2 2.5 copy-start.4
  170.8 2.0 copy-start.8
  174.7 23.9 %slice-start = ((s8[8388608]{0:T(1024)(128)(4,1)}), s8[4194304]{0:T(1024)(128)(4,1)S(1)}, s32[]{:S(2)}) async-start(s8[8388608]{0:T(1024)(128)(4,1)} %bitcast.120), calls=%async_computation.2 | async-start | bytes 8388608
  179.2 19.4 %copy-start.10 = (bf16[1024,1024]{1,0:T(8,128)(2,1)}, bf16[1024,1024]{1,0:T(8,128)(2,1)S(1)}, u32[]{:S(2)}) copy-start(bf16[1024,1024]{1,0:T(8,128)(2,1)S(1)} %get-tuple-element.79) | copy-start | bytes 6291460
  179.2 19.5 %copy-start.9 = (f32[1024,1024]{1,0:T(8,128)S(1)}, f32[1024,1024]{1,0:T(8,128)}, u32[]{:S(2)}) copy-start(f32[1024,1024]{1,0:T(8,128)} %copy-done.8) | copy-start | bytes 12582916
  179.2 19.5 %slice-start.1 = ((s8[8388608]{0:T(1024)(128)(4,1)}), s8[4194304]{0:T(1024)(128)(4,1)S(1)}, s32[]{:S(2)}) async-start(s8[8388608]{0:T(1024)(128)(4,1)} %bitcast.120), calls=%async_computation.3 | async-start | bytes 8388608
  210.4 2.0 copy-start.6
  213.0 5.9 %copy-start.7 = (f32[1024,1024]{1,0:T(8,128)S(1)}, f32[1024,1024]{1,0:T(8,128)}, u32[]{:S(2)}) copy-start(f32[1024,1024]{1,0:T(8,128)} %copy-done.6) | copy-start | bytes 12582916
  223.5 204.1 %all-to-all-start = ((bf16[4,2,128,1024]{3,2,1,0:T(8,128)(2,1)}), bf16[4,2,128,1024]{3,2,1,0:T(8,128)(2,1)}, u32[]{:S(2)}, u32[]{:S(2)}) async-start(bf16[4,2,128,1024]{3,2,1,0:T(8,128)(2,1)} %bitcast.124), calls=%async_computation | async-start | bytes 4194304 | tf_op jit(solution)/shard_map/all_to_all | solution.py:952
  423.5 7.3 %copy-start.21 = (f32[32,1024]{1,0:T(8,128)S(1)}, f32[32,1024]{1,0:T(8,128)}, u32[]{:S(2)}) copy-start(f32[32,1024]{1,0:T(8,128)} %get-tuple-element.132) | copy-start | bytes 393220
  423.5 8.0 %copy-start.20 = (f32[32,1024]{1,0:T(8,128)S(1)}, f32[32,1024]{1,0:T(8,128)}, u32[]{:S(2)}) copy-start(f32[32,1024]{1,0:T(8,128)} %get-tuple-element.134) | copy-start | bytes 393220
  423.5 8.6 %copy-start.19 = (f32[32,1024]{1,0:T(8,128)S(1)}, f32[32,1024]{1,0:T(8,128)}, u32[]{:S(2)}) copy-start(f32[32,1024]{1,0:T(8,128)} %get-tuple-element.135) | copy-start | bytes 393220
  423.5 9.3 %copy-start.18 = (f32[32,1024]{1,0:T(8,128)S(1)}, f32[32,1024]{1,0:T(8,128)}, u32[]{:S(2)}) copy-start(f32[32,1024]{1,0:T(8,128)} %get-tuple-element.137) | copy-start | bytes 393220
  427.6 5.8 %copy-start.16 = (f32[32,4096]{1,0:T(8,128)S(1)}, f32[32,4096]{1,0:T(8,128)}, u32[]{:S(2)}) copy-start(f32[32,4096]{1,0:T(8,128)} %get-tuple-element.141) | copy-start | bytes 1572868
  427.6 6.6 %copy-start.15 = (f32[128,1024]{1,0:T(8,128)S(1)}, f32[128,1024]{1,0:T(8,128)}, u32[]{:S(2)}) copy-start(f32[128,1024]{1,0:T(8,128)} %get-tuple-element.143) | copy-start | bytes 1572868
